TPU v7x, 32 devices: a whole 2x2x4 slice. The times are simulated.
32 devices in a mesh: groups: 2 (over y), dom: 4 (over z), chan: 2 (over x), rep: 2 (over core).
Axes of the slice: x: 2, y: 2, z: 4, core: 2. Of those that a mesh axis runs over, the one named last changes fastest.
Arguments:
- node_feats: bfloat16 [4096, 1024], P(('groups', 'dom', 'rep'), 'chan'), parts along dimension 0, may hold values from -6 to 6
- edge_feats: bfloat16 [24576, 1024], P(('groups', 'dom', 'rep'), 'chan'), parts along dimension 0, may hold values from -6 to 6
- senders: int32 [24576], P(('groups', 'dom', 'rep')), parts along dimension 0, may hold values from 0 to 255
- receiver_slot: int32 [24576], P(('groups', 'dom', 'rep')), parts along dimension 0, may hold values from 0 to 511
- halo_rows: int32 [16, 4, 64], P(('groups', 'dom', 'rep')), parts along dimension 0, may hold values from 0 to 255
- tile_counts: int32 [16], P('groups'), parts along dimension 0, may hold values from 1 to 12, as said below
- weight_in: bfloat16 [3, 1024, 1024], P(None, 'chan'), may hold values from -0.109375 to 0.109375
- weight_out: bfloat16 [1024, 1024], P(None, 'chan'), may hold values from -0.1875 to 0.1875
- norm_gain: float32 [1024], P('chan'), may hold values from 0.25 to 1.75
Outputs:
- updated_edges: bfloat16 [24576, 1024], P(('groups', 'dom', 'rep'), 'chan'), parts along dimension 0
- aggregated: float32 [4096, 1024], P(('groups', 'dom', 'rep'), 'chan'), parts along dimension 0
There are 2 independent parts, one for each index of `groups`. A program takes and returns all parts, laid end to end along the dimension named above; an argument that names none is the same for every part. Nothing has to cross between parts.
Inputs may be any that keep to these rules, and one draw needn't show every extreme that they name: `tile_counts`: A partition with more than 9 live tiles has all 12; then the partition 8 / 2 further on the cycle holds at most 6 and no other partition holds more than 9.
All inputs are finite; a program needn't handle non-finite values.
Results may differ from a plain program's by a relative error of at most 0.0033.
Values may be sent and summed in bfloat16 or wider, within the bound.
No kernel may reach another device: no remote copies, remote signals or barrier semaphores. Data moves between devices by JAX's collectives and lax.ppermute only.
A program may use at most 64 MiB of HBM per device.

v0:
```python
import jax
import jax.numpy as jnp
from jax import lax
from jax.sharding import PartitionSpec as P

TILE = 128
RADIUS = 2


def passed_along(block, axis, distance):
    devices = range(lax.axis_size(axis))
    route = [((i - distance) % len(devices), i) for i in devices]
    return lax.ppermute(block, axis, route)


def edge_update(inputs, weight_in, weight_out, norm_gain):
    channels = weight_in.shape[2]
    partial_pre = jnp.einsum("krc,kcd->rd", inputs, weight_in, preferred_element_type=jnp.float32)
    preact = lax.psum(partial_pre, "chan")
    hidden = jax.nn.silu(preact).astype(jnp.bfloat16)
    projected = jnp.dot(hidden, weight_out, preferred_element_type=jnp.float32)
    totals, squares = lax.psum(
        (jnp.sum(projected, axis=1), jnp.sum(projected * projected, axis=1)), "chan"
    )
    row_mean = totals / channels
    row_var = squares / channels - row_mean * row_mean
    normed = (projected - row_mean[:, None]) * lax.rsqrt(row_var + 1e-05)[:, None] * norm_gain
    return (inputs[0].astype(jnp.float32) + normed).astype(jnp.bfloat16)


def local(
    node_feats,
    edge_feats,
    senders,
    receiver_slot,
    halo_rows,
    tile_counts,
    weight_in,
    weight_out,
    norm_gain,
):
    my_index = lax.axis_index(("dom", "rep"))
    offsets = [shift_by for shift_by in range(-RADIUS, RADIUS + 1) if shift_by != 0]
    local_nodes = node_feats.shape[0]
    halo_size = halo_rows.shape[2]
    slot_count = edge_feats.shape[0]
    outgoing = [
        jnp.take(node_feats, halo_rows[0, slot_index], axis=0) for slot_index in range(len(offsets))
    ]
    incoming = [
        passed_along(outgoing[slot_index], ("dom", "rep"), offsets[slot_index])
        for slot_index in range(len(offsets))
    ]
    extended = jnp.concatenate([node_feats] + incoming, axis=0)
    from_sender = jnp.take(node_feats, senders, axis=0)
    from_receiver = jnp.take(extended, receiver_slot, axis=0)
    inputs = jnp.stack([edge_feats, from_sender, from_receiver])
    live_here = tile_counts[my_index]
    whole_rows = edge_update(inputs, weight_in, weight_out, norm_gain)
    live_mask = jnp.arange(slot_count, dtype=jnp.int32) < TILE * live_here
    finished = jnp.where(live_mask[:, None], whole_rows, edge_feats)
    table_rows = extended.shape[0]
    onehot = (
        (jnp.arange(table_rows, dtype=jnp.int32)[:, None] == receiver_slot[None, :])
        & live_mask[None, :]
    ).astype(jnp.bfloat16)
    slot_sums = jnp.dot(onehot, finished, preferred_element_type=jnp.float32)
    own_sums = slot_sums[:local_nodes]
    pieces = [
        slot_sums[local_nodes + slot_index * halo_size : local_nodes + (slot_index + 1) * halo_size]
        for slot_index in range(len(offsets))
    ]
    returned_sums = [
        passed_along(
            pieces[slot_index].astype(jnp.bfloat16), ("dom", "rep"), -offsets[slot_index]
        ).astype(jnp.float32)
        for slot_index in range(len(offsets))
    ]
    owned_rows = halo_rows[0].reshape(-1)
    placing = (jnp.arange(local_nodes, dtype=jnp.int32)[:, None] == owned_rows[None, :]).astype(
        jnp.float32
    )
    aggregated = own_sums + jnp.dot(
        placing,
        jnp.concatenate(returned_sums, axis=0),
        precision=lax.Precision.HIGHEST,
        preferred_element_type=jnp.float32,
    )
    return (finished, aggregated)


def solution(mesh):
    placed = (
        P(("groups", "dom", "rep"), "chan"),
        P(("groups", "dom", "rep"), "chan"),
        P(("groups", "dom", "rep")),
        P(("groups", "dom", "rep")),
        P(("groups", "dom", "rep"), None, None),
        P("groups"),
        P(None, "chan", None),
        P(None, "chan"),
        P("chan"),
    )
    return jax.shard_map(
        local,
        mesh=mesh,
        in_specs=placed,
        out_specs=(P(("groups", "dom", "rep"), "chan"), P(("groups", "dom", "rep"), "chan")),
        check_vma=False,
    )
```

profile of v0, /device:TPU:0, one launch (start us, length us, event | category | flops | bytes accessed | tf_op | source)
XLA Modules:
  0.0 257.5 jit_solution(2275922931000351219)
XLA Ops:
  7.2 0.0 copy-start
  7.2 0.0 copy-start.1
  7.2 0.0 copy-start.6
  7.2 0.0 all-reduce.3.cloned.1.call-start
  7.3 1.5 compare_and_fusion.2
  8.8 1.7 gather_fusion.2
  10.5 0.7 broadcast_select_fusion.3
  11.2 5.1 %collective-permute-start = (bf16[64,512]{1,0:T(8,128)(2,1)S(1)}, bf16[64,512]{1,0:T(8,128)(2,1)}, u32[]{:S(2)}, u32[]{:S(2)}) collective-permute-start(bf16[64,512]{1,0:T(8,128)(2,1)S(1)} %broadcast_select_fusion.3), channel_id=1, source_target_pairs={{4,0},{5,1},{8,4},{9,5},{12,8},{13,9},{0,12},{1,13},{6,2},{7,3},{1... | collective-permute-start | bytes 196616 | tf_op jit(solution)/shard_map/ppermute | solution.py:13
  16.3 1.2 pad_clamp_fusion.4
  17.5 1.8 gather_fusion.3
  19.3 1.3 broadcast_select_fusion.2
  20.6 0.0 collective-permute-start.1
  20.6 1.3 pad_clamp_fusion.3
  21.9 1.8 gather_fusion.4
  23.7 1.4 broadcast_select_fusion.1
  25.1 0.5 collective-permute-start.2
  25.6 1.2 pad_clamp_fusion.2
  26.8 1.8 gather_fusion.5
  28.6 1.4 broadcast_select_fusion
  29.9 0.7 collective-permute-start.3
  30.6 1.7 constant_dynamic-update-slice_fusion.4
  32.3 0.0 copy-done.6
  32.3 0.6 compare_select_fusion
  32.9 0.6 compare_and_fusion
  33.5 0.6 compare_and_fusion.1
  34.1 0.0 copy-done.1
  34.1 5.4 %gather_fusion = bf16[1536,512]{1,0:T(8,128)(2,1)} fusion(bf16[256,512]{1,0:T(8,128)(2,1)S(1)} %copy-done.1, s32[2048]{0:T(1024)S(1)} %pad_clamp_fusion.1), kind=kCustom, calls=%fused_computation.4 | custom fusion | bytes 3151872 | tf_op jit(solution)/shard_map/jit(_take)/gather | solution.py:55
  39.5 2.9 %bitcast_select_fusion.1 = bf16[1,1536,512]{2,1,0:T(8,128)(2,1)} fusion(bf16[1536,512]{1,0:T(8,128)(2,1)} %gather_fusion, pred[1536]{0:T(1024)(128)(4,1)} %compare_and_fusion.1), kind=kLoop, calls=%fused_computation.22 | loop fusion | flops 786432 | bytes 3147264 | tf_op jit(solution)/shard_map/jit(_take)/select_n | solution.py:55
  42.4 0.0 collective-permute-done
  42.4 1.5 constant_dynamic-update-slice_fusion.3
  43.9 0.0 collective-permute-done.1
  43.9 1.5 constant_dynamic-update-slice_fusion.2
  45.4 0.0 collective-permute-done.2
  45.4 1.5 constant_dynamic-update-slice_fusion.1
  46.8 0.0 collective-permute-done.3
  46.8 0.6 constant_dynamic-update-slice_fusion
  47.5 6.6 %gather_fusion.1 = bf16[1536,512]{1,0:T(8,128)(2,1)} fusion(bf16[512,512]{1,0:T(8,128)(2,1)} %constant_dynamic-update-slice_fusion, s32[2048]{0:T(1024)S(1)} %pad_clamp_fusion), kind=kCustom, calls=%fused_computation.5 | custom fusion | bytes 3151872 | tf_op jit(solution)/shard_map/jit(_take)/gather | solution.py:56
  54.1 1.8 bitcast_select_fusion
  55.9 0.0 copy-done.3
  56.0 0.5 copy-done.4
  56.4 6.9 %fusion.6 = f32[1536,1024]{1,0:T(8,128)} fusion(bf16[3,512,1024]{2,1,0:T(8,128)(2,1)S(1)} %copy-done, bf16[1,1536,512]{2,1,0:T(8,128)(2,1)S(1)} %bitcast_select_fusion, bf16[1,1536,512]{2,1,0:T(8,128)(2,1)S(1)} %copy-done.4, bf16[1,1536,512]{2,1,0:T(8,128)(2,1)S(1)} %bitcast.23), kind=kOutput, calls=%fused_computation.13 | convolution fusion | flops 4836556800 | bytes 14155776 | tf_op jit(solution)/shard_map/krc,kcd->rd/dot_general | solution.py:18
  63.3 0.0 all-reduce.3.cloned.1.call-update
  63.3 0.0 copy-start.11
  63.3 2.6 %copy.11 = bf16[1536,512]{0,1:T(8,128)(2,1)} copy(bf16[1536,512]{1,0:T(8,128)(2,1)} %param.12) | data formatting | bytes 3145728 | tf_op args[1]
  65.9 0.6 dynamic_slice.3
  67.2 0.0 copy-start.10
  67.2 150.4 %all-reduce.3.cloned.1.call-done = f32[1536,1024]{1,0:T(8,128)} async-done(((f32[1536,1024]{1,0:T(8,128)}), f32[1536,1024]{1,0:T(8,128)}) %all-reduce.3.cloned.1.call-update) | async-done | bytes 6291472 | tf_op jit(solution)/shard_map/psum | solution.py:19
  217.6 6.9 %fusion.27 = (f32[1536]{0:T(1024)S(1)}, f32[1536]{0:T(1024)S(1)}, f32[1536,512]{0,1:T(8,128)}) fusion(bf16[1024,512]{1,0:T(8,128)(2,1)} %param.18, f32[1536,1024]{1,0:T(8,128)} %all-reduce.3.cloned.1.call-done), kind=kOutput, calls=%fused_computation.68 | convolution fusion | flops 1620833280 | bytes 10498048 | tf_op jit(solution)/shard_map/dot_general | solution.py:21
  224.5 6.9 %all-reduce = (f32[1536]{0:T(1024)S(1)}, f32[1536]{0:T(1024)S(1)}) all-reduce(f32[1536]{0:T(1024)S(1)} %get-tuple-element.6, f32[1536]{0:T(1024)S(1)} %get-tuple-element.5), channel_id=1, replica_groups=mesh['groups'=2,'dom'=4,'chan'=2,'rep'=2] {'chan'}, use_global_device_ids=true, to_apply=%region_4.6 | all-reduce | flops 3072 | bytes 24576 | tf_op jit(solution)/shard_map/psum | solution.py:22
  231.4 3.8 %fusion.13 = bf16[1536,512]{0,1:T(8,128)(2,1)S(1)} fusion(bf16[1536,512]{0,1:T(8,128)(2,1)} %copy.11, f32[1536,512]{0,1:T(8,128)} %get-tuple-element.29, f32[512]{0:T(512)S(1)} %copy-done.10, f32[1536]{0:T(1024)S(1)} %get-tuple-element.22, f32[1536]{0:T(1024)S(1)} %get-tuple-element.21, pred[1536]{0:T(1024)(128)(4,1)S(1)} %iota_compare_fusion.3), kind=kLoop, calls=%fused_computation.20 | loop fusion | flops 5505024 | bytes 6307328 | tf_op jit(solution)/shard_map/jit(_where)/select_n | solution.py:61
  235.3 1.2 copy-done.2
  236.4 2.0 fusion.29
  238.4 0.7 fusion.28
  239.1 1.7 collective-permute-start.4
  240.8 0.0 collective-permute-start.5
  240.8 3.5 %collective-permute-start.6 = (bf16[64,512]{1,0:T(8,128)(2,1)S(1)}, bf16[64,512]{1,0:T(8,128)(2,1)S(1)}, u32[]{:S(2)}, u32[]{:S(2)}) collective-permute-start(bf16[64,512]{1,0:T(8,128)(2,1)S(1)} %get-tuple-element.19), channel_id=1, source_target_pairs={{1,0},{4,1},{5,4},{8,5},{9,8},{12,9},{13,12},{0,13},{3,2},{6,3},{7... | collective-permute-start | bytes 196616 | tf_op jit(solution)/shard_map/ppermute | solution.py:13
  244.4 0.3 collective-permute-start.7
  244.7 0.1 eq.32
  244.7 2.6 %copy.13 = bf16[1536,512]{1,0:T(8,128)(2,1)} copy(bf16[1536,512]{0,1:T(8,128)(2,1)} %copy-done.2) | data formatting | bytes 3145728
  247.3 0.0 collective-permute-done.4
  247.3 0.0 collective-permute-done.5
  247.3 0.0 collective-permute-done.6
  247.3 1.3 collective-permute-done.7
  248.6 2.1 convolution_add_fusion
  (20 shorter events, 0.1 us)
Async XLA Ops:
  7.2 48.8 %copy-start = (bf16[3,512,1024]{2,1,0:T(8,128)(2,1)S(1)}, bf16[3,512,1024]{2,1,0:T(8,128)(2,1)}, u32[]{:S(2)}) copy-start(bf16[3,512,1024]{2,1,0:T(8,128)(2,1)} %param.17) | copy-start | bytes 9437188
  7.2 26.9 %copy-start.1 = (bf16[256,512]{1,0:T(8,128)(2,1)S(1)}, bf16[256,512]{1,0:T(8,128)(2,1)}, u32[]{:S(2)}) copy-start(bf16[256,512]{1,0:T(8,128)(2,1)} %param.11) | copy-start | bytes 786436
  7.2 25.1 %copy-start.6 = (s32[1536]{0:T(1024)S(1)}, s32[1536]{0:T(1024)}, u32[]{:S(2)}) copy-start(s32[1536]{0:T(1024)} %param.14) | copy-start | bytes 18436
  7.2 26.3 %copy-start.5 = (s32[1536]{0:T(1024)S(1)}, s32[1536]{0:T(1024)}, u32[]{:S(2)}) copy-start(s32[1536]{0:T(1024)} %param.13) | copy-start | bytes 18436
  7.2 210.4 %all-reduce.3.cloned.1.call-start = ((), (), s32[]{:S(2)}) async-start(), calls=%async_computation | async-start | bytes 12582912 | tf_op jit(solution)/shard_map/psum | solution.py:19
  11.2 31.2 %collective-permute-start = (bf16[64,512]{1,0:T(8,128)(2,1)S(1)}, bf16[64,512]{1,0:T(8,128)(2,1)}, u32[]{:S(2)}, u32[]{:S(2)}) collective-permute-start(bf16[64,512]{1,0:T(8,128)(2,1)S(1)} %broadcast_select_fusion.3), channel_id=1, source_target_pairs={{4,0},{5,1},{8,4},{9,5},{12,8},{13,9},{0,12},{1,13},{6,2},{7,3},{1... | collective-permute-start | bytes 196616 | tf_op jit(solution)/shard_map/ppermute | solution.py:13
  20.6 23.2 %collective-permute-start.1 = (bf16[64,512]{1,0:T(8,128)(2,1)}, bf16[64,512]{1,0:T(8,128)(2,1)}, u32[]{:S(2)}, u32[]{:S(2)}) collective-permute-start(bf16[64,512]{1,0:T(8,128)(2,1)} %broadcast_select_fusion.2), channel_id=1, source_target_pairs={{1,0},{4,1},{5,4},{8,5},{9,8},{12,9},{13,12},{0,13},{3,2},{6,3},{7... | collective-permute-start | bytes 196616 | tf_op jit(solution)/shard_map/ppermute | solution.py:13
  25.1 20.3 %collective-permute-start.2 = (bf16[64,512]{1,0:T(8,128)(2,1)}, bf16[64,512]{1,0:T(8,128)(2,1)}, u32[]{:S(2)}, u32[]{:S(2)}) collective-permute-start(bf16[64,512]{1,0:T(8,128)(2,1)} %broadcast_select_fusion.1), channel_id=1, source_target_pairs={{13,0},{0,1},{1,4},{4,5},{5,8},{8,9},{9,12},{12,13},{15,2},{2,3},{... | collective-permute-start | bytes 196616 | tf_op jit(solution)/shard_map/ppermute | solution.py:13
  29.9 16.9 %collective-permute-start.3 = (bf16[64,512]{1,0:T(8,128)(2,1)}, bf16[64,512]{1,0:T(8,128)(2,1)S(1)}, u32[]{:S(2)}, u32[]{:S(2)}) collective-permute-start(bf16[64,512]{1,0:T(8,128)(2,1)} %broadcast_select_fusion), channel_id=1, source_target_pairs={{12,0},{13,1},{0,4},{1,5},{4,8},{5,9},{8,12},{9,13},{14,2},{15,3},... | collective-permute-start | bytes 196616 | tf_op jit(solution)/shard_map/ppermute | solution.py:13
  39.5 2.9 %copy-start.7 = (s32[1536]{0:T(1024)S(1)}, s32[1536]{0:T(1024)}, u32[]{:S(2)}) copy-start(s32[1536]{0:T(1024)} %compare_select_fusion) | copy-start | bytes 18436
  47.5 6.6 %copy-start.9 = (pred[1536]{0:T(1024)(128)(4,1)S(1)}, pred[1536]{0:T(1024)(128)(4,1)}, u32[]{:S(2)}) copy-start(pred[1536]{0:T(1024)(128)(4,1)} %compare_and_fusion) | copy-start | bytes 4612
  54.1 1.9 copy-start.3
  54.1 2.4 copy-start.4
  63.3 2.6 %copy-start.11 = (s32[8]{0:T(128)S(1)}, s32[8]{0:T(128)}, u32[]{:S(2)}) copy-start(s32[8]{0:T(128)} %param.16) | copy-start | bytes 100
  67.2 164.2 %copy-start.10 = (f32[512]{0:T(512)S(1)}, f32[512]{0:T(512)}, u32[]{:S(2)}) copy-start(f32[512]{0:T(512)} %param.19) | copy-start | bytes 6148
  235.2 1.2 copy-start.2
  236.4 8.3 %copy-start.8 = (s32[1,4,64]{2,1,0:T(4,128)S(1)}, s32[1,4,64]{2,1,0:T(4,128)}, u32[]{:S(2)}) copy-start(s32[1,4,64]{2,1,0:T(4,128)} %param.15) | copy-start | bytes 3076
  239.1 8.2 %collective-permute-start.4 = (bf16[64,512]{1,0:T(8,128)(2,1)}, bf16[64,512]{1,0:T(8,128)(2,1)S(1)}, u32[]{:S(2)}, u32[]{:S(2)}) collective-permute-start(bf16[64,512]{1,0:T(8,128)(2,1)} %get-tuple-element.17), channel_id=1, source_target_pairs={{12,0},{13,1},{0,4},{1,5},{4,8},{5,9},{8,12},{9,13},{14,2},{15,3},... | collective-permute-start | bytes 196616 | tf_op jit(solution)/shard_map/ppermute | solution.py:13
  240.8 6.5 %collective-permute-start.5 = (bf16[64,512]{1,0:T(8,128)(2,1)}, bf16[64,512]{1,0:T(8,128)(2,1)S(1)}, u32[]{:S(2)}, u32[]{:S(2)}) collective-permute-start(bf16[64,512]{1,0:T(8,128)(2,1)} %get-tuple-element.20), channel_id=1, source_target_pairs={{13,0},{0,1},{1,4},{4,5},{5,8},{8,9},{9,12},{12,13},{15,2},{2,3},{... | collective-permute-start | bytes 196616 | tf_op jit(solution)/shard_map/ppermute | solution.py:13
  240.8 6.5 %collective-permute-start.6 = (bf16[64,512]{1,0:T(8,128)(2,1)S(1)}, bf16[64,512]{1,0:T(8,128)(2,1)S(1)}, u32[]{:S(2)}, u32[]{:S(2)}) collective-permute-start(bf16[64,512]{1,0:T(8,128)(2,1)S(1)} %get-tuple-element.19), channel_id=1, source_target_pairs={{1,0},{4,1},{5,4},{8,5},{9,8},{12,9},{13,12},{0,13},{3,2},{6,3},{7... | collective-permute-start | bytes 196616 | tf_op jit(solution)/shard_map/ppermute | solution.py:13
  244.4 4.3 %collective-permute-start.7 = (bf16[64,512]{1,0:T(8,128)(2,1)S(1)}, bf16[64,512]{1,0:T(8,128)(2,1)S(1)}, u32[]{:S(2)}, u32[]{:S(2)}) collective-permute-start(bf16[64,512]{1,0:T(8,128)(2,1)S(1)} %get-tuple-element.18), channel_id=1, source_target_pairs={{4,0},{5,1},{8,4},{9,5},{12,8},{13,9},{0,12},{1,13},{6,2},{7,3},{1... | collective-permute-start | bytes 196616 | tf_op jit(solution)/shard_map/ppermute | solution.py:13
Sparse Core Ops, SparseCore 0:
  63.4 154.1 all-reduce.2
where the time goes:
time: 258 us
  waiting for transfers between devices  152 us (59%)
  local copies, waits for them, and re-layouts  34.1 us (13%)
  other arithmetic  20.2 us (8%)
  matrix products  17.8 us (7%)
  between operations  14.8 us (6%)
  starting transfers between devices  11.9 us (5%)
  blocking collectives  6.9 us (3%)
    psum x1, waiting for transfers between devices, edge_update(): preact = lax.psum(partial_pre, 'chan')  150 us
    unnamed x30, local copies, waits for them, and re-layouts  13 us
    ppermute x8, starting transfers between devices, passed_along(): return lax.ppermute(block, axis, route)  11.9 us
    gather x4, local copies, waits for them, and re-layouts, local(): jnp.take(node_feats, halo_rows[0, slot_index], axis=0)  7.15 us
    psum x1, blocking collectives, edge_update(): lax.psum((jnp.sum(projected, axis=1), jnp.sum(projected * projected, axis...  6.9 us
    dot_general x1, matrix products, edge_update(): projected = jnp.dot(hidden, weight_out, preferred_element_type=jnp.float32)  6.88 us
    dot_general x1, matrix products, edge_update(): jnp.einsum('krc,kcd->rd', inputs, weight_in, preferred_element_type=jnp.f...  6.86 us
    gather x1, local copies, waits for them, and re-layouts, local(): from_receiver = jnp.take(extended, receiver_slot, axis=0)  6.6 us
  transfers between devices with their start and end apart: 9, of which 2 were waited for; matrix products, arithmetic and copies ran while one was open for 14% of the time, Pallas kernels for 0%

commit v1 on v0

v1 whole, which is shorter than its diff:
```python
import jax
import jax.numpy as jnp
from jax import lax
from jax.sharding import PartitionSpec as P

TILE = 128
RADIUS = 2
CHUNKS = 3
bf16 = jnp.bfloat16
f32 = jnp.float32


def shifted(block, axis, distance):
    size = lax.axis_size(axis)
    return lax.ppermute(block, axis, [(i, (i + distance) % size) for i in range(size)])


def swapped(block, axis):
    size = lax.axis_size(axis)
    return lax.ppermute(block, axis, [(i, i ^ 1) for i in range(size)])


def fetch(block, dim, distance, order):
    share = sum((lax.axis_index(axis) % 2) << place for place, axis in enumerate(order))
    rows = block.shape[dim] >> len(order)
    piece = lax.dynamic_slice_in_dim(block, share * rows, rows, dim)
    piece = shifted(piece, "chan", distance)
    for axis in order:
        other = swapped(piece, axis)
        first = lax.axis_index(axis) % 2 == 0
        piece = jnp.where(
            first,
            jnp.concatenate([piece, other], axis=dim),
            jnp.concatenate([other, piece], axis=dim),
        )
    return piece


def onehot(rows, columns, live=None):
    hit = rows[:, None] == columns[None, :]
    if live is not None:
        hit = hit & live
    return hit.astype(bf16)


def local(
    node_feats,
    edge_feats,
    senders,
    receiver_slot,
    halo_rows,
    tile_counts,
    weight_in,
    weight_out,
    norm_gain,
):
    ways = lax.axis_size("chan")
    me = lax.axis_index("chan")
    my_index = lax.axis_index(("dom", "rep"))
    offsets = [shift_by for shift_by in range(-RADIUS, RADIUS + 1) if shift_by != 0]
    local_nodes, width = node_feats.shape
    halo_size = halo_rows.shape[2]
    slot_count = edge_feats.shape[0]
    channels = ways * width
    table_rows = local_nodes + len(offsets) * halo_size
    chunk = slot_count // CHUNKS
    mine = chunk // ways
    pairs = [axis for axis in ("groups", "dom", "rep") if lax.axis_size(axis) % 2 == 0]
    order = pairs
    other_order = [axis for axis in ("dom", "groups", "rep") if axis in pairs]
    distances = range(1, ways)

    nodes = [node_feats] + [shifted(node_feats, "chan", d) for d in distances]
    gains = [norm_gain] + [shifted(norm_gain, "chan", d) for d in distances]
    first_pair = [weight_in[:2]] + [fetch(weight_in[:2], 1, d, order) for d in distances]
    third = [weight_in[2]] + [fetch(weight_in[2], 0, d, other_order) for d in distances]
    outs = [weight_out] + [fetch(weight_out, 0, d, other_order) for d in distances]

    def rows_of(array, k, owner):
        return lax.dynamic_slice_in_dim(array, k * chunk + owner * mine, mine, 0)

    edges = [
        [rows_of(edge_feats, k, me)]
        + [shifted(rows_of(edge_feats, k, (me + d) % ways), "chan", d) for d in distances]
        for k in range(CHUNKS)
    ]

    full_nodes = jnp.concatenate(nodes, axis=1)
    node_ids = jnp.arange(local_nodes, dtype=jnp.int32)
    incoming = []
    for j, shift_by in enumerate(offsets):
        rows = jnp.dot(onehot(halo_rows[0, j], node_ids), full_nodes, preferred_element_type=f32)
        incoming.append(shifted(rows.astype(bf16), ("dom", "rep"), shift_by))
    extended = jnp.concatenate([full_nodes] + incoming, axis=0)

    slot_ids = jnp.arange(table_rows, dtype=jnp.int32)
    whole_in = jnp.concatenate(
        [w[0] for w in first_pair] + [w[1] for w in first_pair] + third, axis=0
    )
    whole_out = jnp.concatenate(outs, axis=1)
    gain = jnp.concatenate(gains)
    live_rows = TILE * tile_counts[my_index]

    slot_sums = jnp.zeros((table_rows, width), f32)
    finished = []
    for k in range(CHUNKS):
        sender = rows_of(senders, k, me)
        slot = rows_of(receiver_slot, k, me)
        own = jnp.concatenate(edges[k], axis=1)
        sent = jnp.dot(onehot(sender, node_ids), full_nodes, preferred_element_type=f32)
        got = jnp.dot(onehot(slot, slot_ids), extended, preferred_element_type=f32)
        joined = jnp.concatenate([own, sent.astype(bf16), got.astype(bf16)], axis=1)
        preact = jnp.dot(joined, whole_in, preferred_element_type=f32)
        hidden = jax.nn.silu(preact).astype(bf16)
        projected = jnp.dot(hidden, whole_out, preferred_element_type=f32)
        row_mean = jnp.sum(projected, axis=1, keepdims=True) / channels
        row_square = jnp.sum(projected * projected, axis=1, keepdims=True) / channels
        scale = lax.rsqrt(row_square - row_mean * row_mean + 1e-05)
        normed = (projected - row_mean) * scale * gain
        edge_ids = k * chunk + me * mine + jnp.arange(mine, dtype=jnp.int32)
        live = (edge_ids < live_rows)[:, None]
        updated = jnp.where(live, (own.astype(f32) + normed).astype(bf16), own)
        parts = [updated[:, d * width : (d + 1) * width] for d in range(ways)]
        parts = [parts[0]] + [shifted(parts[d], "chan", -d) for d in distances]
        whole = jnp.zeros((chunk, width), bf16)
        for d in range(ways):
            whole = lax.dynamic_update_slice_in_dim(whole, parts[d], ((me + d) % ways) * mine, 0)
        finished.append(whole)
        slots = receiver_slot[k * chunk : (k + 1) * chunk]
        chunk_live = (k * chunk + jnp.arange(chunk, dtype=jnp.int32)) < live_rows
        slot_sums += jnp.dot(
            onehot(slot_ids, slots, chunk_live[None, :]), whole, preferred_element_type=f32
        )
    own_sums = slot_sums[:local_nodes]
    returned = []
    for j, shift_by in enumerate(offsets):
        start = local_nodes + j * halo_size
        piece = slot_sums[start : start + halo_size].astype(bf16)
        returned.append(shifted(piece, ("dom", "rep"), -shift_by))
    aggregated = own_sums + jnp.dot(
        onehot(node_ids, halo_rows[0].reshape(-1)),
        jnp.concatenate(returned, axis=0),
        preferred_element_type=f32,
    )
    return (jnp.concatenate(finished, axis=0), aggregated)


def solution(mesh):
    placed = (
        P(("groups", "dom", "rep"), "chan"),
        P(("groups", "dom", "rep"), "chan"),
        P(("groups", "dom", "rep")),
        P(("groups", "dom", "rep")),
        P(("groups", "dom", "rep"), None, None),
        P("groups"),
        P(None, "chan", None),
        P(None, "chan"),
        P("chan"),
    )
    return jax.shard_map(
        local,
        mesh=mesh,
        in_specs=placed,
        out_specs=(P(("groups", "dom", "rep"), "chan"), P(("groups", "dom", "rep"), "chan")),
        check_vma=False,
    )
```

time: 258 us -> 138 us (0.53)
  waiting for transfers between devices: 152 us -> 40.1 us
  starting transfers between devices: 11.9 us -> 32.2 us
  local copies, waits for them, and re-layouts: 34.1 us -> 20.3 us
  matrix products: 17.8 us -> 30.9 us
  between operations: 14.8 us -> 2.01 us
  other arithmetic: 20.2 us -> 12.2 us
  blocking collectives: 6.9 us -> 0 us
    psum x1 -> x0, waiting for transfers between devices: 150 us -> none  [edge_update(): preact = lax.psum(partial_pre, 'chan')]
    ppermute x8 -> x28, waiting for transfers between devices: 1.3 us -> 40.1 us  [the longest x19 32.7 us: shifted(): lax.ppermute(block, axis, [(i, (i + distance) % size) for i in range(size)])]
    ppermute x8 -> x28, starting transfers between devices: 11.9 us -> 32.2 us  [the longest x19 23.8 us: shifted(): lax.ppermute(block, axis, [(i, (i + distance) % size) for i in range(size)])]
    gather x6 -> x0, local copies, waits for them, and re-layouts: 19.2 us -> none  [the longest x4 7.15 us: local(): jnp.take(node_feats, halo_rows[0, slot_index], axis=0)]
    dot_general x4 -> x17, matrix products: 17.8 us -> 30.9 us  [the longest x3 18.2 us: local(): projected = jnp.dot(hidden, whole_out, preferred_element_type=f32)]
    psum x1 -> x0, blocking collectives: 6.9 us -> none  [edge_update(): lax.psum((jnp.sum(projected, axis=1), jnp.sum(projected * projected, axis...]
    select_n x9, other arithmetic: 13.9 us -> 7.05 us  [the longest x8 4.59 us: fetch(): jnp.where(first, jnp.concatenate([piece, other], axis=dim), jnp.concatena...]
    dynamic_slice x1 -> x7, local copies, waits for them, and re-layouts: 0.58 us -> 6.72 us  [the longest x3 3.13 us: rows_of(): return lax.dynamic_slice_in_dim(array, k * chunk + owner * mine, mine, 0)]
  transfers between devices with their start and end apart: 9 -> 28, of which waited for: 2 -> 6; matrix products, arithmetic and copies ran while one was open for 14% -> 34% of each run, Pallas kernels for 0% -> 0%
where the time goes in v1:
time: 138 us
  waiting for transfers between devices  40.1 us (29%)
  starting transfers between devices  32.2 us (23%)
  matrix products  30.9 us (22%)
  local copies, waits for them, and re-layouts  20.3 us (15%)
  other arithmetic  12.2 us (9%)
  between operations  2.01 us (1%)
    ppermute x19, waiting for transfers between devices, shifted(): lax.ppermute(block, axis, [(i, (i + distance) % size) for i in range(size)])  32.7 us
    ppermute x19, starting transfers between devices, shifted(): lax.ppermute(block, axis, [(i, (i + distance) % size) for i in range(size)])  23.8 us
    dot_general x3, matrix products, local(): projected = jnp.dot(hidden, whole_out, preferred_element_type=f32)  18.2 us
    ppermute x9, starting transfers between devices, swapped(): return lax.ppermute(block, axis, [(i, i ^ 1) for i in range(size)])  8.38 us
    unnamed x63, local copies, waits for them, and re-layouts  8.21 us
    ppermute x9, waiting for transfers between devices, swapped(): return lax.ppermute(block, axis, [(i, i ^ 1) for i in range(size)])  7.42 us
    select_n x8, other arithmetic, fetch(): jnp.where(first, jnp.concatenate([piece, other], axis=dim), jnp.concatena...  4.59 us
    dot_general x3, matrix products, local(): jnp.dot(onehot(sender, node_ids), full_nodes, preferred_element_type=f32)  4.16 us
  transfers between devices with their start and end apart: 28, of which 6 were waited for; matrix products, arithmetic and copies ran while one was open for 34% of the time, Pallas kernels for 0%

profile of v1, /device:TPU:0, one launch (start us, length us, event | category | flops | bytes accessed | tf_op | source)
XLA Modules:
  0.0 137.6 jit_solution(7508421712600101127)
XLA Ops:
  0.7 1.5 %slice-done = bf16[2,512,1024]{2,1,0:T(8,128)(2,1)S(1)} async-done(((bf16[3,512,1024]{2,1,0:T(8,128)(2,1)}), bf16[2,512,1024]{2,1,0:T(8,128)(2,1)S(1)}, s32[]{:S(2)}) %slice-start) | async-done | bytes 2097176 | tf_op jit(solution)/shard_map/slice | solution.py:75
  2.2 0.7 constant_dynamic-slice_fusion.5
  2.9 2.9 %collective-permute-start.6 = (bf16[2,64,1024]{2,1,0:T(8,128)(2,1)}, bf16[2,64,1024]{2,1,0:T(8,128)(2,1)}, u32[]{:S(2)}, u32[]{:S(2)}) collective-permute-start(bf16[2,64,1024]{2,1,0:T(8,128)(2,1)} %constant_dynamic-slice_fusion.5), channel_id=1, source_target_pairs={{0,2},{2,0},{1,3},{3,1},{4,6},{6,4},{5,7},{7,5},{8,10},{10,8},{9,1... | collective-permute-start | bytes 786440 | tf_op jit(solution)/shard_map/ppermute | solution.py:15
  5.9 1.3 slice.89
  7.2 0.7 dynamic-slice_bitcast_fusion
  8.0 1.6 %constant_dynamic-slice_fusion.4 = bf16[128,512]{1,0:T(8,128)(2,1)} fusion(bf16[1024,512]{1,0:T(8,128)(2,1)} %param.16, s32[]{:T(128)S(6)} %select_n.219), kind=kLoop, calls=%fused_computation.138 | loop fusion | bytes 262148 | tf_op jit(solution)/shard_map/dynamic_slice | solution.py:26
  9.5 1.9 %collective-permute-start.14 = (bf16[128,512]{1,0:T(8,128)(2,1)}, bf16[128,512]{1,0:T(8,128)(2,1)S(1)}, u32[]{:S(2)}, u32[]{:S(2)}) collective-permute-start(bf16[128,512]{1,0:T(8,128)(2,1)} %constant_dynamic-slice_fusion.4), channel_id=1, source_target_pairs={{0,2},{2,0},{1,3},{3,1},{4,6},{6,4},{5,7},{7,5},{8,10},{10,8},{9,1... | collective-permute-start | bytes 393224 | tf_op jit(solution)/shard_map/ppermute | solution.py:15
  11.6 1.9 %collective-permute-start.18 = (f32[512]{0:T(512)}, f32[512]{0:T(512)}, u32[]{:S(2)}, u32[]{:S(2)}) collective-permute-start(f32[512]{0:T(512)} %param.17), channel_id=1, source_target_pairs={{0,2},{2,0},{1,3},{3,1},{4,6},{6,4},{5,7},{7,5},{8,10},{10,8},{9,1... | collective-permute-start | bytes 6152 | tf_op jit(solution)/shard_map/ppermute | solution.py:15
  13.5 2.3 %bitcast_dynamic-update-slice_fusion.2 = bf16[3072,1024]{1,0:T(8,128)(2,1)} fusion(bf16[3,512,1024]{2,1,0:T(8,128)(2,1)} %param.15), kind=kLoop, calls=%fused_computation.49 | loop fusion | bytes 2097152
  15.8 1.0 constant_dynamic-update-slice_fusion.1
  16.8 0.6 dynamic_slice.50
  18.1 0.5 add_compare_fusion.2
  18.6 0.5 add_compare_fusion.3
  19.2 0.6 add_compare_fusion
  19.8 0.5 slice_bitcast_fusion.2
  20.3 0.6 fusion.103
  20.9 1.4 %fusion.102 = (s32[256]{0:T(256)}, s32[256]{0:T(256)}, s32[256]{0:T(256)}) fusion(s32[1536]{0:T(1024)} %param.11, s32[]{:T(128)S(6)} %select_n.196, s32[]{:T(128)S(6)} %select_n.230, s32[]{:T(128)S(6)} %select_n.227), kind=kLoop, calls=%fused_computation.173 | loop fusion | bytes 6156 | tf_op jit(solution)/shard_map/dynamic_slice | solution.py:80
  22.4 1.1 constant_dynamic-slice_fusion.7
  23.5 0.5 add_compare_fusion.4
  24.0 0.5 iota_compare_fusion.25
  24.5 0.7 eq.282
  25.5 0.7 pad_maximum_fusion.5
  26.2 1.7 %collective-permute-start.20 = (bf16[256,512]{1,0:T(8,128)(2,1)}, bf16[256,512]{1,0:T(8,128)(2,1)}, u32[]{:S(2)}, u32[]{:S(2)}) collective-permute-start(bf16[256,512]{1,0:T(8,128)(2,1)} %get-tuple-element.9), channel_id=1, source_target_pairs={{0,2},{2,0},{1,3},{3,1},{4,6},{6,4},{5,7},{7,5},{8,10},{10,8},{9,1... | collective-permute-start | bytes 786440 | tf_op jit(solution)/shard_map/ppermute | solution.py:15
  28.0 1.6 %collective-permute-start.11 = (bf16[64,1024]{1,0:T(8,128)(2,1)}, bf16[64,1024]{1,0:T(8,128)(2,1)S(1)}, u32[]{:S(2)}, u32[]{:S(2)}) collective-permute-start(bf16[64,1024]{1,0:T(8,128)(2,1)} %collective-permute-done.10), channel_id=1, source_target_pairs={{0,4},{4,0},{8,12},{12,8},{1,5},{5,1},{9,13},{13,9},{2,6},{6,2},{1... | collective-permute-start | bytes 393224 | tf_op jit(solution)/shard_map/ppermute | solution.py:20
  30.0 1.0 constant_dynamic-update-slice_fusion
  31.0 0.9 convolution_convert_fusion.9
  31.9 0.8 convolution_convert_fusion.8
  32.7 1.9 %convolution_convert_fusion.3 = bf16[256,1024]{1,0:T(8,128)(2,1)} fusion(bf16[256,1024]{1,0:T(8,128)(2,1)S(1)} %get-tuple-element.24, s32[256]{0:T(256)} %get-tuple-element.32), kind=kOutput, calls=%fused_computation.32 | convolution fusion | flops 134545408 | bytes 1049600 | tf_op jit(solution)/shard_map/dot_general | solution.py:110
  34.6 1.1 convolution_convert_fusion.4
  36.0 1.1 convolution_convert_fusion.5
  37.1 1.5 %collective-permute-start.7 = (bf16[2,64,1024]{2,1,0:T(8,128)(2,1)}, bf16[2,64,1024]{2,1,0:T(8,128)(2,1)S(1)}, u32[]{:S(2)}, u32[]{:S(2)}) collective-permute-start(bf16[2,64,1024]{2,1,0:T(8,128)(2,1)} %collective-permute-done.6), channel_id=1, source_target_pairs={{0,16},{16,0},{1,17},{17,1},{2,18},{18,2},{3,19},{19,3},{4,20},{20... | collective-permute-start | bytes 786440 | tf_op jit(solution)/shard_map/ppermute | solution.py:20
  38.9 3.7 %collective-permute-start.2 = (bf16[64,1024]{1,0:T(8,128)(2,1)S(1)}, bf16[64,1024]{1,0:T(8,128)(2,1)S(1)}, u32[]{:S(2)}, u32[]{:S(2)}) collective-permute-start(bf16[64,1024]{1,0:T(8,128)(2,1)S(1)} %convolution_convert_fusion.9), channel_id=1, source_target_pairs={{0,12},{1,13},{4,0},{5,1},{8,4},{9,5},{12,8},{13,9},{2,14},{3,15},... | collective-permute-start | bytes 393224 | tf_op jit(solution)/shard_map/ppermute | solution.py:15
  42.6 1.0 maximum_select_fusion.7
  43.7 1.2 maximum_select_fusion.4
  44.9 1.6 %collective-permute-start.8 = (bf16[2,128,1024]{2,1,0:T(8,128)(2,1)S(1)}, bf16[2,128,1024]{2,1,0:T(8,128)(2,1)S(1)}, u32[]{:S(2)}, u32[]{:S(2)}) collective-permute-start(bf16[2,128,1024]{2,1,0:T(8,128)(2,1)S(1)} %maximum_select_fusion.4), channel_id=1, source_target_pairs={{0,4},{4,0},{8,12},{12,8},{1,5},{5,1},{9,13},{13,9},{2,6},{6,2},{1... | collective-permute-start | bytes 1572872 | tf_op jit(solution)/shard_map/ppermute | solution.py:20
  47.0 0.9 collective-permute-start.5
  47.9 16.1 %collective-permute-done.4 = bf16[64,1024]{1,0:T(8,128)(2,1)S(1)} collective-permute-done((bf16[64,1024]{1,0:T(8,128)(2,1)S(1)}, bf16[64,1024]{1,0:T(8,128)(2,1)S(1)}, u32[]{:S(2)}, u32[]{:S(2)}) %collective-permute-start.4) | collective-permute-done | bytes 131104 | tf_op jit(solution)/shard_map/ppermute | solution.py:15
  64.0 1.5 %collective-permute-start.12 = (bf16[128,1024]{1,0:T(8,128)(2,1)S(1)}, bf16[128,1024]{1,0:T(8,128)(2,1)S(1)}, u32[]{:S(2)}, u32[]{:S(2)}) collective-permute-start(bf16[128,1024]{1,0:T(8,128)(2,1)S(1)} %maximum_select_fusion.7), channel_id=1, source_target_pairs={{0,16},{16,0},{1,17},{17,1},{2,18},{18,2},{3,19},{19,3},{4,20},{20... | collective-permute-start | bytes 786440 | tf_op jit(solution)/shard_map/ppermute | solution.py:20
  65.5 0.7 collective-permute-start.16
  66.2 0.5 maximum_select_fusion.1
  66.7 0.7 collective-permute-start.9
  67.4 1.3 convolution_convert_fusion
  68.6 7.3 %collective-permute-done.16 = bf16[256,512]{1,0:T(8,128)(2,1)S(1)} collective-permute-done((bf16[256,512]{1,0:T(8,128)(2,1)S(1)}, bf16[256,512]{1,0:T(8,128)(2,1)S(1)}, u32[]{:S(2)}, u32[]{:S(2)}) %collective-permute-start.16) | collective-permute-done | bytes 262176 | tf_op jit(solution)/shard_map/ppermute | solution.py:20
  76.3 1.4 convolution_convert_fusion.1
  77.6 1.3 convolution_convert_fusion.2
  78.9 0.6 collective-permute-start
  80.4 1.0 maximum_select_fusion
  81.6 1.1 copy-done
  83.4 2.6 %copy-done.7 = bf16[3072,1024]{1,0:T(8,128)(2,1)} copy-done((bf16[3072,1024]{1,0:T(8,128)(2,1)}, bf16[3072,1024]{1,0:T(8,128)(2,1)S(1)}, u32[]{:S(2)}) %copy-start.7) | copy-done | bytes 6291480
  86.1 0.7 copy-done.6
  86.8 5.9 %fusion.96 = (f32[256]{0:T(256)S(1)}, f32[256]{0:T(256)S(1)}, f32[256,1024]{1,0:T(8,128)S(1)}) fusion(bf16[1024,512]{1,0:T(8,128)(2,1)S(1)} %maximum_select_fusion.3, bf16[1024,512]{1,0:T(8,128)(2,1)} %param.16, bf16[3072,1024]{1,0:T(8,128)(2,1)} %copy-done.7, bf16[256,1024]{1,0:T(8,128)(2,1)} %convolution_convert_fusion, ...), kind=kOutput, calls=%fused_computation.167 | convolution fusion | flops 2160066048 | bytes 11012096 | tf_op jit(solution)/shard_map/dot_general | solution.py:115
  92.8 6.1 %fusion.95 = (f32[256]{0:T(256)S(1)}, f32[256]{0:T(256)S(1)}, f32[256,1024]{1,0:T(8,128)S(1)}) fusion(bf16[1024,512]{1,0:T(8,128)(2,1)} %copy-done.4, bf16[1024,512]{1,0:T(8,128)(2,1)} %param.16, bf16[3072,1024]{1,0:T(8,128)(2,1)} %copy-done.7, bf16[256,1024]{1,0:T(8,128)(2,1)} %convolution_convert_fusion.1, bf16[256,1024]{1,0:T(8,128)(2,1)S(1)} %copy-done.5, ...), kind=kOutput, calls=%fused_computation.166 | convolution fusion | flops 2160066048 | bytes 11012096 | tf_op jit(solution)/shard_map/dot_general | solution.py:115
  99.0 6.2 %fusion.94 = (f32[256]{0:T(256)S(1)}, f32[256]{0:T(256)S(1)}, f32[256,1024]{1,0:T(8,128)S(1)}) fusion(bf16[1024,512]{1,0:T(8,128)(2,1)} %copy-done.4, bf16[1024,512]{1,0:T(8,128)(2,1)} %param.16, bf16[3072,1024]{1,0:T(8,128)(2,1)} %copy-done.7, bf16[256,1024]{1,0:T(8,128)(2,1)} %convolution_convert_fusion.2, ...), kind=kOutput, calls=%fused_computation.165 | convolution fusion | flops 2160066048 | bytes 11012096 | tf_op jit(solution)/shard_map/dot_general | solution.py:115
  105.2 2.5 %fusion.51 = (bf16[256,1024]{1,0:T(8,128)(2,1)S(1)}, bf16[256,1024]{1,0:T(8,128)(2,1)S(1)}, bf16[256,1024]{1,0:T(8,128)(2,1)S(1)}) fusion(f32[256,1024]{1,0:T(8,128)S(1)} %get-tuple-element.50, bf16[256,512]{1,0:T(8,128)(2,1)} %collective-permute-done, bf16[256,512]{1,0:T(8,128)(2,1)S(1)} %get-tuple-element.8, f32[1024]{0:T(1024)S(1)} %pad_maximum_fusion.5, ...), kind=kLoop, calls=%fused_computation.70 | loop fusion | flops 8650752 | bytes 6302464 | tf_op jit(solution)/shard_map/jit(_where)/select_n | solution.py:122
  107.8 1.5 %collective-permute-start.21 = (bf16[256,512]{1,0:T(8,128)(2,1)S(1)}, bf16[256,512]{1,0:T(8,128)(2,1)S(1)}, u32[]{:S(2)}, u32[]{:S(2)}) collective-permute-start(bf16[256,512]{1,0:T(8,128)(2,1)S(1)} %get-tuple-element.20), channel_id=1, source_target_pairs={{0,2},{2,0},{1,3},{3,1},{4,6},{6,4},{5,7},{7,5},{8,10},{10,8},{9,1... | collective-permute-start | bytes 786440 | tf_op jit(solution)/shard_map/ppermute | solution.py:15
  109.3 0.7 collective-permute-start.19
  110.1 1.5 %collective-permute-start.23 = (bf16[256,512]{1,0:T(8,128)(2,1)S(1)}, bf16[256,512]{1,0:T(8,128)(2,1)S(1)}, u32[]{:S(2)}, u32[]{:S(2)}) collective-permute-start(bf16[256,512]{1,0:T(8,128)(2,1)S(1)} %get-tuple-element.22), channel_id=1, source_target_pairs={{0,2},{2,0},{1,3},{3,1},{4,6},{6,4},{5,7},{7,5},{8,10},{10,8},{9,1... | collective-permute-start | bytes 786440 | tf_op jit(solution)/shard_map/ppermute | solution.py:15
  111.6 5.4 %collective-permute-done.21 = bf16[256,512]{1,0:T(8,128)(2,1)S(1)} collective-permute-done((bf16[256,512]{1,0:T(8,128)(2,1)S(1)}, bf16[256,512]{1,0:T(8,128)(2,1)S(1)}, u32[]{:S(2)}, u32[]{:S(2)}) %collective-permute-start.21) | collective-permute-done | bytes 262176 | tf_op jit(solution)/shard_map/ppermute | solution.py:15
  117.4 10.1 %collective-permute-done.23 = bf16[256,512]{1,0:T(8,128)(2,1)S(1)} collective-permute-done((bf16[256,512]{1,0:T(8,128)(2,1)S(1)}, bf16[256,512]{1,0:T(8,128)(2,1)S(1)}, u32[]{:S(2)}, u32[]{:S(2)}) %collective-permute-start.23) | collective-permute-done | bytes 262176 | tf_op jit(solution)/shard_map/ppermute | solution.py:15
  128.7 3.5 %collective-permute-start.26 = (bf16[64,512]{1,0:T(8,128)(2,1)S(1)}, bf16[64,512]{1,0:T(8,128)(2,1)S(1)}, u32[]{:S(2)}, u32[]{:S(2)}) collective-permute-start(bf16[64,512]{1,0:T(8,128)(2,1)S(1)} %get-tuple-element.16), channel_id=1, source_target_pairs={{0,13},{1,0},{4,1},{5,4},{8,5},{9,8},{12,9},{13,12},{2,15},{3,2},{... | collective-permute-start | bytes 196616 | tf_op jit(solution)/shard_map/ppermute | solution.py:15
  132.3 2.0 %collective-permute-start.27 = (bf16[64,512]{1,0:T(8,128)(2,1)S(1)}, bf16[64,512]{1,0:T(8,128)(2,1)S(1)}, u32[]{:S(2)}, u32[]{:S(2)}) collective-permute-start(bf16[64,512]{1,0:T(8,128)(2,1)S(1)} %get-tuple-element.15), channel_id=1, source_target_pairs={{0,12},{1,13},{4,0},{5,1},{8,4},{9,5},{12,8},{13,9},{2,14},{3,15},... | collective-permute-start | bytes 196616 | tf_op jit(solution)/shard_map/ppermute | solution.py:15
  134.2 1.2 pad_maximum_fusion.1
  135.5 1.0 collective-permute-done.27
  136.5 1.0 slice_add_fusion
  (118 shorter events, 5.9 us)
Async XLA Ops:
  0.6 1.6 %slice-start = ((bf16[3,512,1024]{2,1,0:T(8,128)(2,1)}), bf16[2,512,1024]{2,1,0:T(8,128)(2,1)S(1)}, s32[]{:S(2)}) async-start(bf16[3,512,1024]{2,1,0:T(8,128)(2,1)} %param.15), calls=%async_computation | async-start | bytes 4194304 | tf_op jit(solution)/shard_map/slice | solution.py:75
  0.7 16.1 %copy-start.24 = (s32[8]{0:T(128)S(1)}, s32[8]{0:T(128)}, u32[]{:S(2)}) copy-start(s32[8]{0:T(128)} %param.14) | copy-start | bytes 100
  0.7 19.1 %copy-start.9 = (s32[1,4,64]{2,1,0:T(4,128)S(1)}, s32[1,4,64]{2,1,0:T(4,128)}, u32[]{:S(2)}) copy-start(s32[1,4,64]{2,1,0:T(4,128)} %param.13) | copy-start | bytes 3076
  0.7 19.6 %copy-start.8 = (s32[1536]{0:T(1024)S(1)}, s32[1536]{0:T(1024)}, u32[]{:S(2)}) copy-start(s32[1536]{0:T(1024)} %param.12) | copy-start | bytes 18436
  2.9 19.4 %copy-start.1 = (bf16[1536,512]{1,0:T(8,128)(2,1)S(1)}, bf16[1536,512]{1,0:T(8,128)(2,1)}, u32[]{:S(2)}) copy-start(bf16[1536,512]{1,0:T(8,128)(2,1)} %param.10) | copy-start | bytes 4718596
  2.9 34.2 %collective-permute-start.6 = (bf16[2,64,1024]{2,1,0:T(8,128)(2,1)}, bf16[2,64,1024]{2,1,0:T(8,128)(2,1)}, u32[]{:S(2)}, u32[]{:S(2)}) collective-permute-start(bf16[2,64,1024]{2,1,0:T(8,128)(2,1)} %constant_dynamic-slice_fusion.5), channel_id=1, source_target_pairs={{0,2},{2,0},{1,3},{3,1},{4,6},{6,4},{5,7},{7,5},{8,10},{10,8},{9,1... | collective-permute-start | bytes 786440 | tf_op jit(solution)/shard_map/ppermute | solution.py:15
  7.8 18.4 %collective-permute-start.10 = (bf16[64,1024]{1,0:T(8,128)(2,1)}, bf16[64,1024]{1,0:T(8,128)(2,1)}, u32[]{:S(2)}, u32[]{:S(2)}) collective-permute-start(bf16[64,1024]{1,0:T(8,128)(2,1)} %dynamic-slice_bitcast_fusion), channel_id=1, source_target_pairs={{0,2},{2,0},{1,3},{3,1},{4,6},{6,4},{5,7},{7,5},{8,10},{10,8},{9,1... | collective-permute-start | bytes 393224 | tf_op jit(solution)/shard_map/ppermute | solution.py:15
  9.5 18.4 %collective-permute-start.14 = (bf16[128,512]{1,0:T(8,128)(2,1)}, bf16[128,512]{1,0:T(8,128)(2,1)S(1)}, u32[]{:S(2)}, u32[]{:S(2)}) collective-permute-start(bf16[128,512]{1,0:T(8,128)(2,1)} %constant_dynamic-slice_fusion.4), channel_id=1, source_target_pairs={{0,2},{2,0},{1,3},{3,1},{4,6},{6,4},{5,7},{7,5},{8,10},{10,8},{9,1... | collective-permute-start | bytes 393224 | tf_op jit(solution)/shard_map/ppermute | solution.py:15
  11.4 18.1 %collective-permute-start.1 = (bf16[256,512]{1,0:T(8,128)(2,1)}, bf16[256,512]{1,0:T(8,128)(2,1)}, u32[]{:S(2)}, u32[]{:S(2)}) collective-permute-start(bf16[256,512]{1,0:T(8,128)(2,1)} %param.9), channel_id=1, source_target_pairs={{0,2},{2,0},{1,3},{3,1},{4,6},{6,4},{5,7},{7,5},{8,10},{10,8},{9,1... | collective-permute-start | bytes 786440 | tf_op jit(solution)/shard_map/ppermute | solution.py:15
  11.6 13.6 %collective-permute-start.18 = (f32[512]{0:T(512)}, f32[512]{0:T(512)}, u32[]{:S(2)}, u32[]{:S(2)}) collective-permute-start(f32[512]{0:T(512)} %param.17), channel_id=1, source_target_pairs={{0,2},{2,0},{1,3},{3,1},{4,6},{6,4},{5,7},{7,5},{8,10},{10,8},{9,1... | collective-permute-start | bytes 6152 | tf_op jit(solution)/shard_map/ppermute | solution.py:15
  23.4 11.1 %copy-start.11 = (s32[256]{0:T(256)S(1)}, s32[256]{0:T(256)}, u32[]{:S(2)}) copy-start(s32[256]{0:T(256)} %get-tuple-element.33) | copy-start | bytes 3076
  23.4 12.3 %copy-start.17 = (s32[64]{0:T(128)S(1)}, s32[64]{0:T(128)}, u32[]{:S(2)}) copy-start(s32[64]{0:T(128)} %get-tuple-element.41) | copy-start | bytes 772
  23.5 12.5 %copy-start.10 = (s32[256]{0:T(256)S(1)}, s32[256]{0:T(256)}, u32[]{:S(2)}) copy-start(s32[256]{0:T(256)} %get-tuple-element.31) | copy-start | bytes 3076
  23.5 15.2 %copy-start.16 = (s32[64]{0:T(128)S(1)}, s32[64]{0:T(128)}, u32[]{:S(2)}) copy-start(s32[64]{0:T(128)} %get-tuple-element.40) | copy-start | bytes 772
  25.2 58.2 %collective-permute-start.22 = (bf16[256,512]{1,0:T(8,128)(2,1)}, bf16[256,512]{1,0:T(8,128)(2,1)S(1)}, u32[]{:S(2)}, u32[]{:S(2)}) collective-permute-start(bf16[256,512]{1,0:T(8,128)(2,1)} %get-tuple-element.12), channel_id=1, source_target_pairs={{0,2},{2,0},{1,3},{3,1},{4,6},{6,4},{5,7},{7,5},{8,10},{10,8},{9,1... | collective-permute-start | bytes 786440 | tf_op jit(solution)/shard_map/ppermute | solution.py:15
  26.2 66.5 %collective-permute-start.20 = (bf16[256,512]{1,0:T(8,128)(2,1)}, bf16[256,512]{1,0:T(8,128)(2,1)}, u32[]{:S(2)}, u32[]{:S(2)}) collective-permute-start(bf16[256,512]{1,0:T(8,128)(2,1)} %get-tuple-element.9), channel_id=1, source_target_pairs={{0,2},{2,0},{1,3},{3,1},{4,6},{6,4},{5,7},{7,5},{8,10},{10,8},{9,1... | collective-permute-start | bytes 786440 | tf_op jit(solution)/shard_map/ppermute | solution.py:15
  28.0 10.9 %collective-permute-start.11 = (bf16[64,1024]{1,0:T(8,128)(2,1)}, bf16[64,1024]{1,0:T(8,128)(2,1)S(1)}, u32[]{:S(2)}, u32[]{:S(2)}) collective-permute-start(bf16[64,1024]{1,0:T(8,128)(2,1)} %collective-permute-done.10), channel_id=1, source_target_pairs={{0,4},{4,0},{8,12},{12,8},{1,5},{5,1},{9,13},{13,9},{2,6},{6,2},{1... | collective-permute-start | bytes 393224 | tf_op jit(solution)/shard_map/ppermute | solution.py:20
  29.5 15.4 %collective-permute-start.15 = (bf16[128,512]{1,0:T(8,128)(2,1)S(1)}, bf16[128,512]{1,0:T(8,128)(2,1)S(1)}, u32[]{:S(2)}, u32[]{:S(2)}) collective-permute-start(bf16[128,512]{1,0:T(8,128)(2,1)S(1)} %collective-permute-done.14), channel_id=1, source_target_pairs={{0,4},{4,0},{8,12},{12,8},{1,5},{5,1},{9,13},{13,9},{2,6},{6,2},{1... | collective-permute-start | bytes 393224 | tf_op jit(solution)/shard_map/ppermute | solution.py:20
  37.1 30.2 %copy-start.15 = (s32[256]{0:T(256)S(1)}, s32[256]{0:T(256)}, u32[]{:S(2)}) copy-start(s32[256]{0:T(256)} %get-tuple-element.35) | copy-start | bytes 3076
  37.1 6.6 %collective-permute-start.7 = (bf16[2,64,1024]{2,1,0:T(8,128)(2,1)}, bf16[2,64,1024]{2,1,0:T(8,128)(2,1)S(1)}, u32[]{:S(2)}, u32[]{:S(2)}) collective-permute-start(bf16[2,64,1024]{2,1,0:T(8,128)(2,1)} %collective-permute-done.6), channel_id=1, source_target_pairs={{0,16},{16,0},{1,17},{17,1},{2,18},{18,2},{3,19},{19,3},{4,20},{20... | collective-permute-start | bytes 786440 | tf_op jit(solution)/shard_map/ppermute | solution.py:20
  38.9 7.7 %collective-permute-start.2 = (bf16[64,1024]{1,0:T(8,128)(2,1)S(1)}, bf16[64,1024]{1,0:T(8,128)(2,1)S(1)}, u32[]{:S(2)}, u32[]{:S(2)}) collective-permute-start(bf16[64,1024]{1,0:T(8,128)(2,1)S(1)} %convolution_convert_fusion.9), channel_id=1, source_target_pairs={{0,12},{1,13},{4,0},{5,1},{8,4},{9,5},{12,8},{13,9},{2,14},{3,15},... | collective-permute-start | bytes 393224 | tf_op jit(solution)/shard_map/ppermute | solution.py:15
  43.7 3.2 %collective-permute-start.3 = (bf16[64,1024]{1,0:T(8,128)(2,1)S(1)}, bf16[64,1024]{1,0:T(8,128)(2,1)S(1)}, u32[]{:S(2)}, u32[]{:S(2)}) collective-permute-start(bf16[64,1024]{1,0:T(8,128)(2,1)S(1)} %convolution_convert_fusion.8), channel_id=1, source_target_pairs={{0,13},{1,0},{4,1},{5,4},{8,5},{9,8},{12,9},{13,12},{2,15},{3,2},{... | collective-permute-start | bytes 393224 | tf_op jit(solution)/shard_map/ppermute | solution.py:15
  44.9 31.3 %copy-start.14 = (s32[256]{0:T(256)S(1)}, s32[256]{0:T(256)}, u32[]{:S(2)}) copy-start(s32[256]{0:T(256)} %get-tuple-element.36) | copy-start | bytes 3076
  44.9 21.2 %collective-permute-start.8 = (bf16[2,128,1024]{2,1,0:T(8,128)(2,1)S(1)}, bf16[2,128,1024]{2,1,0:T(8,128)(2,1)S(1)}, u32[]{:S(2)}, u32[]{:S(2)}) collective-permute-start(bf16[2,128,1024]{2,1,0:T(8,128)(2,1)S(1)} %maximum_select_fusion.4), channel_id=1, source_target_pairs={{0,4},{4,0},{8,12},{12,8},{1,5},{5,1},{9,13},{13,9},{2,6},{6,2},{1... | collective-permute-start | bytes 1572872 | tf_op jit(solution)/shard_map/ppermute | solution.py:20
  46.7 17.3 %collective-permute-start.4 = (bf16[64,1024]{1,0:T(8,128)(2,1)S(1)}, bf16[64,1024]{1,0:T(8,128)(2,1)S(1)}, u32[]{:S(2)}, u32[]{:S(2)}) collective-permute-start(bf16[64,1024]{1,0:T(8,128)(2,1)S(1)} %convolution_convert_fusion.7), channel_id=1, source_target_pairs={{0,1},{1,4},{4,5},{5,8},{8,9},{9,12},{12,13},{13,0},{2,3},{3,6},{6... | collective-permute-start | bytes 393224 | tf_op jit(solution)/shard_map/ppermute | solution.py:15
  47.0 18.5 %collective-permute-start.5 = (bf16[64,1024]{1,0:T(8,128)(2,1)S(1)}, bf16[64,1024]{1,0:T(8,128)(2,1)S(1)}, u32[]{:S(2)}, u32[]{:S(2)}) collective-permute-start(bf16[64,1024]{1,0:T(8,128)(2,1)S(1)} %convolution_convert_fusion.6), channel_id=1, source_target_pairs={{0,4},{1,5},{4,8},{5,9},{8,12},{9,13},{12,0},{13,1},{2,6},{3,7},{6... | collective-permute-start | bytes 393224 | tf_op jit(solution)/shard_map/ppermute | solution.py:15
  64.0 14.9 %collective-permute-start.12 = (bf16[128,1024]{1,0:T(8,128)(2,1)S(1)}, bf16[128,1024]{1,0:T(8,128)(2,1)S(1)}, u32[]{:S(2)}, u32[]{:S(2)}) collective-permute-start(bf16[128,1024]{1,0:T(8,128)(2,1)S(1)} %maximum_select_fusion.7), channel_id=1, source_target_pairs={{0,16},{16,0},{1,17},{17,1},{2,18},{18,2},{3,19},{19,3},{4,20},{20... | collective-permute-start | bytes 786440 | tf_op jit(solution)/shard_map/ppermute | solution.py:20
  65.5 10.4 %collective-permute-start.16 = (bf16[256,512]{1,0:T(8,128)(2,1)S(1)}, bf16[256,512]{1,0:T(8,128)(2,1)S(1)}, u32[]{:S(2)}, u32[]{:S(2)}) collective-permute-start(bf16[256,512]{1,0:T(8,128)(2,1)S(1)} %maximum_select_fusion.8), channel_id=1, source_target_pairs={{0,16},{16,0},{1,17},{17,1},{2,18},{18,2},{3,19},{19,3},{4,20},{20... | collective-permute-start | bytes 786440 | tf_op jit(solution)/shard_map/ppermute | solution.py:20
  66.2 11.4 %copy-start.13 = (s32[256]{0:T(256)S(1)}, s32[256]{0:T(256)}, u32[]{:S(2)}) copy-start(s32[256]{0:T(256)} %get-tuple-element.34) | copy-start | bytes 3076
  66.2 15.3 %slice-start.1 = ((s8[6291456]{0:T(1024)(128)(4,1)}), s8[4194304]{0:T(1024)(128)(4,1)S(1)}, s32[]{:S(2)}) async-start(s8[6291456]{0:T(1024)(128)(4,1)} %bitcast.41), calls=%async_computation.1 | async-start | bytes 8388608
  66.7 13.7 %collective-permute-start.9 = (bf16[2,256,1024]{2,1,0:T(8,128)(2,1)S(1)}, bf16[2,256,1024]{2,1,0:T(8,128)(2,1)S(1)}, u32[]{:S(2)}, u32[]{:S(2)}) collective-permute-start(bf16[2,256,1024]{2,1,0:T(8,128)(2,1)S(1)} %maximum_select_fusion.1), channel_id=1, source_target_pairs={{0,1},{1,0},{2,3},{3,2},{4,5},{5,4},{6,7},{7,6},{8,9},{9,8},{10,11... | collective-permute-start | bytes 3145736 | tf_op jit(solution)/shard_map/ppermute | solution.py:20
  76.2 3.5 %collective-permute-start.17 = (bf16[512,512]{1,0:T(8,128)(2,1)S(1)}, bf16[512,512]{1,0:T(8,128)(2,1)S(1)}, u32[]{:S(2)}, u32[]{:S(2)}) collective-permute-start(bf16[512,512]{1,0:T(8,128)(2,1)S(1)} %maximum_select_fusion.6), channel_id=1, source_target_pairs={{0,1},{1,0},{2,3},{3,2},{4,5},{5,4},{6,7},{7,6},{8,9},{9,8},{10,11... | collective-permute-start | bytes 1572872 | tf_op jit(solution)/shard_map/ppermute | solution.py:20
  77.6 3.8 %slice-start.2 = ((s8[6291456]{0:T(1024)(128)(4,1)}), s8[2097152]{0:T(1024)(128)(4,1)S(1)}, s32[]{:S(2)}) async-start(s8[6291456]{0:T(1024)(128)(4,1)} %bitcast.41), calls=%async_computation.2 | async-start | bytes 4194304
  78.9 20.0 %collective-permute-start = (bf16[256,512]{1,0:T(8,128)(2,1)}, bf16[256,512]{1,0:T(8,128)(2,1)}, u32[]{:S(2)}, u32[]{:S(2)}) collective-permute-start(bf16[256,512]{1,0:T(8,128)(2,1)} %get-tuple-element.11), channel_id=1, source_target_pairs={{0,2},{2,0},{1,3},{3,1},{4,6},{6,4},{5,7},{7,5},{8,10},{10,8},{9,1... | collective-permute-start | bytes 786440 | tf_op jit(solution)/shard_map/ppermute | solution.py:15
  79.7 3.3 %collective-permute-start.13 = (bf16[256,1024]{1,0:T(8,128)(2,1)S(1)}, bf16[256,1024]{1,0:T(8,128)(2,1)S(1)}, u32[]{:S(2)}, u32[]{:S(2)}) collective-permute-start(bf16[256,1024]{1,0:T(8,128)(2,1)S(1)} %maximum_select_fusion.5), channel_id=1, source_target_pairs={{0,1},{1,0},{2,3},{3,2},{4,5},{5,4},{6,7},{7,6},{8,9},{9,8},{10,11... | collective-permute-start | bytes 1572872 | tf_op jit(solution)/shard_map/ppermute | solution.py:20
  80.4 6.4 %copy-start.4 = (bf16[1024,512]{1,0:T(8,128)(2,1)}, bf16[1024,512]{1,0:T(8,128)(2,1)S(1)}, u32[]{:S(2)}) copy-start(bf16[1024,512]{1,0:T(8,128)(2,1)S(1)} %maximum_select_fusion.3) | copy-start | bytes 3145732
  80.4 2.3 %copy-start = (bf16[3,512,1024]{2,1,0:T(8,128)(2,1)S(1)}, bf16[3,512,1024]{2,1,0:T(8,128)(2,1)}, u32[]{:S(2)}) copy-start(bf16[3,512,1024]{2,1,0:T(8,128)(2,1)} %param.15) | copy-start | bytes 9437188
  82.7 4.0 %copy-start.3 = (bf16[256,512]{1,0:T(8,128)(2,1)S(1)}, bf16[256,512]{1,0:T(8,128)(2,1)}, u32[]{:S(2)}) copy-start(bf16[256,512]{1,0:T(8,128)(2,1)} %get-tuple-element.13) | copy-start | bytes 786436
  83.4 2.7 %copy-start.7 = (bf16[3072,1024]{1,0:T(8,128)(2,1)}, bf16[3072,1024]{1,0:T(8,128)(2,1)S(1)}, u32[]{:S(2)}) copy-start(bf16[3072,1024]{1,0:T(8,128)(2,1)S(1)} %fusion.27) | copy-start | bytes 18874372
  86.1 0.7 copy-start.6
  86.8 6.0 %copy-start.2 = (bf16[256,512]{1,0:T(8,128)(2,1)S(1)}, bf16[256,512]{1,0:T(8,128)(2,1)}, u32[]{:S(2)}) copy-start(bf16[256,512]{1,0:T(8,128)(2,1)} %get-tuple-element.10) | copy-start | bytes 786436
  86.8 6.0 %copy-start.5 = (bf16[256,1024]{1,0:T(8,128)(2,1)S(1)}, bf16[256,1024]{1,0:T(8,128)(2,1)}, u32[]{:S(2)}) copy-start(bf16[256,1024]{1,0:T(8,128)(2,1)} %convolution_convert_fusion.4) | copy-start | bytes 1572868
  98.9 6.2 %copy-start.21 = (pred[256]{0:T(512)(128)(4,1)S(1)}, pred[256]{0:T(512)(128)(4,1)}, u32[]{:S(2)}) copy-start(pred[256]{0:T(512)(128)(4,1)} %add_compare_fusion.2) | copy-start | bytes 772
  98.9 6.2 %copy-start.22 = (pred[256]{0:T(512)(128)(4,1)S(1)}, pred[256]{0:T(512)(128)(4,1)}, u32[]{:S(2)}) copy-start(pred[256]{0:T(512)(128)(4,1)} %add_compare_fusion.3) | copy-start | bytes 772
  98.9 6.2 %copy-start.23 = (pred[256]{0:T(512)(128)(4,1)S(1)}, pred[256]{0:T(512)(128)(4,1)}, u32[]{:S(2)}) copy-start(pred[256]{0:T(512)(128)(4,1)} %add_compare_fusion.4) | copy-start | bytes 772
  107.7 9.3 %copy-start.19 = (pred[512]{0:T(512)(128)(4,1)S(1)}, pred[512]{0:T(512)(128)(4,1)}, u32[]{:S(2)}) copy-start(pred[512]{0:T(512)(128)(4,1)} %get-tuple-element.56) | copy-start | bytes 1540
  107.8 19.9 %copy-start.18 = (pred[512]{0:T(512)(128)(4,1)S(1)}, pred[512]{0:T(512)(128)(4,1)}, u32[]{:S(2)}) copy-start(pred[512]{0:T(512)(128)(4,1)} %get-tuple-element.55) | copy-start | bytes 1540
  107.8 9.2 %collective-permute-start.21 = (bf16[256,512]{1,0:T(8,128)(2,1)S(1)}, bf16[256,512]{1,0:T(8,128)(2,1)S(1)}, u32[]{:S(2)}, u32[]{:S(2)}) collective-permute-start(bf16[256,512]{1,0:T(8,128)(2,1)S(1)} %get-tuple-element.20), channel_id=1, source_target_pairs={{0,2},{2,0},{1,3},{3,1},{4,6},{6,4},{5,7},{7,5},{8,10},{10,8},{9,1... | collective-permute-start | bytes 786440 | tf_op jit(solution)/shard_map/ppermute | solution.py:15
  109.3 18.7 %collective-permute-start.19 = (bf16[256,512]{1,0:T(8,128)(2,1)S(1)}, bf16[256,512]{1,0:T(8,128)(2,1)S(1)}, u32[]{:S(2)}, u32[]{:S(2)}) collective-permute-start(bf16[256,512]{1,0:T(8,128)(2,1)S(1)} %get-tuple-element.18), channel_id=1, source_target_pairs={{0,2},{2,0},{1,3},{3,1},{4,6},{6,4},{5,7},{7,5},{8,10},{10,8},{9,1... | collective-permute-start | bytes 786440 | tf_op jit(solution)/shard_map/ppermute | solution.py:15
  110.0 18.1 %copy-start.20 = (pred[512]{0:T(512)(128)(4,1)S(1)}, pred[512]{0:T(512)(128)(4,1)}, u32[]{:S(2)}) copy-start(pred[512]{0:T(512)(128)(4,1)} %iota_compare_fusion.25) | copy-start | bytes 1540
  110.1 17.5 %collective-permute-start.23 = (bf16[256,512]{1,0:T(8,128)(2,1)S(1)}, bf16[256,512]{1,0:T(8,128)(2,1)S(1)}, u32[]{:S(2)}, u32[]{:S(2)}) collective-permute-start(bf16[256,512]{1,0:T(8,128)(2,1)S(1)} %get-tuple-element.22), channel_id=1, source_target_pairs={{0,2},{2,0},{1,3},{3,1},{4,6},{6,4},{5,7},{7,5},{8,10},{10,8},{9,1... | collective-permute-start | bytes 786440 | tf_op jit(solution)/shard_map/ppermute | solution.py:15
  128.1 8.4 %copy-start.12 = (s32[256]{0:T(256)S(1)}, s32[256]{0:T(256)}, u32[]{:S(2)}) copy-start(s32[256]{0:T(256)} %eq.282) | copy-start | bytes 3076
  128.6 6.9 %collective-permute-start.24 = (bf16[64,512]{1,0:T(8,128)(2,1)S(1)}, bf16[64,512]{1,0:T(8,128)(2,1)S(1)}, u32[]{:S(2)}, u32[]{:S(2)}) collective-permute-start(bf16[64,512]{1,0:T(8,128)(2,1)S(1)} %get-tuple-element.14), channel_id=1, source_target_pairs={{0,4},{1,5},{4,8},{5,9},{8,12},{9,13},{12,0},{13,1},{2,6},{3,7},{6... | collective-permute-start | bytes 196616 | tf_op jit(solution)/shard_map/ppermute | solution.py:15
  128.7 6.8 %collective-permute-start.25 = (bf16[64,512]{1,0:T(8,128)(2,1)S(1)}, bf16[64,512]{1,0:T(8,128)(2,1)S(1)}, u32[]{:S(2)}, u32[]{:S(2)}) collective-permute-start(bf16[64,512]{1,0:T(8,128)(2,1)S(1)} %get-tuple-element.17), channel_id=1, source_target_pairs={{0,1},{1,4},{4,5},{5,8},{8,9},{9,12},{12,13},{13,0},{2,3},{3,6},{6... | collective-permute-start | bytes 196616 | tf_op jit(solution)/shard_map/ppermute | solution.py:15
  128.7 6.7 %collective-permute-start.26 = (bf16[64,512]{1,0:T(8,128)(2,1)S(1)}, bf16[64,512]{1,0:T(8,128)(2,1)S(1)}, u32[]{:S(2)}, u32[]{:S(2)}) collective-permute-start(bf16[64,512]{1,0:T(8,128)(2,1)S(1)} %get-tuple-element.16), channel_id=1, source_target_pairs={{0,13},{1,0},{4,1},{5,4},{8,5},{9,8},{12,9},{13,12},{2,15},{3,2},{... | collective-permute-start | bytes 196616 | tf_op jit(solution)/shard_map/ppermute | solution.py:15
  132.3 4.3 %collective-permute-start.27 = (bf16[64,512]{1,0:T(8,128)(2,1)S(1)}, bf16[64,512]{1,0:T(8,128)(2,1)S(1)}, u32[]{:S(2)}, u32[]{:S(2)}) collective-permute-start(bf16[64,512]{1,0:T(8,128)(2,1)S(1)} %get-tuple-element.15), channel_id=1, source_target_pairs={{0,12},{1,13},{4,0},{5,1},{8,4},{9,5},{12,8},{13,9},{2,14},{3,15},... | collective-permute-start | bytes 196616 | tf_op jit(solution)/shard_map/ppermute | solution.py:15

commit v2 on v0

v2 whole, which is shorter than its diff:
```python
import functools

import jax
import jax.numpy as jnp
from jax import lax
from jax.experimental import pallas as pl
from jax.experimental.pallas import tpu as pltpu
from jax.sharding import PartitionSpec as P

TILE = 128
RADIUS = 2
GAIN_ROWS = 16
SHARERS_A = ("dom", "rep")
SHARERS_B = ("groups", "rep")
bf16 = jnp.bfloat16
f32 = jnp.float32
i32 = jnp.int32
VMEM_BYTES = 24 * 1024 * 1024
PREPARE_VMEM_BYTES = 60 * 1024 * 1024
HBM = pl.BlockSpec(memory_space=pltpu.HBM)
VMEM = pl.BlockSpec(memory_space=pltpu.VMEM)
SMEM = pl.BlockSpec(memory_space=pltpu.SMEM)


def shape(*dims, dtype=bf16):
    return jax.ShapeDtypeStruct(dims, dtype)


def params(vmem=VMEM_BYTES):
    return pltpu.CompilerParams(vmem_limit_bytes=vmem)


def shifted(block, axis, distance):
    size = lax.axis_size(axis)
    return lax.ppermute(block, axis, [(i, (i + distance) % size) for i in range(size)])


def swapped(block, axis):
    size = lax.axis_size(axis)
    return lax.ppermute(block, axis, [(i, i ^ 1) for i in range(size)])


def even(axes):
    return [axis for axis in axes if lax.axis_size(axis) % 2 == 0]


def share_index(axes):
    return sum((lax.axis_index(axis) % 2) << place for place, axis in enumerate(axes))


def tie(array, *others):
    return lax.optimization_barrier((array, *others))[0]


def dot(a, b):
    return jnp.dot(a, b, preferred_element_type=f32)


def column(row):
    return jnp.transpose(jnp.broadcast_to(row, (128, row.shape[1])))


def onehot(ids, count):
    lanes = lax.broadcasted_iota(i32, ids.shape, 1)
    hits = [(ids == lanes + base).astype(f32).astype(bf16) for base in range(0, count, 128)]
    return jnp.concatenate(hits, axis=1) if len(hits) > 1 else hits[0]


def copier(sems):
    copies = []

    def copy(source, target):
        copies.append(pltpu.make_async_copy(source, target, sems.at[len(copies)]))
        copies[-1].start()

    def finish():
        for c in copies:
            c.wait()

    return copy, finish


def share_kernel(ways, axes_a, axes_b, w_in, w_out, nodes, gain, first, second, sems):
    copy, finish = copier(sems)
    width = w_out.shape[1]
    rows_a, rows_b = width >> len(axes_a), width >> len(axes_b)
    start_a = pl.multiple_of(share_index(axes_a) * rows_a, rows_a)
    start_b = pl.multiple_of(share_index(axes_b) * rows_b, rows_b)
    for part in range(2):
        copy(w_in.at[part, pl.ds(start_a, rows_a), :], first.at[pl.ds(part * rows_a, rows_a), :])
    copy(w_in.at[2, pl.ds(start_b, rows_b), :], second.at[0])
    for h in range(ways):
        copy(w_out.at[pl.ds(h * width + start_b, rows_b), :], second.at[1, :, pl.ds(h * width, width)])
    base = 2 * rows_a
    count = nodes.shape[0] // ways
    for h in range(ways):
        copy(nodes.at[pl.ds(h * count, count), :], first.at[pl.ds(base, count), pl.ds(h * width, width)])
    high = gain[...].astype(bf16)
    middle = (gain[...] - high.astype(f32)).astype(bf16)
    low = (gain[...] - high.astype(f32) - middle.astype(f32)).astype(bf16)
    row_ids = lax.broadcasted_iota(i32, (GAIN_ROWS, width), 0)
    rows = jnp.where(row_ids == 0, high.astype(f32), 0.0)
    rows = jnp.where(row_ids == 1, middle.astype(f32), rows)
    rows = jnp.where(row_ids == 2, low.astype(f32), rows)
    first[base + count :, :] = jnp.concatenate([rows.astype(bf16)] * ways, axis=1)
    finish()


def prepare_shares(weight_in, weight_out, nodes, gain, ways, axes_a, axes_b):
    width = weight_out.shape[1]
    rows = 2 * (width >> len(axes_a)) + nodes.shape[0] // ways + GAIN_ROWS
    return pl.pallas_call(
        functools.partial(share_kernel, ways, axes_a, axes_b),
        out_shape=[shape(rows, ways * width), shape(2, width >> len(axes_b), ways * width)],
        in_specs=[HBM, HBM, HBM, VMEM],
        out_specs=[VMEM] * 2,
        scratch_shapes=[pltpu.SemaphoreType.DMA((3 + 2 * ways,))],
        compiler_params=params(PREPARE_VMEM_BYTES),
        name="prepare_shares",
    )(weight_in, weight_out, nodes, gain)


def block_kernel(ways, edges, *rest):
    blocks, sems = rest[:-1], rest[-1]
    copy, finish = copier(sems)
    me = lax.axis_index("chan")
    mine = edges.shape[0] // ways
    for d in range(1, ways):
        row = pl.multiple_of(lax.rem(me + d, ways) * mine, TILE)
        copy(edges.at[pl.ds(row, mine), :], blocks[d - 1])
    finish()


def prepare_blocks(edge_feats, ways):
    slot_count, width = edge_feats.shape
    return pl.pallas_call(
        functools.partial(block_kernel, ways),
        out_shape=[shape(slot_count // ways, width)] * (ways - 1),
        in_specs=[HBM],
        out_specs=[VMEM] * (ways - 1),
        scratch_shapes=[pltpu.SemaphoreType.DMA((ways - 1,))],
        compiler_params=params(),
        name="prepare_blocks",
    )(edge_feats)


def unpack_kernel(ways, halo_count, rows_ref, nodes, *refs):
    messages, outs = refs[: ways - 1], list(refs[ways - 1 :])
    halos = [outs.pop(0) for _ in range(halo_count)]
    pieces, others, gains = (outs[i :: 3] for i in range(3))
    count, width = nodes.shape
    for d in range(1, ways):
        message, piece, other, gain = messages[d - 1], pieces[d - 1], others[d - 1], gains[d - 1]
        rows = piece.shape[1]
        for part in range(2):
            piece[part] = message[part * rows : (part + 1) * rows, :]
        base, packed = 2 * rows, count // ways
        for h in range(ways):
            other[h * packed : (h + 1) * packed, :] = message[base : base + packed, h * width : (h + 1) * width]
        parts = message[base + packed :, :width].astype(f32)
        gain[...] = parts[0:1, :] + parts[1:2, :] + parts[2:3, :]
    for j in range(halo_count):
        hits = onehot(column(rows_ref[0, j : j + 1, :]), count)
        for d in range(ways):
            table = nodes[...] if d == 0 else others[d - 1][...]
            halos[j][:, d * width : (d + 1) * width] = dot(hits, table).astype(bf16)


def unpack(halo_rows, nodes, messages, ways, axes_a):
    _, offsets, size = halo_rows.shape
    count, width = nodes.shape
    each = [shape(2, width >> len(axes_a), ways * width), shape(count, width), shape(1, width, dtype=f32)]
    outs = pl.pallas_call(
        functools.partial(unpack_kernel, ways, offsets),
        out_shape=[shape(size, ways * width)] * offsets + each * (ways - 1),
        compiler_params=params(),
        cost_estimate=pl.CostEstimate(flops=6000000 * 1000, bytes_accessed=4 * 1024 * 1024, transcendentals=0),
        name="unpack",
    )(halo_rows, nodes, *messages)
    return (outs[:offsets], *(outs[offsets + i :: 3] for i in range(3)))


def gather_shares(piece, axes):
    pieces = [piece]
    for axis in axes:
        pieces = pieces + [swapped(p, axis) for p in pieces]
    return pieces


def assemble_kernel(axes, *refs):
    pieces, out = refs[:-1], refs[-1]
    share = share_index(axes)
    rows = pieces[0].shape[1]
    for m, piece in enumerate(pieces):
        start = pl.multiple_of((share ^ m) * rows, rows)
        for part in range(out.shape[0]):
            out[part, pl.ds(start, rows), :] = piece[part]


def assemble(pieces, axes):
    parts, rows, channels = pieces[0].shape
    return pl.pallas_call(
        functools.partial(assemble_kernel, axes),
        out_shape=shape(parts, rows * len(pieces), channels),
        compiler_params=params(),
        name="assemble",
    )(*pieces)


def split_rows(slot_count, ways):
    tiles = slot_count // (ways * TILE)
    first = -(-tiles // 3)
    second = (tiles - first + 1) // 2
    return [size * TILE for size in (first, second, tiles - first - second) if size]


def starts_of(sizes):
    return [sum(sizes[:k]) for k in range(len(sizes))]


def edge_kernel(ways, before, mine, counts, sender_ref, slot_ref, *refs):
    refs = list(refs)

    def take(count):
        taken = refs[:count]
        del refs[:count]
        return taken

    own, nodes, gains, halos = take(ways), take(ways), take(ways), take(2 * RADIUS)
    w_in, w_out = take(2)
    others_a, others_b = take(ways - 1), take(ways - 1)
    outs = refs
    width = own[0].shape[1]
    channels = ways * width
    me = lax.axis_index("chan")
    first = pl.multiple_of(me * (own[0].shape[0] // ways) + before, TILE)
    edges = [own[0][pl.ds(first, mine), :]] + [e[before : before + mine, :] for e in own[1:]]
    local_nodes = nodes[0].shape[0]
    halo_count = sum(h.shape[0] for h in halos)
    to_sender = onehot(column(sender_ref[:, pl.ds(first, mine)]), local_nodes)
    to_slot = onehot(column(slot_ref[:, pl.ds(first, mine)]), local_nodes + halo_count)
    table = jnp.concatenate([h[...] for h in halos], axis=0)
    preact = None
    for d in range(ways):
        if d == 0:
            weights = (w_in[0], w_in[1], w_in[2])
        else:
            weights = (others_a[d - 1][0], others_a[d - 1][1], others_b[d - 1][0])
        sent = dot(to_sender, nodes[d][...]).astype(bf16)
        got = dot(to_slot[:, :local_nodes], nodes[d][...])
        got = (got + dot(to_slot[:, local_nodes:], table[:, d * width : (d + 1) * width])).astype(bf16)
        term = dot(edges[d], weights[0]) + dot(sent, weights[1]) + dot(got, weights[2])
        preact = term if preact is None else preact + term
    hidden = (preact / (1.0 + jnp.exp(-preact))).astype(bf16)
    projected = [dot(hidden, w_out[...])]
    for d in range(1, ways):
        blocks = [slice(h * width, (h + 1) * width) for h in range(ways)]
        projected.append(sum(dot(hidden[:, b], others_b[d - 1][1, :, b]) for b in blocks))
    mean = sum(jnp.sum(p, axis=1, keepdims=True) for p in projected) / channels
    square = sum(jnp.sum(p * p, axis=1, keepdims=True) for p in projected) / channels
    scale = lax.rsqrt(square - mean * mean + 1e-05)
    part = lax.axis_index("dom") * lax.axis_size("rep") + lax.axis_index("rep")
    live_rows = TILE * counts[part] - first
    live = lax.broadcasted_iota(i32, (mine, width), 0) < live_rows
    for d in range(ways):
        normed = (projected[d] - mean) * scale * gains[d][...]
        outs[d][...] = jnp.where(live, (edges[d].astype(f32) + normed).astype(bf16), edges[d])


def edge_update(k, before, mine, counts, senders, slots, edges, nodes, gains, halos, w_in, w_out, others_a, others_b):
    ways = len(nodes)
    width = edges[0].shape[1]
    channels = ways * width
    operands = [*edges, *nodes, *gains, *halos, w_in, w_out, *others_a, *others_b]
    return pl.pallas_call(
        functools.partial(edge_kernel, ways, before, mine),
        out_shape=[shape(mine, width)] * ways,
        in_specs=[SMEM] + [VMEM] * (2 + len(operands)),
        out_specs=[VMEM] * ways,
        compiler_params=params(),
        cost_estimate=pl.CostEstimate(
            flops=2 * mine * channels * (4 * channels + 768),
            bytes_accessed=8 * channels * channels,
            transcendentals=mine * channels,
        ),
        name=f"edge_update_{k}",
    )(counts, senders, slots, *operands)


def collect_kernel(ways, places, local_nodes, last, counts, slot_ref, *refs):
    refs = list(refs)
    parts = [refs.pop(0) for _ in places]
    sums = refs.pop(0)[...] if len(refs) > (1 + 2 * RADIUS if last else 1) else None
    me = lax.axis_index("chan")
    part = lax.axis_index("dom") * lax.axis_size("rep") + lax.axis_index("rep")
    live_rows = TILE * counts[part]
    whole = slot_ref.shape[1] // ways
    table_rows = refs[0].shape[0] + (sum(r.shape[0] for r in refs[1:]) if last else 0)
    for (d, before), block in zip(places, parts):
        mine = block.shape[0]
        first = pl.multiple_of(lax.rem(me + d, ways) * whole + before, TILE)
        slots = slot_ref[:, pl.ds(first, mine)]
        ids = first + lax.broadcasted_iota(i32, (1, mine), 1)
        slots = jnp.where(ids < live_rows, slots, -1)
        rows = lax.broadcasted_iota(i32, (table_rows, mine), 0)
        hits = (rows == jnp.broadcast_to(slots, (table_rows, mine))).astype(f32).astype(bf16)
        term = dot(hits, block[...])
        sums = term if sums is None else sums + term
    if not last:
        refs[0][...] = sums
        return
    refs[0][...] = sums[:local_nodes]
    start = local_nodes
    for out in refs[1:]:
        size = out.shape[0]
        out[...] = sums[start : start + size].astype(bf16)
        start += size


def collect(places, parts, sums, counts, slots, ways, local_nodes, halo_size, last):
    width = parts[0].shape[1]
    table_rows = local_nodes + 2 * RADIUS * halo_size
    before = [] if sums is None else [sums]
    if last:
        outs = [shape(local_nodes, width, dtype=f32)] + [shape(halo_size, width)] * (2 * RADIUS)
    else:
        outs = [shape(table_rows, width, dtype=f32)]
    return pl.pallas_call(
        functools.partial(collect_kernel, ways, places, local_nodes, last),
        out_shape=outs,
        in_specs=[SMEM] + [VMEM] * (1 + len(parts) + len(before)),
        out_specs=[VMEM] * len(outs),
        compiler_params=params(),
        name="collect",
    )(counts, slots, *parts, *before)


def finish_kernel(rows_ref, own, *refs):
    returned, out = refs[:-1], refs[-1]
    total = own[...]
    for j, rows in enumerate(returned):
        size = rows.shape[0]
        ids = lax.broadcasted_iota(i32, (own.shape[0], size), 0)
        hits = (ids == jnp.broadcast_to(rows_ref[0, j : j + 1, :], ids.shape)).astype(f32).astype(bf16)
        total = total + dot(hits, rows[...])
    out[...] = total


def finish(halo_rows, own, returned):
    return pl.pallas_call(
        finish_kernel,
        out_shape=shape(*own.shape, dtype=f32),
        compiler_params=params(),
        name="finish",
    )(halo_rows, own, *returned)


def local(
    node_feats,
    edge_feats,
    senders,
    receiver_slot,
    halo_rows,
    tile_counts,
    weight_in,
    weight_out,
    norm_gain,
):
    ways = lax.axis_size("chan")
    me = lax.axis_index("chan")
    offsets = [shift_by for shift_by in range(-RADIUS, RADIUS + 1) if shift_by != 0]
    local_nodes, width = node_feats.shape
    halo_size = halo_rows.shape[2]
    slot_count = edge_feats.shape[0]
    sizes = split_rows(slot_count, ways)
    whole = slot_count // ways
    distances = range(1, ways)
    axes_a, axes_b = even(SHARERS_A), even(SHARERS_B)

    gain = norm_gain.reshape(1, width)
    sender_row, slot_row = senders.reshape(1, -1), receiver_slot.reshape(1, -1)
    message_a, message_b = prepare_shares(weight_in, weight_out, node_feats, gain, ways, axes_a, axes_b)
    blocks = prepare_blocks(edge_feats, ways)
    blocks = [tie(block, sender_row, slot_row) for block in blocks]
    crossed_a = [shifted(message_a, "chan", d) for d in distances]
    crossed_b = [shifted(message_b, "chan", d) for d in distances]
    outgoing, pieces, nodes, gains = unpack(halo_rows, node_feats, crossed_a, ways, axes_a)
    nodes, gains = [node_feats, *nodes], [gain, *gains]
    halos = [shifted(rows, ("dom", "rep"), by) for rows, by in zip(outgoing, offsets)]
    edges = [edge_feats] + [shifted(blocks[d - 1], "chan", d) for d in distances]
    crossed_b = [tie(piece, *halos) for piece in crossed_b]
    others_a = [assemble(gather_shares(piece, axes_a), axes_a) for piece in pieces]
    others_b = [assemble(gather_shares(piece, axes_b), axes_b) for piece in crossed_b]

    def collected(places, parts, sums, last=False):
        return collect(places, parts, sums, tile_counts, slot_row, ways, local_nodes, halo_size, last)

    finished = jnp.zeros((slot_count, width), bf16)
    kept, arrived = [], []
    for k, (before, mine) in enumerate(zip(starts_of(sizes), sizes)):
        parts = edge_update(
            k, before, mine, tile_counts, sender_row, slot_row, edges, nodes, gains, halos,
            weight_in, weight_out, others_a, others_b,
        )
        edges[0] = tie(edges[0], *parts)
        kept.append(parts[0])
        arrived.append([shifted(parts[d], "chan", -d) for d in distances])
        for d, part in enumerate([parts[0], *arrived[-1]]):
            first = ((me + d) % ways) * whole + before
            finished = lax.dynamic_update_slice_in_dim(finished, part, first, 0)
    starts = starts_of(sizes)
    (sums,) = collected([(0, b) for b in starts], kept, None)
    for k in range(len(sizes) - 1):
        (sums,) = collected([(d, starts[k]) for d in distances], arrived[k], sums)
    own, *pieces = collected([(d, starts[-1]) for d in distances], arrived[-1], sums, True)
    returned = [shifted(piece, ("dom", "rep"), -by) for piece, by in zip(pieces, offsets)]
    return (finished, finish(halo_rows, own, returned))


def solution(mesh):
    placed = (
        P(("groups", "dom", "rep"), "chan"),
        P(("groups", "dom", "rep"), "chan"),
        P(("groups", "dom", "rep")),
        P(("groups", "dom", "rep")),
        P(("groups", "dom", "rep"), None, None),
        P("groups"),
        P(None, "chan", None),
        P(None, "chan"),
        P("chan"),
    )
    return jax.shard_map(
        local,
        mesh=mesh,
        in_specs=placed,
        out_specs=(P(("groups", "dom", "rep"), "chan"), P(("groups", "dom", "rep"), "chan")),
        check_vma=False,
    )
```

time: 258 us -> 92.5 us (0.36)
  waiting for transfers between devices: 152 us -> 48.6 us
  local copies, waits for them, and re-layouts: 34.1 us -> 0.31 us
  other arithmetic: 20.2 us -> 0 us
  Pallas kernels: 0 us -> 19.9 us
  matrix products: 17.8 us -> 0 us
  between operations: 14.8 us -> 0.91 us
  starting transfers between devices: 11.9 us -> 22.6 us
  blocking collectives: 6.9 us -> 0 us
    psum x1 -> x0, waiting for transfers between devices: 150 us -> none  [edge_update(): preact = lax.psum(partial_pre, 'chan')]
    ppermute x8 -> x20, waiting for transfers between devices: 1.3 us -> 48.6 us  [the longest x14 37.1 us: shifted(): lax.ppermute(block, axis, [(i, (i + distance) % size) for i in range(size)])]
    pallas_call x0 -> x13, Pallas kernels: none -> 19.9 us  [the longest x3 11.1 us: edge_update(): pl.pallas_call(functools.partial(edge_kernel, ways, before, mine), out_sh...]
    gather x6 -> x0, local copies, waits for them, and re-layouts: 19.2 us -> none  [the longest x4 7.15 us: local(): jnp.take(node_feats, halo_rows[0, slot_index], axis=0)]
    dot_general x4 -> x0, matrix products: 17.8 us -> none  [the longest x1 6.88 us: edge_update(): projected = jnp.dot(hidden, weight_out, preferred_element_type=jnp.float32)]
    select_n x9 -> x0, other arithmetic: 13.9 us -> none  [the longest x4 4.76 us: local(): jnp.take(node_feats, halo_rows[0, slot_index], axis=0)]
    unnamed x30 -> x20, local copies, waits for them, and re-layouts: 13 us -> 0.05 us
    ppermute x8 -> x20, starting transfers between devices: 11.9 us -> 22.6 us  [the longest x14 18.7 us: shifted(): lax.ppermute(block, axis, [(i, (i + distance) % size) for i in range(size)])]
  transfers between devices with their start and end apart: 9 -> 20, of which waited for: 2 -> 11; matrix products, arithmetic and copies ran while one was open for 14% -> 0% of each run, Pallas kernels for 0% -> 12%
where the time goes in v2:
time: 92.5 us; the launch traced here: 92.3 us
  waiting for transfers between devices  48.6 us (53%)
  starting transfers between devices  22.6 us (24%)
  Pallas kernels  19.9 us (22%)
    ppermute x14, waiting for transfers between devices, shifted(): lax.ppermute(block, axis, [(i, (i + distance) % size) for i in range(size)])  37.1 us
    ppermute x14, starting transfers between devices, shifted(): lax.ppermute(block, axis, [(i, (i + distance) % size) for i in range(size)])  18.7 us
    ppermute x6, waiting for transfers between devices, swapped(): return lax.ppermute(block, axis, [(i, i ^ 1) for i in range(size)])  11.5 us
    pallas_call x3, Pallas kernels, edge_update(): pl.pallas_call(functools.partial(edge_kernel, ways, before, mine), out_sh...  11.1 us
    ppermute x6, starting transfers between devices, swapped(): return lax.ppermute(block, axis, [(i, i ^ 1) for i in range(size)])  3.86 us
    pallas_call x4, Pallas kernels, collect(): pl.pallas_call(functools.partial(collect_kernel, ways, places, local_node...  3.6 us
    pallas_call x1, Pallas kernels, prepare_shares(): pl.pallas_call(functools.partial(share_kernel, ways, axes_a, axes_b), out...  3.12 us
  transfers between devices with their start and end apart: 20, of which 11 were waited for; matrix products, arithmetic and copies ran while one was open for 0% of the time, Pallas kernels for 12%

profile of v2, /device:TPU:0, one launch (start us, length us, event | category | flops | bytes accessed | tf_op | source)
XLA Modules:
  0.0 92.3 jit_solution(4937712991452605874)
XLA Ops:
  0.6 0.0 copy-start.3
  0.6 0.0 copy-start.6
  0.6 3.1 %prepare_shares.1 = (bf16[400,1024]{1,0:T(8,128)(2,1)}, bf16[2,128,1024]{2,1,0:T(8,128)(2,1)}) custom-call(bf16[3,512,1024]{2,1,0:T(8,128)(2,1)} %refs_10_.5, bf16[1024,512]{1,0:T(8,128)(2,1)} %refs_11_.5, bf16[256,512]{1,0:T(8,128)(2,1)} %refs_2_.5, f32[1,512]{1,0:T(1,128)} %bitcast.1), custom_call_target="tpu_custom_call" | custom-call | tf_op jit(solution)/shard_map/prepare_shares/pallas_call | solution.py:112
  3.8 3.0 %collective-permute-start.1 = (bf16[400,1024]{1,0:T(8,128)(2,1)}, bf16[400,1024]{1,0:T(8,128)(2,1)S(1)}, u32[]{:S(2)}, u32[]{:S(2)}) collective-permute-start(bf16[400,1024]{1,0:T(8,128)(2,1)} %get-tuple-element.27), channel_id=1, source_target_pairs={{0,2},{2,0},{1,3},{3,1},{4,6},{6,4},{5,7},{7,5},{8,10},{10,8},{9,1... | collective-permute-start | bytes 2457608 | tf_op jit(solution)/shard_map/ppermute | solution.py:35
  6.8 0.1 collective-permute-start.9
  6.9 19.2 %collective-permute-done.1.refs_0_ = bf16[400,1024]{1,0:T(8,128)(2,1)S(1)} collective-permute-done((bf16[400,1024]{1,0:T(8,128)(2,1)}, bf16[400,1024]{1,0:T(8,128)(2,1)S(1)}, u32[]{:S(2)}, u32[]{:S(2)}) %collective-permute-start.1) | collective-permute-done | bytes 819232 | tf_op jit(solution)/shard_map/ppermute | solution.py:35
  26.1 0.0 copy-done.6
  26.1 0.5 unpack.1
  26.6 4.2 %collective-permute-start.2 = (bf16[64,1024]{1,0:T(8,128)(2,1)S(1)}, bf16[64,1024]{1,0:T(8,128)(2,1)S(1)}, u32[]{:S(2)}, u32[]{:S(2)}) collective-permute-start(bf16[64,1024]{1,0:T(8,128)(2,1)S(1)} %get-tuple-element.30), channel_id=1, source_target_pairs={{0,12},{1,13},{4,0},{5,1},{8,4},{9,5},{12,8},{13,9},{2,14},{3,15},... | collective-permute-start | bytes 393224 | tf_op jit(solution)/shard_map/ppermute | solution.py:35
  30.8 0.0 collective-permute-start.3
  30.8 0.5 collective-permute-start.4
  31.3 0.0 collective-permute-start.5
  31.3 5.1 %collective-permute-done.9.refs_0_ = bf16[2,128,1024]{2,1,0:T(8,128)(2,1)S(1)} collective-permute-done((bf16[2,128,1024]{2,1,0:T(8,128)(2,1)}, bf16[2,128,1024]{2,1,0:T(8,128)(2,1)S(1)}, u32[]{:S(2)}, u32[]{:S(2)}) %collective-permute-start.9) | collective-permute-done | bytes 524320 | tf_op jit(solution)/shard_map/ppermute | solution.py:35
  36.5 1.8 %collective-permute-start.6 = (bf16[2,128,1024]{2,1,0:T(8,128)(2,1)S(1)}, bf16[2,128,1024]{2,1,0:T(8,128)(2,1)S(1)}, u32[]{:S(2)}, u32[]{:S(2)}) collective-permute-start(bf16[2,128,1024]{2,1,0:T(8,128)(2,1)S(1)} %get-tuple-element.34.refs_0_), channel_id=1, source_target_pairs={{0,4},{4,0},{8,12},{12,8},{1,5},{5,1},{9,13},{13,9},{2,6},{6,2},{1... | collective-permute-start | bytes 1572872 | tf_op jit(solution)/shard_map/ppermute | solution.py:40
  38.3 0.0 collective-permute-done.2.refs_6_
  38.3 0.0 collective-permute-done.3.refs_7_
  38.3 0.0 collective-permute-done.4.refs_8_
  38.3 1.7 %collective-permute-done.5.refs_9_ = bf16[64,1024]{1,0:T(8,128)(2,1)S(1)} collective-permute-done((bf16[64,1024]{1,0:T(8,128)(2,1)S(1)}, bf16[64,1024]{1,0:T(8,128)(2,1)S(1)}, u32[]{:S(2)}, u32[]{:S(2)}) %collective-permute-start.5) | collective-permute-done | bytes 131104 | tf_op jit(solution)/shard_map/ppermute | solution.py:35
  40.1 1.5 %collective-permute-start.10 = (bf16[2,128,1024]{2,1,0:T(8,128)(2,1)S(1)}, bf16[2,128,1024]{2,1,0:T(8,128)(2,1)S(1)}, u32[]{:S(2)}, u32[]{:S(2)}) collective-permute-start(bf16[2,128,1024]{2,1,0:T(8,128)(2,1)S(1)} %collective-permute-done.9.refs_0_), channel_id=1, source_target_pairs={{0,16},{16,0},{1,17},{17,1},{2,18},{18,2},{3,19},{19,3},{4,20},{20... | collective-permute-start | bytes 1572872 | tf_op jit(solution)/shard_map/ppermute | solution.py:40
  41.6 0.0 copy-done.8
  41.6 0.1 prepare_blocks.1
  41.7 1.6 %collective-permute-start = (bf16[768,512]{1,0:T(8,128)(2,1)S(1)}, bf16[768,512]{1,0:T(8,128)(2,1)S(1)}, u32[]{:S(2)}, u32[]{:S(2)}) collective-permute-start(bf16[768,512]{1,0:T(8,128)(2,1)S(1)} %prepare_blocks.1), channel_id=1, source_target_pairs={{0,2},{2,0},{1,3},{3,1},{4,6},{6,4},{5,7},{7,5},{8,10},{10,8},{9,1... | collective-permute-start | bytes 2359304 | tf_op jit(solution)/shard_map/ppermute | solution.py:35
  43.3 0.0 collective-permute-start.7
  43.3 7.8 %collective-permute-done.6.refs_1_ = bf16[2,128,1024]{2,1,0:T(8,128)(2,1)S(1)} collective-permute-done((bf16[2,128,1024]{2,1,0:T(8,128)(2,1)S(1)}, bf16[2,128,1024]{2,1,0:T(8,128)(2,1)S(1)}, u32[]{:S(2)}, u32[]{:S(2)}) %collective-permute-start.6) | collective-permute-done | bytes 524320 | tf_op jit(solution)/shard_map/ppermute | solution.py:40
  51.1 0.0 collective-permute-start.8
  51.1 0.5 collective-permute-start.11
  51.6 2.0 %collective-permute-done.10.refs_1_ = bf16[2,128,1024]{2,1,0:T(8,128)(2,1)S(1)} collective-permute-done((bf16[2,128,1024]{2,1,0:T(8,128)(2,1)S(1)}, bf16[2,128,1024]{2,1,0:T(8,128)(2,1)S(1)}, u32[]{:S(2)}, u32[]{:S(2)}) %collective-permute-start.10) | collective-permute-done | bytes 524320 | tf_op jit(solution)/shard_map/ppermute | solution.py:40
  53.6 0.0 collective-permute-start.12
  53.6 0.0 collective-permute-done.7.refs_2_
  53.6 0.0 collective-permute-done.8.refs_3_
  53.6 0.2 assemble.2.refs_12_
  53.8 0.0 copy-start
  53.8 0.0 copy-start.2
  53.8 0.0 copy-start.4
  53.8 0.0 copy-start.5
  53.8 0.0 collective-permute-done.11.refs_2_
  53.8 1.7 %collective-permute-done.12.refs_3_ = bf16[2,128,1024]{2,1,0:T(8,128)(2,1)S(1)} collective-permute-done((bf16[2,128,1024]{2,1,0:T(8,128)(2,1)S(1)}, bf16[2,128,1024]{2,1,0:T(8,128)(2,1)S(1)}, u32[]{:S(2)}, u32[]{:S(2)}) %collective-permute-start.12) | collective-permute-done | bytes 524320 | tf_op jit(solution)/shard_map/ppermute | solution.py:40
  55.5 0.2 assemble.3.refs_13_
  55.7 5.0 %collective-permute-done.refs_1_ = bf16[768,512]{1,0:T(8,128)(2,1)S(1)} collective-permute-done((bf16[768,512]{1,0:T(8,128)(2,1)S(1)}, bf16[768,512]{1,0:T(8,128)(2,1)S(1)}, u32[]{:S(2)}, u32[]{:S(2)}) %collective-permute-start) | collective-permute-done | bytes 786464 | tf_op jit(solution)/shard_map/ppermute | solution.py:35
  60.6 0.0 copy-done.2
  60.7 3.7 %edge_update_0.1 = (bf16[256,512]{1,0:T(8,128)(2,1)S(1)}, bf16[256,512]{1,0:T(8,128)(2,1)S(1)}) custom-call(s32[8]{0:T(128)S(1)} %copy-done.5, s32[1,1536]{1,0:T(1,128)S(1)} %reshape.13.sender_ref, s32[1,1536]{1,0:T(1,128)S(1)} %reshape.14.slot_ref, bf16[1536,512]{1,0:T(8,128)(2,1)S(1)} %copy-done.1, bf16[768,512]{1,0:T(8,128)(2,1)S(1)} %collective-permute-done.refs_1_, ...), custom_call_target="tpu_custom_call" | custom-call | flops 2550136832 | bytes 8388608 | tf_op jit(solution)/shard_map/edge_update_0/pallas_call | solution.py:275
  64.4 1.6 %collective-permute-start.13 = (bf16[256,512]{1,0:T(8,128)(2,1)S(1)}, bf16[256,512]{1,0:T(8,128)(2,1)S(1)}, u32[]{:S(2)}, u32[]{:S(2)}) collective-permute-start(bf16[256,512]{1,0:T(8,128)(2,1)S(1)} %get-tuple-element.38), channel_id=1, source_target_pairs={{0,2},{2,0},{1,3},{3,1},{4,6},{6,4},{5,7},{7,5},{8,10},{10,8},{9,1... | collective-permute-start | bytes 786440 | tf_op jit(solution)/shard_map/ppermute | solution.py:35
  65.9 3.7 %edge_update_1.1 = (bf16[256,512]{1,0:T(8,128)(2,1)S(1)}, bf16[256,512]{1,0:T(8,128)(2,1)S(1)}) custom-call(s32[8]{0:T(128)S(1)} %copy-done.5, s32[1,1536]{1,0:T(1,128)S(1)} %reshape.13.sender_ref, s32[1,1536]{1,0:T(1,128)S(1)} %reshape.14.slot_ref, bf16[1536,512]{1,0:T(8,128)(2,1)S(1)} %copy-done.1, bf16[768,512]{1,0:T(8,128)(2,1)S(1)} %collective-permute-done.refs_1_, ...), custom_call_target="tpu_custom_call" | custom-call | flops 2550136832 | bytes 8388608 | tf_op jit(solution)/shard_map/edge_update_1/pallas_call | solution.py:275
  69.6 0.6 collective-permute-start.14
  70.2 3.7 %edge_update_2.1 = (bf16[256,512]{1,0:T(8,128)(2,1)S(1)}, bf16[256,512]{1,0:T(8,128)(2,1)S(1)}) custom-call(s32[8]{0:T(128)S(1)} %copy-done.5, s32[1,1536]{1,0:T(1,128)S(1)} %reshape.13.sender_ref, s32[1,1536]{1,0:T(1,128)S(1)} %reshape.14.slot_ref, bf16[1536,512]{1,0:T(8,128)(2,1)S(1)} %copy-done.1, bf16[768,512]{1,0:T(8,128)(2,1)S(1)} %collective-permute-done.refs_1_, ...), custom_call_target="tpu_custom_call" | custom-call | flops 2550136832 | bytes 8388608 | tf_op jit(solution)/shard_map/edge_update_2/pallas_call | solution.py:275
  73.9 1.6 %collective-permute-start.15 = (bf16[256,512]{1,0:T(8,128)(2,1)S(1)}, bf16[256,512]{1,0:T(8,128)(2,1)S(1)}, u32[]{:S(2)}, u32[]{:S(2)}) collective-permute-start(bf16[256,512]{1,0:T(8,128)(2,1)S(1)} %get-tuple-element.44), channel_id=1, source_target_pairs={{0,2},{2,0},{1,3},{3,1},{4,6},{6,4},{5,7},{7,5},{8,10},{10,8},{9,1... | collective-permute-start | bytes 786440 | tf_op jit(solution)/shard_map/ppermute | solution.py:35
  75.5 1.1 %collect.4.refs_1_ = f32[512,512]{1,0:T(8,128)S(1)} custom-call(s32[8]{0:T(128)S(1)} %copy-done.5, s32[1,1536]{1,0:T(1,128)S(1)} %reshape.14.slot_ref, bf16[256,512]{1,0:T(8,128)(2,1)S(1)} %get-tuple-element.37.refs_0_, bf16[256,512]{1,0:T(8,128)(2,1)S(1)} %get-tuple-element.40.refs_1_, bf16[256,512]{1,0:T(8,128)(2,1)S(1)} %get-tuple-element.43.refs_2_), custom_call_target="tpu_custom_call" | custom-call | tf_op jit(solution)/shard_map/collect/pallas_call | solution.py:328
  76.6 0.1 broadcast_in_dim.3
  76.7 0.0 collective-permute-done.13.refs_0_
  76.7 0.8 collect.5.refs_1_
  77.6 1.4 %collective-permute-done.14.refs_0_ = bf16[256,512]{1,0:T(8,128)(2,1)S(1)} collective-permute-done((bf16[256,512]{1,0:T(8,128)(2,1)S(1)}, bf16[256,512]{1,0:T(8,128)(2,1)S(1)}, u32[]{:S(2)}, u32[]{:S(2)}) %collective-permute-start.14) | collective-permute-done | bytes 262176 | tf_op jit(solution)/shard_map/ppermute | solution.py:35
  78.9 0.8 collect.6.refs_1_
  79.8 2.6 %collective-permute-done.15.refs_0_ = bf16[256,512]{1,0:T(8,128)(2,1)S(1)} collective-permute-done((bf16[256,512]{1,0:T(8,128)(2,1)S(1)}, bf16[256,512]{1,0:T(8,128)(2,1)S(1)}, u32[]{:S(2)}, u32[]{:S(2)}) %collective-permute-start.15) | collective-permute-done | bytes 262176 | tf_op jit(solution)/shard_map/ppermute | solution.py:35
  82.4 0.8 collect.7
  83.2 0.1 collective-permute-start.16
  83.3 0.1 collective-permute-start.17
  83.3 3.5 %collective-permute-start.18 = (bf16[64,512]{1,0:T(8,128)(2,1)S(1)}, bf16[64,512]{1,0:T(8,128)(2,1)S(1)}, u32[]{:S(2)}, u32[]{:S(2)}) collective-permute-start(bf16[64,512]{1,0:T(8,128)(2,1)S(1)} %get-tuple-element.48), channel_id=1, source_target_pairs={{0,13},{1,0},{4,1},{5,4},{8,5},{9,8},{12,9},{13,12},{2,15},{3,2},{... | collective-permute-start | bytes 196616 | tf_op jit(solution)/shard_map/ppermute | solution.py:35
  86.9 2.0 %collective-permute-start.19 = (bf16[64,512]{1,0:T(8,128)(2,1)S(1)}, bf16[64,512]{1,0:T(8,128)(2,1)S(1)}, u32[]{:S(2)}, u32[]{:S(2)}) collective-permute-start(bf16[64,512]{1,0:T(8,128)(2,1)S(1)} %get-tuple-element.49), channel_id=1, source_target_pairs={{0,12},{1,13},{4,0},{5,1},{8,4},{9,5},{12,8},{13,9},{2,14},{3,15},... | collective-permute-start | bytes 196616 | tf_op jit(solution)/shard_map/ppermute | solution.py:35
  89.0 0.0 copy-start.7
  89.0 0.6 collective-permute-done.16.refs_0_
  89.6 0.0 collective-permute-done.17.refs_1_
  89.6 0.0 collective-permute-done.18.refs_2_
  89.6 1.5 %collective-permute-done.19.refs_3_ = bf16[64,512]{1,0:T(8,128)(2,1)S(1)} collective-permute-done((bf16[64,512]{1,0:T(8,128)(2,1)S(1)}, bf16[64,512]{1,0:T(8,128)(2,1)S(1)}, u32[]{:S(2)}, u32[]{:S(2)}) %collective-permute-start.19) | collective-permute-done | bytes 65568 | tf_op jit(solution)/shard_map/ppermute | solution.py:35
  91.1 1.2 %finish.1 = f32[256,512]{1,0:T(8,128)} custom-call(s32[1,4,64]{2,1,0:T(4,128)S(1)} %copy-done.6, f32[256,512]{1,0:T(8,128)S(1)} %get-tuple-element.45.own, bf16[64,512]{1,0:T(8,128)(2,1)S(1)} %collective-permute-done.16.refs_0_, bf16[64,512]{1,0:T(8,128)(2,1)S(1)} %collective-permute-done.17.refs_1_, bf16[64,512]{1,0:T(8,128)(2,1)S(1)} %collective-permute-done.18.refs_2_, ...), custom_call_target="tpu_custom_call" | custom-call | tf_op jit(solution)/shard_map/finish/pallas_call | solution.py:350
  (18 shorter events, 0.2 us)
Async XLA Ops:
  0.6 25.4 %copy-start.3 = (bf16[256,512]{1,0:T(8,128)(2,1)S(1)}, bf16[256,512]{1,0:T(8,128)(2,1)}, u32[]{:S(2)}) copy-start(bf16[256,512]{1,0:T(8,128)(2,1)} %refs_2_.5) | copy-start | bytes 786436
  0.6 25.4 %copy-start.6 = (s32[1,4,64]{2,1,0:T(4,128)S(1)}, s32[1,4,64]{2,1,0:T(4,128)}, u32[]{:S(2)}) copy-start(s32[1,4,64]{2,1,0:T(4,128)} %rows_ref.3) | copy-start | bytes 3076
  3.8 22.3 %collective-permute-start.1 = (bf16[400,1024]{1,0:T(8,128)(2,1)}, bf16[400,1024]{1,0:T(8,128)(2,1)S(1)}, u32[]{:S(2)}, u32[]{:S(2)}) collective-permute-start(bf16[400,1024]{1,0:T(8,128)(2,1)} %get-tuple-element.27), channel_id=1, source_target_pairs={{0,2},{2,0},{1,3},{3,1},{4,6},{6,4},{5,7},{7,5},{8,10},{10,8},{9,1... | collective-permute-start | bytes 2457608 | tf_op jit(solution)/shard_map/ppermute | solution.py:35
  6.8 34.8 %copy-start.8 = (s32[1536]{0:T(1024)S(1)}, s32[1536]{0:T(1024)}, u32[]{:S(2)}) copy-start(s32[1536]{0:T(1024)} %param.12) | copy-start | bytes 18436
  6.8 34.8 %copy-start.9 = (s32[1536]{0:T(1024)S(1)}, s32[1536]{0:T(1024)}, u32[]{:S(2)}) copy-start(s32[1536]{0:T(1024)} %param.11) | copy-start | bytes 18436
  6.8 34.8 %copy-start.1 = (bf16[1536,512]{1,0:T(8,128)(2,1)S(1)}, bf16[1536,512]{1,0:T(8,128)(2,1)}, u32[]{:S(2)}) copy-start(bf16[1536,512]{1,0:T(8,128)(2,1)} %refs_0_.3) | copy-start | bytes 4718596
  6.8 29.7 %collective-permute-start.9 = (bf16[2,128,1024]{2,1,0:T(8,128)(2,1)}, bf16[2,128,1024]{2,1,0:T(8,128)(2,1)S(1)}, u32[]{:S(2)}, u32[]{:S(2)}) collective-permute-start(bf16[2,128,1024]{2,1,0:T(8,128)(2,1)} %get-tuple-element.35), channel_id=1, source_target_pairs={{0,2},{2,0},{1,3},{3,1},{4,6},{6,4},{5,7},{7,5},{8,10},{10,8},{9,1... | collective-permute-start | bytes 1572872 | tf_op jit(solution)/shard_map/ppermute | solution.py:35
  26.6 11.7 %collective-permute-start.2 = (bf16[64,1024]{1,0:T(8,128)(2,1)S(1)}, bf16[64,1024]{1,0:T(8,128)(2,1)S(1)}, u32[]{:S(2)}, u32[]{:S(2)}) collective-permute-start(bf16[64,1024]{1,0:T(8,128)(2,1)S(1)} %get-tuple-element.30), channel_id=1, source_target_pairs={{0,12},{1,13},{4,0},{5,1},{8,4},{9,5},{12,8},{13,9},{2,14},{3,15},... | collective-permute-start | bytes 393224 | tf_op jit(solution)/shard_map/ppermute | solution.py:35
  30.8 7.5 %collective-permute-start.3 = (bf16[64,1024]{1,0:T(8,128)(2,1)S(1)}, bf16[64,1024]{1,0:T(8,128)(2,1)S(1)}, u32[]{:S(2)}, u32[]{:S(2)}) collective-permute-start(bf16[64,1024]{1,0:T(8,128)(2,1)S(1)} %get-tuple-element.31), channel_id=1, source_target_pairs={{0,13},{1,0},{4,1},{5,4},{8,5},{9,8},{12,9},{13,12},{2,15},{3,2},{... | collective-permute-start | bytes 393224 | tf_op jit(solution)/shard_map/ppermute | solution.py:35
  30.8 7.5 %collective-permute-start.4 = (bf16[64,1024]{1,0:T(8,128)(2,1)S(1)}, bf16[64,1024]{1,0:T(8,128)(2,1)S(1)}, u32[]{:S(2)}, u32[]{:S(2)}) collective-permute-start(bf16[64,1024]{1,0:T(8,128)(2,1)S(1)} %get-tuple-element.32), channel_id=1, source_target_pairs={{0,1},{1,4},{4,5},{5,8},{8,9},{9,12},{12,13},{13,0},{2,3},{3,6},{6... | collective-permute-start | bytes 393224 | tf_op jit(solution)/shard_map/ppermute | solution.py:35
  31.3 8.7 %collective-permute-start.5 = (bf16[64,1024]{1,0:T(8,128)(2,1)S(1)}, bf16[64,1024]{1,0:T(8,128)(2,1)S(1)}, u32[]{:S(2)}, u32[]{:S(2)}) collective-permute-start(bf16[64,1024]{1,0:T(8,128)(2,1)S(1)} %get-tuple-element.33), channel_id=1, source_target_pairs={{0,4},{1,5},{4,8},{5,9},{8,12},{9,13},{12,0},{13,1},{2,6},{3,7},{6... | collective-permute-start | bytes 393224 | tf_op jit(solution)/shard_map/ppermute | solution.py:35
  36.5 14.6 %collective-permute-start.6 = (bf16[2,128,1024]{2,1,0:T(8,128)(2,1)S(1)}, bf16[2,128,1024]{2,1,0:T(8,128)(2,1)S(1)}, u32[]{:S(2)}, u32[]{:S(2)}) collective-permute-start(bf16[2,128,1024]{2,1,0:T(8,128)(2,1)S(1)} %get-tuple-element.34.refs_0_), channel_id=1, source_target_pairs={{0,4},{4,0},{8,12},{12,8},{1,5},{5,1},{9,13},{13,9},{2,6},{6,2},{1... | collective-permute-start | bytes 1572872 | tf_op jit(solution)/shard_map/ppermute | solution.py:40
  40.1 13.5 %collective-permute-start.10 = (bf16[2,128,1024]{2,1,0:T(8,128)(2,1)S(1)}, bf16[2,128,1024]{2,1,0:T(8,128)(2,1)S(1)}, u32[]{:S(2)}, u32[]{:S(2)}) collective-permute-start(bf16[2,128,1024]{2,1,0:T(8,128)(2,1)S(1)} %collective-permute-done.9.refs_0_), channel_id=1, source_target_pairs={{0,16},{16,0},{1,17},{17,1},{2,18},{18,2},{3,19},{19,3},{4,20},{20... | collective-permute-start | bytes 1572872 | tf_op jit(solution)/shard_map/ppermute | solution.py:40
  41.7 18.9 %collective-permute-start = (bf16[768,512]{1,0:T(8,128)(2,1)S(1)}, bf16[768,512]{1,0:T(8,128)(2,1)S(1)}, u32[]{:S(2)}, u32[]{:S(2)}) collective-permute-start(bf16[768,512]{1,0:T(8,128)(2,1)S(1)} %prepare_blocks.1), channel_id=1, source_target_pairs={{0,2},{2,0},{1,3},{3,1},{4,6},{6,4},{5,7},{7,5},{8,10},{10,8},{9,1... | collective-permute-start | bytes 2359304 | tf_op jit(solution)/shard_map/ppermute | solution.py:35
  43.3 10.3 %collective-permute-start.7 = (bf16[2,128,1024]{2,1,0:T(8,128)(2,1)S(1)}, bf16[2,128,1024]{2,1,0:T(8,128)(2,1)S(1)}, u32[]{:S(2)}, u32[]{:S(2)}) collective-permute-start(bf16[2,128,1024]{2,1,0:T(8,128)(2,1)S(1)} %get-tuple-element.34.refs_0_), channel_id=1, source_target_pairs={{0,1},{1,0},{2,3},{3,2},{4,5},{5,4},{6,7},{7,6},{8,9},{9,8},{10,11... | collective-permute-start | bytes 1572872 | tf_op jit(solution)/shard_map/ppermute | solution.py:40
  51.1 2.5 %collective-permute-start.8 = (bf16[2,128,1024]{2,1,0:T(8,128)(2,1)S(1)}, bf16[2,128,1024]{2,1,0:T(8,128)(2,1)S(1)}, u32[]{:S(2)}, u32[]{:S(2)}) collective-permute-start(bf16[2,128,1024]{2,1,0:T(8,128)(2,1)S(1)} %collective-permute-done.6.refs_1_), channel_id=1, source_target_pairs={{0,1},{1,0},{2,3},{3,2},{4,5},{5,4},{6,7},{7,6},{8,9},{9,8},{10,11... | collective-permute-start | bytes 1572872 | tf_op jit(solution)/shard_map/ppermute | solution.py:40
  51.1 2.7 %collective-permute-start.11 = (bf16[2,128,1024]{2,1,0:T(8,128)(2,1)S(1)}, bf16[2,128,1024]{2,1,0:T(8,128)(2,1)S(1)}, u32[]{:S(2)}, u32[]{:S(2)}) collective-permute-start(bf16[2,128,1024]{2,1,0:T(8,128)(2,1)S(1)} %collective-permute-done.9.refs_0_), channel_id=1, source_target_pairs={{0,1},{1,0},{2,3},{3,2},{4,5},{5,4},{6,7},{7,6},{8,9},{9,8},{10,11... | collective-permute-start | bytes 1572872 | tf_op jit(solution)/shard_map/ppermute | solution.py:40
  53.6 1.9 %collective-permute-start.12 = (bf16[2,128,1024]{2,1,0:T(8,128)(2,1)S(1)}, bf16[2,128,1024]{2,1,0:T(8,128)(2,1)S(1)}, u32[]{:S(2)}, u32[]{:S(2)}) collective-permute-start(bf16[2,128,1024]{2,1,0:T(8,128)(2,1)S(1)} %collective-permute-done.10.refs_1_), channel_id=1, source_target_pairs={{0,1},{1,0},{2,3},{3,2},{4,5},{5,4},{6,7},{7,6},{8,9},{9,8},{10,11... | collective-permute-start | bytes 1572872 | tf_op jit(solution)/shard_map/ppermute | solution.py:40
  53.8 6.9 %copy-start = (bf16[3,512,1024]{2,1,0:T(8,128)(2,1)S(1)}, bf16[3,512,1024]{2,1,0:T(8,128)(2,1)}, u32[]{:S(2)}) copy-start(bf16[3,512,1024]{2,1,0:T(8,128)(2,1)} %refs_10_.5) | copy-start | bytes 9437188
  53.8 6.9 %copy-start.2 = (bf16[1024,512]{1,0:T(8,128)(2,1)S(1)}, bf16[1024,512]{1,0:T(8,128)(2,1)}, u32[]{:S(2)}) copy-start(bf16[1024,512]{1,0:T(8,128)(2,1)} %refs_11_.5) | copy-start | bytes 3145732
  53.8 6.9 %copy-start.4 = (f32[512]{0:T(512)S(1)}, f32[512]{0:T(512)}, u32[]{:S(2)}) copy-start(f32[512]{0:T(512)} %param.17) | copy-start | bytes 6148
  53.8 6.8 %copy-start.5 = (s32[8]{0:T(128)S(1)}, s32[8]{0:T(128)}, u32[]{:S(2)}) copy-start(s32[8]{0:T(128)} %counts.13) | copy-start | bytes 100
  64.4 12.4 %collective-permute-start.13 = (bf16[256,512]{1,0:T(8,128)(2,1)S(1)}, bf16[256,512]{1,0:T(8,128)(2,1)S(1)}, u32[]{:S(2)}, u32[]{:S(2)}) collective-permute-start(bf16[256,512]{1,0:T(8,128)(2,1)S(1)} %get-tuple-element.38), channel_id=1, source_target_pairs={{0,2},{2,0},{1,3},{3,1},{4,6},{6,4},{5,7},{7,5},{8,10},{10,8},{9,1... | collective-permute-start | bytes 786440 | tf_op jit(solution)/shard_map/ppermute | solution.py:35
  69.6 9.3 %collective-permute-start.14 = (bf16[256,512]{1,0:T(8,128)(2,1)S(1)}, bf16[256,512]{1,0:T(8,128)(2,1)S(1)}, u32[]{:S(2)}, u32[]{:S(2)}) collective-permute-start(bf16[256,512]{1,0:T(8,128)(2,1)S(1)} %get-tuple-element.41), channel_id=1, source_target_pairs={{0,2},{2,0},{1,3},{3,1},{4,6},{6,4},{5,7},{7,5},{8,10},{10,8},{9,1... | collective-permute-start | bytes 786440 | tf_op jit(solution)/shard_map/ppermute | solution.py:35
  73.9 8.5 %collective-permute-start.15 = (bf16[256,512]{1,0:T(8,128)(2,1)S(1)}, bf16[256,512]{1,0:T(8,128)(2,1)S(1)}, u32[]{:S(2)}, u32[]{:S(2)}) collective-permute-start(bf16[256,512]{1,0:T(8,128)(2,1)S(1)} %get-tuple-element.44), channel_id=1, source_target_pairs={{0,2},{2,0},{1,3},{3,1},{4,6},{6,4},{5,7},{7,5},{8,10},{10,8},{9,1... | collective-permute-start | bytes 786440 | tf_op jit(solution)/shard_map/ppermute | solution.py:35
  83.2 6.4 %collective-permute-start.16 = (bf16[64,512]{1,0:T(8,128)(2,1)S(1)}, bf16[64,512]{1,0:T(8,128)(2,1)S(1)}, u32[]{:S(2)}, u32[]{:S(2)}) collective-permute-start(bf16[64,512]{1,0:T(8,128)(2,1)S(1)} %get-tuple-element.46), channel_id=1, source_target_pairs={{0,4},{1,5},{4,8},{5,9},{8,12},{9,13},{12,0},{13,1},{2,6},{3,7},{6... | collective-permute-start | bytes 196616 | tf_op jit(solution)/shard_map/ppermute | solution.py:35
  83.3 6.4 %collective-permute-start.17 = (bf16[64,512]{1,0:T(8,128)(2,1)S(1)}, bf16[64,512]{1,0:T(8,128)(2,1)S(1)}, u32[]{:S(2)}, u32[]{:S(2)}) collective-permute-start(bf16[64,512]{1,0:T(8,128)(2,1)S(1)} %get-tuple-element.47), channel_id=1, source_target_pairs={{0,1},{1,4},{4,5},{5,8},{8,9},{9,12},{12,13},{13,0},{2,3},{3,6},{6... | collective-permute-start | bytes 196616 | tf_op jit(solution)/shard_map/ppermute | solution.py:35
  83.3 6.3 %collective-permute-start.18 = (bf16[64,512]{1,0:T(8,128)(2,1)S(1)}, bf16[64,512]{1,0:T(8,128)(2,1)S(1)}, u32[]{:S(2)}, u32[]{:S(2)}) collective-permute-start(bf16[64,512]{1,0:T(8,128)(2,1)S(1)} %get-tuple-element.48), channel_id=1, source_target_pairs={{0,13},{1,0},{4,1},{5,4},{8,5},{9,8},{12,9},{13,12},{2,15},{3,2},{... | collective-permute-start | bytes 196616 | tf_op jit(solution)/shard_map/ppermute | solution.py:35
  86.9 4.3 %collective-permute-start.19 = (bf16[64,512]{1,0:T(8,128)(2,1)S(1)}, bf16[64,512]{1,0:T(8,128)(2,1)S(1)}, u32[]{:S(2)}, u32[]{:S(2)}) collective-permute-start(bf16[64,512]{1,0:T(8,128)(2,1)S(1)} %get-tuple-element.49), channel_id=1, source_target_pairs={{0,12},{1,13},{4,0},{5,1},{8,4},{9,5},{12,8},{13,9},{2,14},{3,15},... | collective-permute-start | bytes 196616 | tf_op jit(solution)/shard_map/ppermute | solution.py:35
  89.0 3.4 %copy-start.7 = (bf16[1536,512]{1,0:T(8,128)(2,1)}, bf16[1536,512]{1,0:T(8,128)(2,1)S(1)}, u32[]{:S(2)}) copy-start(bf16[1536,512]{1,0:T(8,128)(2,1)S(1)} %constant_dynamic-update-slice_fusion) | copy-start | bytes 4718596

commit v3 on v2

--- a/solution.py
+++ b/solution.py
@@ -10,7 +10,7 @@
 TILE = 128
 RADIUS = 2
 GAIN_ROWS = 16
-SHARERS_A = ("dom", "rep")
+SHARERS_A = ("groups", "dom", "rep")
 SHARERS_B = ("groups", "rep")
 bf16 = jnp.bfloat16
 f32 = jnp.float32
@@ -80,21 +80,14 @@
     return copy, finish
 
 
-def share_kernel(ways, axes_a, axes_b, w_in, w_out, nodes, gain, first, second, sems):
+def first_kernel(axes, w_in, nodes, gain, packed, first, sems):
     copy, finish = copier(sems)
-    width = w_out.shape[1]
-    rows_a, rows_b = width >> len(axes_a), width >> len(axes_b)
-    start_a = pl.multiple_of(share_index(axes_a) * rows_a, rows_a)
-    start_b = pl.multiple_of(share_index(axes_b) * rows_b, rows_b)
+    count, width = nodes.shape
+    rows = width >> len(axes)
+    start = pl.multiple_of(share_index(axes) * rows, rows)
     for part in range(2):
-        copy(w_in.at[part, pl.ds(start_a, rows_a), :], first.at[pl.ds(part * rows_a, rows_a), :])
-    copy(w_in.at[2, pl.ds(start_b, rows_b), :], second.at[0])
-    for h in range(ways):
-        copy(w_out.at[pl.ds(h * width + start_b, rows_b), :], second.at[1, :, pl.ds(h * width, width)])
-    base = 2 * rows_a
-    count = nodes.shape[0] // ways
-    for h in range(ways):
-        copy(nodes.at[pl.ds(h * count, count), :], first.at[pl.ds(base, count), pl.ds(h * width, width)])
+        copy(w_in.at[part, pl.ds(start, rows), :], first.at[part])
+    copy(nodes, packed.at[pl.ds(0, count), :])
     high = gain[...].astype(bf16)
     middle = (gain[...] - high.astype(f32)).astype(bf16)
     low = (gain[...] - high.astype(f32) - middle.astype(f32)).astype(bf16)
@@ -102,22 +95,45 @@
     rows = jnp.where(row_ids == 0, high.astype(f32), 0.0)
     rows = jnp.where(row_ids == 1, middle.astype(f32), rows)
     rows = jnp.where(row_ids == 2, low.astype(f32), rows)
-    first[base + count :, :] = jnp.concatenate([rows.astype(bf16)] * ways, axis=1)
+    packed[count:, :] = rows.astype(bf16)
     finish()
 
 
-def prepare_shares(weight_in, weight_out, nodes, gain, ways, axes_a, axes_b):
+def prepare_first(weight_in, nodes, gain, ways, axes):
+    count, width = nodes.shape
+    return pl.pallas_call(
+        functools.partial(first_kernel, axes),
+        out_shape=[shape(count + GAIN_ROWS, width), shape(2, width >> len(axes), ways * width)],
+        in_specs=[HBM, HBM, VMEM],
+        out_specs=[VMEM] * 2,
+        scratch_shapes=[pltpu.SemaphoreType.DMA((3,))],
+        compiler_params=params(PREPARE_VMEM_BYTES),
+        name="prepare_first",
+    )(weight_in, nodes, gain)
+
+
+def second_kernel(ways, axes, w_in, w_out, second, sems):
+    copy, finish = copier(sems)
+    width = w_out.shape[1]
+    rows = width >> len(axes)
+    start = pl.multiple_of(share_index(axes) * rows, rows)
+    copy(w_in.at[2, pl.ds(start, rows), :], second.at[0])
+    for h in range(ways):
+        copy(w_out.at[pl.ds(h * width + start, rows), :], second.at[1, :, pl.ds(h * width, width)])
+    finish()
+
+
+def prepare_second(weight_in, weight_out, ways, axes):
     width = weight_out.shape[1]
-    rows = 2 * (width >> len(axes_a)) + nodes.shape[0] // ways + GAIN_ROWS
-    return pl.pallas_call(
-        functools.partial(share_kernel, ways, axes_a, axes_b),
-        out_shape=[shape(rows, ways * width), shape(2, width >> len(axes_b), ways * width)],
-        in_specs=[HBM, HBM, HBM, VMEM],
-        out_specs=[VMEM] * 2,
-        scratch_shapes=[pltpu.SemaphoreType.DMA((3 + 2 * ways,))],
+    return pl.pallas_call(
+        functools.partial(second_kernel, ways, axes),
+        out_shape=shape(2, width >> len(axes), ways * width),
+        in_specs=[HBM, HBM],
+        out_specs=VMEM,
+        scratch_shapes=[pltpu.SemaphoreType.DMA((1 + ways,))],
         compiler_params=params(PREPARE_VMEM_BYTES),
-        name="prepare_shares",
-    )(weight_in, weight_out, nodes, gain)
+        name="prepare_second",
+    )(weight_in, weight_out)
 
 
 def block_kernel(ways, edges, *rest):
@@ -147,18 +163,13 @@
 def unpack_kernel(ways, halo_count, rows_ref, nodes, *refs):
     messages, outs = refs[: ways - 1], list(refs[ways - 1 :])
     halos = [outs.pop(0) for _ in range(halo_count)]
-    pieces, others, gains = (outs[i :: 3] for i in range(3))
+    others, gains = outs[::2], outs[1::2]
     count, width = nodes.shape
     for d in range(1, ways):
-        message, piece, other, gain = messages[d - 1], pieces[d - 1], others[d - 1], gains[d - 1]
-        rows = piece.shape[1]
-        for part in range(2):
-            piece[part] = message[part * rows : (part + 1) * rows, :]
-        base, packed = 2 * rows, count // ways
-        for h in range(ways):
-            other[h * packed : (h + 1) * packed, :] = message[base : base + packed, h * width : (h + 1) * width]
-        parts = message[base + packed :, :width].astype(f32)
-        gain[...] = parts[0:1, :] + parts[1:2, :] + parts[2:3, :]
+        message = messages[d - 1]
+        others[d - 1][...] = message[:count, :]
+        parts = message[count:, :].astype(f32)
+        gains[d - 1][...] = parts[0:1, :] + parts[1:2, :] + parts[2:3, :]
     for j in range(halo_count):
         hits = onehot(column(rows_ref[0, j : j + 1, :]), count)
         for d in range(ways):
@@ -166,10 +177,10 @@
             halos[j][:, d * width : (d + 1) * width] = dot(hits, table).astype(bf16)
 
 
-def unpack(halo_rows, nodes, messages, ways, axes_a):
+def unpack(halo_rows, nodes, messages, ways):
     _, offsets, size = halo_rows.shape
     count, width = nodes.shape
-    each = [shape(2, width >> len(axes_a), ways * width), shape(count, width), shape(1, width, dtype=f32)]
+    each = [shape(count, width), shape(1, width, dtype=f32)]
     outs = pl.pallas_call(
         functools.partial(unpack_kernel, ways, offsets),
         out_shape=[shape(size, ways * width)] * offsets + each * (ways - 1),
@@ -177,12 +188,30 @@
         cost_estimate=pl.CostEstimate(flops=6000000 * 1000, bytes_accessed=4 * 1024 * 1024, transcendentals=0),
         name="unpack",
     )(halo_rows, nodes, *messages)
-    return (outs[:offsets], *(outs[offsets + i :: 3] for i in range(3)))
-
-
-def gather_shares(piece, axes):
+    return outs[:offsets], outs[offsets::2], outs[offsets + 1 :: 2]
+
+
+def join_kernel(first, second, out):
+    rows = first.shape[1]
+    out[:, :rows, :] = first[...]
+    out[:, rows:, :] = second[...]
+
+
+def join(first, second):
+    parts, rows, channels = first.shape
+    return pl.pallas_call(
+        join_kernel,
+        out_shape=shape(parts, 2 * rows, channels),
+        compiler_params=params(),
+        name="join",
+    )(first, second)
+
+
+def gather_shares(piece, axes, waits):
     pieces = [piece]
     for axis in axes:
+        if axis == "rep":
+            pieces[-1] = tie(pieces[-1], *waits)
         pieces = pieces + [swapped(p, axis) for p in pieces]
     return pieces
 
@@ -190,11 +219,13 @@
 def assemble_kernel(axes, *refs):
     pieces, out = refs[:-1], refs[-1]
     share = share_index(axes)
-    rows = pieces[0].shape[1]
-    for m, piece in enumerate(pieces):
+    each = (1 << len(axes)) // len(pieces)
+    rows = pieces[0].shape[1] // each
+    for m in range(len(pieces) * each):
         start = pl.multiple_of((share ^ m) * rows, rows)
+        place = m % each * rows
         for part in range(out.shape[0]):
-            out[part, pl.ds(start, rows), :] = piece[part]
+            out[part, pl.ds(start, rows), :] = pieces[m // each][part, place : place + rows, :]
 
 
 def assemble(pieces, axes):
@@ -379,18 +410,23 @@
 
     gain = norm_gain.reshape(1, width)
     sender_row, slot_row = senders.reshape(1, -1), receiver_slot.reshape(1, -1)
-    message_a, message_b = prepare_shares(weight_in, weight_out, node_feats, gain, ways, axes_a, axes_b)
+    packed, message_a = prepare_first(weight_in, node_feats, gain, ways, axes_a)
+    message_b = prepare_second(weight_in, weight_out, ways, axes_b)
     blocks = prepare_blocks(edge_feats, ways)
     blocks = [tie(block, sender_row, slot_row) for block in blocks]
+    received = [shifted(packed, "chan", d) for d in distances]
     crossed_a = [shifted(message_a, "chan", d) for d in distances]
     crossed_b = [shifted(message_b, "chan", d) for d in distances]
-    outgoing, pieces, nodes, gains = unpack(halo_rows, node_feats, crossed_a, ways, axes_a)
+    outgoing, nodes, gains = unpack(halo_rows, node_feats, received, ways)
     nodes, gains = [node_feats, *nodes], [gain, *gains]
     halos = [shifted(rows, ("dom", "rep"), by) for rows, by in zip(outgoing, offsets)]
     edges = [edge_feats] + [shifted(blocks[d - 1], "chan", d) for d in distances]
-    crossed_b = [tie(piece, *halos) for piece in crossed_b]
-    others_a = [assemble(gather_shares(piece, axes_a), axes_a) for piece in pieces]
-    others_b = [assemble(gather_shares(piece, axes_b), axes_b) for piece in crossed_b]
+    pieces = [tie(piece, *halos[:3]) for piece in crossed_a]
+    pieces = [join(piece, swapped(piece, axes_a[0])) for piece in pieces]
+    pieces = [tie(piece, *halos[3:]) for piece in pieces]
+    crossed_b = [tie(piece, *pieces) for piece in crossed_b]
+    others_a = [assemble(gather_shares(piece, axes_a[1:], edges[1:]), axes_a) for piece in pieces]
+    others_b = [assemble(gather_shares(piece, axes_b, ()), axes_b) for piece in crossed_b]
 
     def collected(places, parts, sums, last=False):
         return collect(places, parts, sums, tile_counts, slot_row, ways, local_nodes, halo_size, last)

time: 92.5 us -> 85.2 us (0.921)
  waiting for transfers between devices: 48.6 us -> 38.6 us
  local copies, waits for them, and re-layouts: 0.31 us -> 1.73 us
  Pallas kernels: 19.9 us -> 21.3 us
    ppermute x14 -> x15, waiting for transfers between devices: 37.1 us -> 23 us  [shifted(): lax.ppermute(block, axis, [(i, (i + distance) % size) for i in range(size)])]
    ppermute x6 -> x7, waiting for transfers between devices: 11.5 us -> 15.7 us  [swapped(): return lax.ppermute(block, axis, [(i, i ^ 1) for i in range(size)])]
    unnamed x20, local copies, waits for them, and re-layouts: 0.05 us -> 1.47 us
    pallas_call x1 -> x3, Pallas kernels: 3.12 us -> 4.49 us  [the longest x1 2.6 us: prepare_first(): pl.pallas_call(functools.partial(first_kernel, axes), out_shape=[shape(co...]
    ppermute x6 -> x7, starting transfers between devices: 3.86 us -> 2.72 us  [swapped(): return lax.ppermute(block, axis, [(i, i ^ 1) for i in range(size)])]
    ppermute x14 -> x15, starting transfers between devices: 18.7 us -> 19.8 us  [shifted(): lax.ppermute(block, axis, [(i, (i + distance) % size) for i in range(size)])]
  transfers between devices with their start and end apart: 20 -> 22, of which waited for: 11 -> 16; matrix products, arithmetic and copies ran while one was open for 0% -> 0% of each run, Pallas kernels for 12% -> 15%
where the time goes in v3:
time: 85.2 us; the launch traced here: 85 us
  waiting for transfers between devices  38.6 us (45%)
  starting transfers between devices  22.5 us (26%)
  Pallas kernels  21.3 us (25%)
  local copies, waits for them, and re-layouts  1.73 us (2%)
  between operations  0.9 us (1%)
    ppermute x15, waiting for transfers between devices, shifted(): lax.ppermute(block, axis, [(i, (i + distance) % size) for i in range(size)])  23 us
    ppermute x15, starting transfers between devices, shifted(): lax.ppermute(block, axis, [(i, (i + distance) % size) for i in range(size)])  19.8 us
    ppermute x7, waiting for transfers between devices, swapped(): return lax.ppermute(block, axis, [(i, i ^ 1) for i in range(size)])  15.7 us
    pallas_call x3, Pallas kernels, edge_update(): pl.pallas_call(functools.partial(edge_kernel, ways, before, mine), out_sh...  11 us
    pallas_call x4, Pallas kernels, collect(): pl.pallas_call(functools.partial(collect_kernel, ways, places, local_node...  3.63 us
    ppermute x7, starting transfers between devices, swapped(): return lax.ppermute(block, axis, [(i, i ^ 1) for i in range(size)])  2.72 us
    pallas_call x1, Pallas kernels, prepare_first(): pl.pallas_call(functools.partial(first_kernel, axes), out_shape=[shape(co...  2.6 us
    pallas_call x1, Pallas kernels, prepare_second(): pl.pallas_call(functools.partial(second_kernel, ways, axes), out_shape=sh...  1.86 us
  transfers between devices with their start and end apart: 22, of which 16 were waited for; matrix products, arithmetic and copies ran while one was open for 0% of the time, Pallas kernels for 15%

profile of v3, /device:TPU:0, one launch (start us, length us, event | category | flops | bytes accessed | tf_op | source)
XLA Modules:
  0.0 85.0 jit_solution(10925897473655639727)
XLA Ops:
  0.6 2.6 %prepare_first.1 = (bf16[272,512]{1,0:T(8,128)(2,1)}, bf16[2,64,1024]{2,1,0:T(8,128)(2,1)}) custom-call(bf16[3,512,1024]{2,1,0:T(8,128)(2,1)} %refs_10_.5, bf16[256,512]{1,0:T(8,128)(2,1)} %refs_2_.5, f32[1,512]{1,0:T(1,128)} %bitcast.1), custom_call_target="tpu_custom_call" | custom-call | tf_op jit(solution)/shard_map/prepare_first/pallas_call | solution.py:104
  3.2 3.0 %collective-permute-start.1 = (bf16[272,512]{1,0:T(8,128)(2,1)}, bf16[272,512]{1,0:T(8,128)(2,1)S(1)}, u32[]{:S(2)}, u32[]{:S(2)}) collective-permute-start(bf16[272,512]{1,0:T(8,128)(2,1)} %get-tuple-element.29), channel_id=1, source_target_pairs={{0,2},{2,0},{1,3},{3,1},{4,6},{6,4},{5,7},{7,5},{8,10},{10,8},{9,1... | collective-permute-start | bytes 835592 | tf_op jit(solution)/shard_map/ppermute | solution.py:35
  6.2 0.1 collective-permute-start.6
  6.3 1.9 %prepare_second.1 = bf16[2,128,1024]{2,1,0:T(8,128)(2,1)} custom-call(bf16[3,512,1024]{2,1,0:T(8,128)(2,1)} %refs_10_.5, bf16[1024,512]{1,0:T(8,128)(2,1)} %refs_11_.5), custom_call_target="tpu_custom_call" | custom-call | tf_op jit(solution)/shard_map/prepare_second/pallas_call | solution.py:128
  8.2 0.0 copy-start.8
  8.2 0.0 copy-start.9
  8.2 0.0 copy-start.1
  8.2 2.0 %collective-permute-start.11 = (bf16[2,128,1024]{2,1,0:T(8,128)(2,1)}, bf16[2,128,1024]{2,1,0:T(8,128)(2,1)S(1)}, u32[]{:S(2)}, u32[]{:S(2)}) collective-permute-start(bf16[2,128,1024]{2,1,0:T(8,128)(2,1)} %prepare_second.1), channel_id=1, source_target_pairs={{0,2},{2,0},{1,3},{3,1},{4,6},{6,4},{5,7},{7,5},{8,10},{10,8},{9,1... | collective-permute-start | bytes 1572872 | tf_op jit(solution)/shard_map/ppermute | solution.py:35
  10.2 3.7 %collective-permute-done.1.refs_0_ = bf16[272,512]{1,0:T(8,128)(2,1)S(1)} collective-permute-done((bf16[272,512]{1,0:T(8,128)(2,1)}, bf16[272,512]{1,0:T(8,128)(2,1)S(1)}, u32[]{:S(2)}, u32[]{:S(2)}) %collective-permute-start.1) | collective-permute-done | bytes 278560 | tf_op jit(solution)/shard_map/ppermute | solution.py:35
  13.9 0.5 unpack.1
  14.5 4.2 %collective-permute-start.2 = (bf16[64,1024]{1,0:T(8,128)(2,1)S(1)}, bf16[64,1024]{1,0:T(8,128)(2,1)S(1)}, u32[]{:S(2)}, u32[]{:S(2)}) collective-permute-start(bf16[64,1024]{1,0:T(8,128)(2,1)S(1)} %get-tuple-element.32), channel_id=1, source_target_pairs={{0,12},{1,13},{4,0},{5,1},{8,4},{9,5},{12,8},{13,9},{2,14},{3,15},... | collective-permute-start | bytes 393224 | tf_op jit(solution)/shard_map/ppermute | solution.py:35
  18.7 0.5 collective-permute-start.4
  19.2 0.3 collective-permute-done.6.first
  19.5 2.9 %collective-permute-done.2.refs_6_ = bf16[64,1024]{1,0:T(8,128)(2,1)S(1)} collective-permute-done((bf16[64,1024]{1,0:T(8,128)(2,1)S(1)}, bf16[64,1024]{1,0:T(8,128)(2,1)S(1)}, u32[]{:S(2)}, u32[]{:S(2)}) %collective-permute-start.2) | collective-permute-done | bytes 131104 | tf_op jit(solution)/shard_map/ppermute | solution.py:35
  22.4 1.4 %collective-permute-done.3.refs_7_ = bf16[64,1024]{1,0:T(8,128)(2,1)S(1)} collective-permute-done((bf16[64,1024]{1,0:T(8,128)(2,1)S(1)}, bf16[64,1024]{1,0:T(8,128)(2,1)S(1)}, u32[]{:S(2)}, u32[]{:S(2)}) %collective-permute-start.3) | collective-permute-done | bytes 131104 | tf_op jit(solution)/shard_map/ppermute | solution.py:35
  23.8 1.1 %collective-permute-done.4.refs_8_ = bf16[64,1024]{1,0:T(8,128)(2,1)S(1)} collective-permute-done((bf16[64,1024]{1,0:T(8,128)(2,1)S(1)}, bf16[64,1024]{1,0:T(8,128)(2,1)S(1)}, u32[]{:S(2)}, u32[]{:S(2)}) %collective-permute-start.4) | collective-permute-done | bytes 131104 | tf_op jit(solution)/shard_map/ppermute | solution.py:35
  24.9 1.5 %collective-permute-start.7 = (bf16[2,64,1024]{2,1,0:T(8,128)(2,1)S(1)}, bf16[2,64,1024]{2,1,0:T(8,128)(2,1)S(1)}, u32[]{:S(2)}, u32[]{:S(2)}) collective-permute-start(bf16[2,64,1024]{2,1,0:T(8,128)(2,1)S(1)} %collective-permute-done.6.first), channel_id=1, source_target_pairs={{0,16},{16,0},{1,17},{17,1},{2,18},{18,2},{3,19},{19,3},{4,20},{20... | collective-permute-start | bytes 786440 | tf_op jit(solution)/shard_map/ppermute | solution.py:40
  26.5 0.1 prepare_blocks.1
  26.5 1.6 %collective-permute-start = (bf16[768,512]{1,0:T(8,128)(2,1)S(1)}, bf16[768,512]{1,0:T(8,128)(2,1)S(1)}, u32[]{:S(2)}, u32[]{:S(2)}) collective-permute-start(bf16[768,512]{1,0:T(8,128)(2,1)S(1)} %prepare_blocks.1), channel_id=1, source_target_pairs={{0,2},{2,0},{1,3},{3,1},{4,6},{6,4},{5,7},{7,5},{8,10},{10,8},{9,1... | collective-permute-start | bytes 2359304 | tf_op jit(solution)/shard_map/ppermute | solution.py:35
  28.1 0.0 collective-permute-start.5
  28.1 3.2 %collective-permute-done.7.second = bf16[2,64,1024]{2,1,0:T(8,128)(2,1)S(1)} collective-permute-done((bf16[2,64,1024]{2,1,0:T(8,128)(2,1)S(1)}, bf16[2,64,1024]{2,1,0:T(8,128)(2,1)S(1)}, u32[]{:S(2)}, u32[]{:S(2)}) %collective-permute-start.7) | collective-permute-done | bytes 262176 | tf_op jit(solution)/shard_map/ppermute | solution.py:40
  31.3 3.6 %collective-permute-done.5.refs_9_ = bf16[64,1024]{1,0:T(8,128)(2,1)S(1)} collective-permute-done((bf16[64,1024]{1,0:T(8,128)(2,1)S(1)}, bf16[64,1024]{1,0:T(8,128)(2,1)S(1)}, u32[]{:S(2)}, u32[]{:S(2)}) %collective-permute-start.5) | collective-permute-done | bytes 131104 | tf_op jit(solution)/shard_map/ppermute | solution.py:35
  34.9 0.0 collective-permute-done.11.refs_0_
  34.9 0.5 collective-permute-start.12
  35.4 0.0 collective-permute-start.8
  35.4 0.0 collective-permute-start.13
  35.4 0.5 collective-permute-start.9
  35.9 10.6 %collective-permute-done.12.refs_1_ = bf16[2,128,1024]{2,1,0:T(8,128)(2,1)S(1)} collective-permute-done((bf16[2,128,1024]{2,1,0:T(8,128)(2,1)S(1)}, bf16[2,128,1024]{2,1,0:T(8,128)(2,1)S(1)}, u32[]{:S(2)}, u32[]{:S(2)}) %collective-permute-start.12) | collective-permute-done | bytes 524320 | tf_op jit(solution)/shard_map/ppermute | solution.py:40
  46.5 0.3 collective-permute-done.refs_1_
  46.8 0.0 collective-permute-done.8.refs_1_
  46.8 0.2 collective-permute-start.10
  47.0 0.0 collective-permute-done.13.refs_2_
  47.0 1.4 %collective-permute-done.14.refs_3_ = bf16[2,128,1024]{2,1,0:T(8,128)(2,1)S(1)} collective-permute-done((bf16[2,128,1024]{2,1,0:T(8,128)(2,1)S(1)}, bf16[2,128,1024]{2,1,0:T(8,128)(2,1)S(1)}, u32[]{:S(2)}, u32[]{:S(2)}) %collective-permute-start.14) | collective-permute-done | bytes 524320 | tf_op jit(solution)/shard_map/ppermute | solution.py:40
  48.4 0.2 assemble.3.refs_13_
  48.5 0.0 copy-start
  48.6 0.0 copy-start.2
  48.6 0.0 copy-start.4
  48.6 0.0 copy-start.5
  48.6 0.0 collective-permute-done.9.refs_2_
  48.6 0.5 collective-permute-done.10.refs_3_
  49.1 0.2 assemble.2.refs_12_
  49.3 1.1 %copy-done = bf16[3,512,1024]{2,1,0:T(8,128)(2,1)S(1)} copy-done((bf16[3,512,1024]{2,1,0:T(8,128)(2,1)S(1)}, bf16[3,512,1024]{2,1,0:T(8,128)(2,1)}, u32[]{:S(2)}) %copy-start) | copy-done | bytes 3145752
  50.4 0.3 copy-done.2
  50.7 3.7 %edge_update_0.1 = (bf16[256,512]{1,0:T(8,128)(2,1)S(1)}, bf16[256,512]{1,0:T(8,128)(2,1)S(1)}) custom-call(s32[8]{0:T(128)S(1)} %copy-done.5, s32[1,1536]{1,0:T(1,128)S(1)} %reshape.13.sender_ref, s32[1,1536]{1,0:T(1,128)S(1)} %reshape.14.slot_ref, bf16[1536,512]{1,0:T(8,128)(2,1)S(1)} %copy-done.1, bf16[768,512]{1,0:T(8,128)(2,1)S(1)} %collective-permute-done.refs_1_, ...), custom_call_target="tpu_custom_call" | custom-call | flops 2550136832 | bytes 8388608 | tf_op jit(solution)/shard_map/edge_update_0/pallas_call | solution.py:306
  54.4 0.6 collective-permute-start.15
  55.0 3.7 %edge_update_1.1 = (bf16[256,512]{1,0:T(8,128)(2,1)S(1)}, bf16[256,512]{1,0:T(8,128)(2,1)S(1)}) custom-call(s32[8]{0:T(128)S(1)} %copy-done.5, s32[1,1536]{1,0:T(1,128)S(1)} %reshape.13.sender_ref, s32[1,1536]{1,0:T(1,128)S(1)} %reshape.14.slot_ref, bf16[1536,512]{1,0:T(8,128)(2,1)S(1)} %copy-done.1, bf16[768,512]{1,0:T(8,128)(2,1)S(1)} %collective-permute-done.refs_1_, ...), custom_call_target="tpu_custom_call" | custom-call | flops 2550136832 | bytes 8388608 | tf_op jit(solution)/shard_map/edge_update_1/pallas_call | solution.py:306
  58.7 1.6 %collective-permute-start.16 = (bf16[256,512]{1,0:T(8,128)(2,1)S(1)}, bf16[256,512]{1,0:T(8,128)(2,1)S(1)}, u32[]{:S(2)}, u32[]{:S(2)}) collective-permute-start(bf16[256,512]{1,0:T(8,128)(2,1)S(1)} %get-tuple-element.45), channel_id=1, source_target_pairs={{0,2},{2,0},{1,3},{3,1},{4,6},{6,4},{5,7},{7,5},{8,10},{10,8},{9,1... | collective-permute-start | bytes 786440 | tf_op jit(solution)/shard_map/ppermute | solution.py:35
  60.3 3.7 %edge_update_2.1 = (bf16[256,512]{1,0:T(8,128)(2,1)S(1)}, bf16[256,512]{1,0:T(8,128)(2,1)S(1)}) custom-call(s32[8]{0:T(128)S(1)} %copy-done.5, s32[1,1536]{1,0:T(1,128)S(1)} %reshape.13.sender_ref, s32[1,1536]{1,0:T(1,128)S(1)} %reshape.14.slot_ref, bf16[1536,512]{1,0:T(8,128)(2,1)S(1)} %copy-done.1, bf16[768,512]{1,0:T(8,128)(2,1)S(1)} %collective-permute-done.refs_1_, ...), custom_call_target="tpu_custom_call" | custom-call | flops 2550136832 | bytes 8388608 | tf_op jit(solution)/shard_map/edge_update_2/pallas_call | solution.py:306
  63.9 0.6 collective-permute-start.17
  64.5 1.1 %collect.4.refs_1_ = f32[512,512]{1,0:T(8,128)S(1)} custom-call(s32[8]{0:T(128)S(1)} %copy-done.5, s32[1,1536]{1,0:T(1,128)S(1)} %reshape.14.slot_ref, bf16[256,512]{1,0:T(8,128)(2,1)S(1)} %get-tuple-element.41.refs_0_, bf16[256,512]{1,0:T(8,128)(2,1)S(1)} %get-tuple-element.44.refs_1_, bf16[256,512]{1,0:T(8,128)(2,1)S(1)} %get-tuple-element.47.refs_2_), custom_call_target="tpu_custom_call" | custom-call | tf_op jit(solution)/shard_map/collect/pallas_call | solution.py:359
  65.6 0.1 broadcast_in_dim.3
  65.8 0.8 collect.5.refs_1_
  66.7 2.6 %collective-permute-done.16.refs_0_ = bf16[256,512]{1,0:T(8,128)(2,1)S(1)} collective-permute-done((bf16[256,512]{1,0:T(8,128)(2,1)S(1)}, bf16[256,512]{1,0:T(8,128)(2,1)S(1)}, u32[]{:S(2)}, u32[]{:S(2)}) %collective-permute-start.16) | collective-permute-done | bytes 262176 | tf_op jit(solution)/shard_map/ppermute | solution.py:35
  69.2 0.8 collect.6.refs_1_
  70.1 4.0 %collective-permute-done.17.refs_0_ = bf16[256,512]{1,0:T(8,128)(2,1)S(1)} collective-permute-done((bf16[256,512]{1,0:T(8,128)(2,1)S(1)}, bf16[256,512]{1,0:T(8,128)(2,1)S(1)}, u32[]{:S(2)}, u32[]{:S(2)}) %collective-permute-start.17) | collective-permute-done | bytes 262176 | tf_op jit(solution)/shard_map/ppermute | solution.py:35
  74.1 0.8 collect.7
  74.9 0.7 collective-permute-start.18
  75.6 3.5 %collective-permute-start.20 = (bf16[64,512]{1,0:T(8,128)(2,1)S(1)}, bf16[64,512]{1,0:T(8,128)(2,1)S(1)}, u32[]{:S(2)}, u32[]{:S(2)}) collective-permute-start(bf16[64,512]{1,0:T(8,128)(2,1)S(1)} %get-tuple-element.52), channel_id=1, source_target_pairs={{0,13},{1,0},{4,1},{5,4},{8,5},{9,8},{12,9},{13,12},{2,15},{3,2},{... | collective-permute-start | bytes 196616 | tf_op jit(solution)/shard_map/ppermute | solution.py:35
  79.1 1.4 %collective-permute-start.21 = (bf16[64,512]{1,0:T(8,128)(2,1)S(1)}, bf16[64,512]{1,0:T(8,128)(2,1)S(1)}, u32[]{:S(2)}, u32[]{:S(2)}) collective-permute-start(bf16[64,512]{1,0:T(8,128)(2,1)S(1)} %get-tuple-element.53), channel_id=1, source_target_pairs={{0,12},{1,13},{4,0},{5,1},{8,4},{9,5},{12,8},{13,9},{2,14},{3,15},... | collective-permute-start | bytes 196616 | tf_op jit(solution)/shard_map/ppermute | solution.py:35
  80.7 0.0 copy-start.7
  80.7 1.1 %collective-permute-done.18.refs_0_ = bf16[64,512]{1,0:T(8,128)(2,1)S(1)} collective-permute-done((bf16[64,512]{1,0:T(8,128)(2,1)S(1)}, bf16[64,512]{1,0:T(8,128)(2,1)S(1)}, u32[]{:S(2)}, u32[]{:S(2)}) %collective-permute-start.18) | collective-permute-done | bytes 65568 | tf_op jit(solution)/shard_map/ppermute | solution.py:35
  81.8 0.1 collective-permute-done.19.refs_1_
  81.8 2.0 %collective-permute-done.21.refs_3_ = bf16[64,512]{1,0:T(8,128)(2,1)S(1)} collective-permute-done((bf16[64,512]{1,0:T(8,128)(2,1)S(1)}, bf16[64,512]{1,0:T(8,128)(2,1)S(1)}, u32[]{:S(2)}, u32[]{:S(2)}) %collective-permute-start.21) | collective-permute-done | bytes 65568 | tf_op jit(solution)/shard_map/ppermute | solution.py:35
  83.8 1.2 %finish.1 = f32[256,512]{1,0:T(8,128)} custom-call(s32[1,4,64]{2,1,0:T(4,128)S(1)} %copy-done.6, f32[256,512]{1,0:T(8,128)S(1)} %get-tuple-element.49.own, bf16[64,512]{1,0:T(8,128)(2,1)S(1)} %collective-permute-done.18.refs_0_, bf16[64,512]{1,0:T(8,128)(2,1)S(1)} %collective-permute-done.19.refs_1_, bf16[64,512]{1,0:T(8,128)(2,1)S(1)} %collective-permute-done.20.refs_2_, ...), custom_call_target="tpu_custom_call" | custom-call | tf_op jit(solution)/shard_map/finish/pallas_call | solution.py:381
  (24 shorter events, 0.2 us)
Async XLA Ops:
  3.2 10.7 %collective-permute-start.1 = (bf16[272,512]{1,0:T(8,128)(2,1)}, bf16[272,512]{1,0:T(8,128)(2,1)S(1)}, u32[]{:S(2)}, u32[]{:S(2)}) collective-permute-start(bf16[272,512]{1,0:T(8,128)(2,1)} %get-tuple-element.29), channel_id=1, source_target_pairs={{0,2},{2,0},{1,3},{3,1},{4,6},{6,4},{5,7},{7,5},{8,10},{10,8},{9,1... | collective-permute-start | bytes 835592 | tf_op jit(solution)/shard_map/ppermute | solution.py:35
  6.2 7.7 %copy-start.3 = (bf16[256,512]{1,0:T(8,128)(2,1)S(1)}, bf16[256,512]{1,0:T(8,128)(2,1)}, u32[]{:S(2)}) copy-start(bf16[256,512]{1,0:T(8,128)(2,1)} %refs_2_.5) | copy-start | bytes 786436
  6.2 7.7 %copy-start.6 = (s32[1,4,64]{2,1,0:T(4,128)S(1)}, s32[1,4,64]{2,1,0:T(4,128)}, u32[]{:S(2)}) copy-start(s32[1,4,64]{2,1,0:T(4,128)} %rows_ref.3) | copy-start | bytes 3076
  6.2 13.3 %collective-permute-start.6 = (bf16[2,64,1024]{2,1,0:T(8,128)(2,1)}, bf16[2,64,1024]{2,1,0:T(8,128)(2,1)S(1)}, u32[]{:S(2)}, u32[]{:S(2)}) collective-permute-start(bf16[2,64,1024]{2,1,0:T(8,128)(2,1)} %get-tuple-element.36), channel_id=1, source_target_pairs={{0,2},{2,0},{1,3},{3,1},{4,6},{6,4},{5,7},{7,5},{8,10},{10,8},{9,1... | collective-permute-start | bytes 786440 | tf_op jit(solution)/shard_map/ppermute | solution.py:35
  8.2 18.2 %copy-start.8 = (s32[1536]{0:T(1024)S(1)}, s32[1536]{0:T(1024)}, u32[]{:S(2)}) copy-start(s32[1536]{0:T(1024)} %param.12) | copy-start | bytes 18436
  8.2 18.2 %copy-start.9 = (s32[1536]{0:T(1024)S(1)}, s32[1536]{0:T(1024)}, u32[]{:S(2)}) copy-start(s32[1536]{0:T(1024)} %param.11) | copy-start | bytes 18436
  8.2 18.2 %copy-start.1 = (bf16[1536,512]{1,0:T(8,128)(2,1)S(1)}, bf16[1536,512]{1,0:T(8,128)(2,1)}, u32[]{:S(2)}) copy-start(bf16[1536,512]{1,0:T(8,128)(2,1)} %refs_0_.3) | copy-start | bytes 4718596
  8.2 26.6 %collective-permute-start.11 = (bf16[2,128,1024]{2,1,0:T(8,128)(2,1)}, bf16[2,128,1024]{2,1,0:T(8,128)(2,1)S(1)}, u32[]{:S(2)}, u32[]{:S(2)}) collective-permute-start(bf16[2,128,1024]{2,1,0:T(8,128)(2,1)} %prepare_second.1), channel_id=1, source_target_pairs={{0,2},{2,0},{1,3},{3,1},{4,6},{6,4},{5,7},{7,5},{8,10},{10,8},{9,1... | collective-permute-start | bytes 1572872 | tf_op jit(solution)/shard_map/ppermute | solution.py:35
  14.5 7.9 %collective-permute-start.2 = (bf16[64,1024]{1,0:T(8,128)(2,1)S(1)}, bf16[64,1024]{1,0:T(8,128)(2,1)S(1)}, u32[]{:S(2)}, u32[]{:S(2)}) collective-permute-start(bf16[64,1024]{1,0:T(8,128)(2,1)S(1)} %get-tuple-element.32), channel_id=1, source_target_pairs={{0,12},{1,13},{4,0},{5,1},{8,4},{9,5},{12,8},{13,9},{2,14},{3,15},... | collective-permute-start | bytes 393224 | tf_op jit(solution)/shard_map/ppermute | solution.py:35
  18.7 5.1 %collective-permute-start.3 = (bf16[64,1024]{1,0:T(8,128)(2,1)S(1)}, bf16[64,1024]{1,0:T(8,128)(2,1)S(1)}, u32[]{:S(2)}, u32[]{:S(2)}) collective-permute-start(bf16[64,1024]{1,0:T(8,128)(2,1)S(1)} %get-tuple-element.33), channel_id=1, source_target_pairs={{0,13},{1,0},{4,1},{5,4},{8,5},{9,8},{12,9},{13,12},{2,15},{3,2},{... | collective-permute-start | bytes 393224 | tf_op jit(solution)/shard_map/ppermute | solution.py:35
  18.7 6.2 %collective-permute-start.4 = (bf16[64,1024]{1,0:T(8,128)(2,1)S(1)}, bf16[64,1024]{1,0:T(8,128)(2,1)S(1)}, u32[]{:S(2)}, u32[]{:S(2)}) collective-permute-start(bf16[64,1024]{1,0:T(8,128)(2,1)S(1)} %get-tuple-element.34), channel_id=1, source_target_pairs={{0,1},{1,4},{4,5},{5,8},{8,9},{9,12},{12,13},{13,0},{2,3},{3,6},{6... | collective-permute-start | bytes 393224 | tf_op jit(solution)/shard_map/ppermute | solution.py:35
  24.9 6.4 %collective-permute-start.7 = (bf16[2,64,1024]{2,1,0:T(8,128)(2,1)S(1)}, bf16[2,64,1024]{2,1,0:T(8,128)(2,1)S(1)}, u32[]{:S(2)}, u32[]{:S(2)}) collective-permute-start(bf16[2,64,1024]{2,1,0:T(8,128)(2,1)S(1)} %collective-permute-done.6.first), channel_id=1, source_target_pairs={{0,16},{16,0},{1,17},{17,1},{2,18},{18,2},{3,19},{19,3},{4,20},{20... | collective-permute-start | bytes 786440 | tf_op jit(solution)/shard_map/ppermute | solution.py:40
  26.5 20.3 %collective-permute-start = (bf16[768,512]{1,0:T(8,128)(2,1)S(1)}, bf16[768,512]{1,0:T(8,128)(2,1)S(1)}, u32[]{:S(2)}, u32[]{:S(2)}) collective-permute-start(bf16[768,512]{1,0:T(8,128)(2,1)S(1)} %prepare_blocks.1), channel_id=1, source_target_pairs={{0,2},{2,0},{1,3},{3,1},{4,6},{6,4},{5,7},{7,5},{8,10},{10,8},{9,1... | collective-permute-start | bytes 2359304 | tf_op jit(solution)/shard_map/ppermute | solution.py:35
  28.1 6.8 %collective-permute-start.5 = (bf16[64,1024]{1,0:T(8,128)(2,1)S(1)}, bf16[64,1024]{1,0:T(8,128)(2,1)S(1)}, u32[]{:S(2)}, u32[]{:S(2)}) collective-permute-start(bf16[64,1024]{1,0:T(8,128)(2,1)S(1)} %get-tuple-element.35), channel_id=1, source_target_pairs={{0,4},{1,5},{4,8},{5,9},{8,12},{9,13},{12,0},{13,1},{2,6},{3,7},{6... | collective-permute-start | bytes 393224 | tf_op jit(solution)/shard_map/ppermute | solution.py:35
  34.9 11.6 %collective-permute-start.12 = (bf16[2,128,1024]{2,1,0:T(8,128)(2,1)S(1)}, bf16[2,128,1024]{2,1,0:T(8,128)(2,1)S(1)}, u32[]{:S(2)}, u32[]{:S(2)}) collective-permute-start(bf16[2,128,1024]{2,1,0:T(8,128)(2,1)S(1)} %collective-permute-done.11.refs_0_), channel_id=1, source_target_pairs={{0,16},{16,0},{1,17},{17,1},{2,18},{18,2},{3,19},{19,3},{4,20},{20... | collective-permute-start | bytes 1572872 | tf_op jit(solution)/shard_map/ppermute | solution.py:40
  35.4 11.4 %collective-permute-start.8 = (bf16[2,128,1024]{2,1,0:T(8,128)(2,1)S(1)}, bf16[2,128,1024]{2,1,0:T(8,128)(2,1)S(1)}, u32[]{:S(2)}, u32[]{:S(2)}) collective-permute-start(bf16[2,128,1024]{2,1,0:T(8,128)(2,1)S(1)} %join.1.refs_0_), channel_id=1, source_target_pairs={{0,4},{4,0},{8,12},{12,8},{1,5},{5,1},{9,13},{13,9},{2,6},{6,2},{1... | collective-permute-start | bytes 1572872 | tf_op jit(solution)/shard_map/ppermute | solution.py:40
  35.4 11.6 %collective-permute-start.13 = (bf16[2,128,1024]{2,1,0:T(8,128)(2,1)S(1)}, bf16[2,128,1024]{2,1,0:T(8,128)(2,1)S(1)}, u32[]{:S(2)}, u32[]{:S(2)}) collective-permute-start(bf16[2,128,1024]{2,1,0:T(8,128)(2,1)S(1)} %collective-permute-done.11.refs_0_), channel_id=1, source_target_pairs={{0,1},{1,0},{2,3},{3,2},{4,5},{5,4},{6,7},{7,6},{8,9},{9,8},{10,11... | collective-permute-start | bytes 1572872 | tf_op jit(solution)/shard_map/ppermute | solution.py:40
  35.4 13.2 %collective-permute-start.9 = (bf16[2,128,1024]{2,1,0:T(8,128)(2,1)S(1)}, bf16[2,128,1024]{2,1,0:T(8,128)(2,1)S(1)}, u32[]{:S(2)}, u32[]{:S(2)}) collective-permute-start(bf16[2,128,1024]{2,1,0:T(8,128)(2,1)S(1)} %join.1.refs_0_), channel_id=1, source_target_pairs={{0,1},{1,0},{2,3},{3,2},{4,5},{5,4},{6,7},{7,6},{8,9},{9,8},{10,11... | collective-permute-start | bytes 1572872 | tf_op jit(solution)/shard_map/ppermute | solution.py:40
  46.5 1.9 %collective-permute-start.14 = (bf16[2,128,1024]{2,1,0:T(8,128)(2,1)S(1)}, bf16[2,128,1024]{2,1,0:T(8,128)(2,1)S(1)}, u32[]{:S(2)}, u32[]{:S(2)}) collective-permute-start(bf16[2,128,1024]{2,1,0:T(8,128)(2,1)S(1)} %collective-permute-done.12.refs_1_), channel_id=1, source_target_pairs={{0,1},{1,0},{2,3},{3,2},{4,5},{5,4},{6,7},{7,6},{8,9},{9,8},{10,11... | collective-permute-start | bytes 1572872 | tf_op jit(solution)/shard_map/ppermute | solution.py:40
  46.8 2.3 %collective-permute-start.10 = (bf16[2,128,1024]{2,1,0:T(8,128)(2,1)S(1)}, bf16[2,128,1024]{2,1,0:T(8,128)(2,1)S(1)}, u32[]{:S(2)}, u32[]{:S(2)}) collective-permute-start(bf16[2,128,1024]{2,1,0:T(8,128)(2,1)S(1)} %collective-permute-done.8.refs_1_), channel_id=1, source_target_pairs={{0,1},{1,0},{2,3},{3,2},{4,5},{5,4},{6,7},{7,6},{8,9},{9,8},{10,11... | collective-permute-start | bytes 1572872 | tf_op jit(solution)/shard_map/ppermute | solution.py:40
  48.5 1.9 %copy-start = (bf16[3,512,1024]{2,1,0:T(8,128)(2,1)S(1)}, bf16[3,512,1024]{2,1,0:T(8,128)(2,1)}, u32[]{:S(2)}) copy-start(bf16[3,512,1024]{2,1,0:T(8,128)(2,1)} %refs_10_.5) | copy-start | bytes 9437188
  48.6 2.2 %copy-start.2 = (bf16[1024,512]{1,0:T(8,128)(2,1)S(1)}, bf16[1024,512]{1,0:T(8,128)(2,1)}, u32[]{:S(2)}) copy-start(bf16[1024,512]{1,0:T(8,128)(2,1)} %refs_11_.5) | copy-start | bytes 3145732
  48.6 2.2 %copy-start.4 = (f32[512]{0:T(512)S(1)}, f32[512]{0:T(512)}, u32[]{:S(2)}) copy-start(f32[512]{0:T(512)} %param.17) | copy-start | bytes 6148
  48.6 2.1 %copy-start.5 = (s32[8]{0:T(128)S(1)}, s32[8]{0:T(128)}, u32[]{:S(2)}) copy-start(s32[8]{0:T(128)} %counts.13) | copy-start | bytes 100
  54.4 11.4 %collective-permute-start.15 = (bf16[256,512]{1,0:T(8,128)(2,1)S(1)}, bf16[256,512]{1,0:T(8,128)(2,1)S(1)}, u32[]{:S(2)}, u32[]{:S(2)}) collective-permute-start(bf16[256,512]{1,0:T(8,128)(2,1)S(1)} %get-tuple-element.42), channel_id=1, source_target_pairs={{0,2},{2,0},{1,3},{3,1},{4,6},{6,4},{5,7},{7,5},{8,10},{10,8},{9,1... | collective-permute-start | bytes 786440 | tf_op jit(solution)/shard_map/ppermute | solution.py:35
  58.7 10.6 %collective-permute-start.16 = (bf16[256,512]{1,0:T(8,128)(2,1)S(1)}, bf16[256,512]{1,0:T(8,128)(2,1)S(1)}, u32[]{:S(2)}, u32[]{:S(2)}) collective-permute-start(bf16[256,512]{1,0:T(8,128)(2,1)S(1)} %get-tuple-element.45), channel_id=1, source_target_pairs={{0,2},{2,0},{1,3},{3,1},{4,6},{6,4},{5,7},{7,5},{8,10},{10,8},{9,1... | collective-permute-start | bytes 786440 | tf_op jit(solution)/shard_map/ppermute | solution.py:35
  63.9 10.1 %collective-permute-start.17 = (bf16[256,512]{1,0:T(8,128)(2,1)S(1)}, bf16[256,512]{1,0:T(8,128)(2,1)S(1)}, u32[]{:S(2)}, u32[]{:S(2)}) collective-permute-start(bf16[256,512]{1,0:T(8,128)(2,1)S(1)} %get-tuple-element.48), channel_id=1, source_target_pairs={{0,2},{2,0},{1,3},{3,1},{4,6},{6,4},{5,7},{7,5},{8,10},{10,8},{9,1... | collective-permute-start | bytes 786440 | tf_op jit(solution)/shard_map/ppermute | solution.py:35
  74.9 6.9 %collective-permute-start.18 = (bf16[64,512]{1,0:T(8,128)(2,1)S(1)}, bf16[64,512]{1,0:T(8,128)(2,1)S(1)}, u32[]{:S(2)}, u32[]{:S(2)}) collective-permute-start(bf16[64,512]{1,0:T(8,128)(2,1)S(1)} %get-tuple-element.50), channel_id=1, source_target_pairs={{0,4},{1,5},{4,8},{5,9},{8,12},{9,13},{12,0},{13,1},{2,6},{3,7},{6... | collective-permute-start | bytes 196616 | tf_op jit(solution)/shard_map/ppermute | solution.py:35
  75.6 6.2 %collective-permute-start.19 = (bf16[64,512]{1,0:T(8,128)(2,1)S(1)}, bf16[64,512]{1,0:T(8,128)(2,1)S(1)}, u32[]{:S(2)}, u32[]{:S(2)}) collective-permute-start(bf16[64,512]{1,0:T(8,128)(2,1)S(1)} %get-tuple-element.51), channel_id=1, source_target_pairs={{0,1},{1,4},{4,5},{5,8},{8,9},{9,12},{12,13},{13,0},{2,3},{3,6},{6... | collective-permute-start | bytes 196616 | tf_op jit(solution)/shard_map/ppermute | solution.py:35
  75.6 6.2 %collective-permute-start.20 = (bf16[64,512]{1,0:T(8,128)(2,1)S(1)}, bf16[64,512]{1,0:T(8,128)(2,1)S(1)}, u32[]{:S(2)}, u32[]{:S(2)}) collective-permute-start(bf16[64,512]{1,0:T(8,128)(2,1)S(1)} %get-tuple-element.52), channel_id=1, source_target_pairs={{0,13},{1,0},{4,1},{5,4},{8,5},{9,8},{12,9},{13,12},{2,15},{3,2},{... | collective-permute-start | bytes 196616 | tf_op jit(solution)/shard_map/ppermute | solution.py:35
  79.1 4.7 %collective-permute-start.21 = (bf16[64,512]{1,0:T(8,128)(2,1)S(1)}, bf16[64,512]{1,0:T(8,128)(2,1)S(1)}, u32[]{:S(2)}, u32[]{:S(2)}) collective-permute-start(bf16[64,512]{1,0:T(8,128)(2,1)S(1)} %get-tuple-element.53), channel_id=1, source_target_pairs={{0,12},{1,13},{4,0},{5,1},{8,4},{9,5},{12,8},{13,9},{2,14},{3,15},... | collective-permute-start | bytes 196616 | tf_op jit(solution)/shard_map/ppermute | solution.py:35
  80.7 4.3 %copy-start.7 = (bf16[1536,512]{1,0:T(8,128)(2,1)}, bf16[1536,512]{1,0:T(8,128)(2,1)S(1)}, u32[]{:S(2)}) copy-start(bf16[1536,512]{1,0:T(8,128)(2,1)S(1)} %constant_dynamic-update-slice_fusion) | copy-start | bytes 4718596

commit v4 on v3

--- a/solution.py
+++ b/solution.py
@@ -80,36 +80,26 @@
     return copy, finish
 
 
-def first_kernel(axes, w_in, nodes, gain, packed, first, sems):
+def first_kernel(axes, w_in, first, sems):
     copy, finish = copier(sems)
-    count, width = nodes.shape
-    rows = width >> len(axes)
+    rows = w_in.shape[1] >> len(axes)
     start = pl.multiple_of(share_index(axes) * rows, rows)
     for part in range(2):
         copy(w_in.at[part, pl.ds(start, rows), :], first.at[part])
-    copy(nodes, packed.at[pl.ds(0, count), :])
-    high = gain[...].astype(bf16)
-    middle = (gain[...] - high.astype(f32)).astype(bf16)
-    low = (gain[...] - high.astype(f32) - middle.astype(f32)).astype(bf16)
-    row_ids = lax.broadcasted_iota(i32, (GAIN_ROWS, width), 0)
-    rows = jnp.where(row_ids == 0, high.astype(f32), 0.0)
-    rows = jnp.where(row_ids == 1, middle.astype(f32), rows)
-    rows = jnp.where(row_ids == 2, low.astype(f32), rows)
-    packed[count:, :] = rows.astype(bf16)
     finish()
 
 
-def prepare_first(weight_in, nodes, gain, ways, axes):
-    count, width = nodes.shape
+def prepare_first(weight_in, axes):
+    _, width, channels = weight_in.shape
     return pl.pallas_call(
         functools.partial(first_kernel, axes),
-        out_shape=[shape(count + GAIN_ROWS, width), shape(2, width >> len(axes), ways * width)],
-        in_specs=[HBM, HBM, VMEM],
-        out_specs=[VMEM] * 2,
-        scratch_shapes=[pltpu.SemaphoreType.DMA((3,))],
+        out_shape=shape(2, width >> len(axes), channels),
+        in_specs=[HBM],
+        out_specs=VMEM,
+        scratch_shapes=[pltpu.SemaphoreType.DMA((2,))],
         compiler_params=params(PREPARE_VMEM_BYTES),
         name="prepare_first",
-    )(weight_in, nodes, gain)
+    )(weight_in)
 
 
 def second_kernel(ways, axes, w_in, w_out, second, sems):
@@ -136,59 +126,67 @@
     )(weight_in, weight_out)
 
 
-def block_kernel(ways, edges, *rest):
+def gain_terms(gain, width):
+    high = gain.astype(bf16)
+    middle = (gain - high.astype(f32)).astype(bf16)
+    low = (gain - high.astype(f32) - middle.astype(f32)).astype(bf16)
+    row_ids = lax.broadcasted_iota(i32, (GAIN_ROWS, width), 0)
+    rows = jnp.where(row_ids == 0, high.astype(f32), 0.0)
+    rows = jnp.where(row_ids == 1, middle.astype(f32), rows)
+    return jnp.where(row_ids == 2, low.astype(f32), rows).astype(bf16)
+
+
+def block_kernel(ways, split, early, edges, gain, *rest):
     blocks, sems = rest[:-1], rest[-1]
     copy, finish = copier(sems)
     me = lax.axis_index("chan")
-    mine = edges.shape[0] // ways
+    width = edges.shape[1]
     for d in range(1, ways):
-        row = pl.multiple_of(lax.rem(me + d, ways) * mine, TILE)
-        copy(edges.at[pl.ds(row, mine), :], blocks[d - 1])
+        row = pl.multiple_of(lax.rem(me + d, ways) * split, TILE)
+        copy(edges.at[pl.ds(row, split), :], blocks[d - 1].at[pl.ds(0, split), :])
+        if early:
+            copy(edges.at[pl.ds(ways * split, early), :], blocks[d - 1].at[pl.ds(split, early), :])
+        blocks[d - 1][split + early :, :] = gain_terms(gain[...], width)
+    if len(blocks) == ways:
+        late = blocks[-1].shape[0]
+        copy(edges.at[pl.ds(ways * split + early, late), :], blocks[-1])
     finish()
 
 
-def prepare_blocks(edge_feats, ways):
-    slot_count, width = edge_feats.shape
-    return pl.pallas_call(
-        functools.partial(block_kernel, ways),
-        out_shape=[shape(slot_count // ways, width)] * (ways - 1),
-        in_specs=[HBM],
-        out_specs=[VMEM] * (ways - 1),
-        scratch_shapes=[pltpu.SemaphoreType.DMA((ways - 1,))],
+def prepare_blocks(edge_feats, gain, ways, split, early, late):
+    width = edge_feats.shape[1]
+    outs = [shape(split + early + GAIN_ROWS, width)] * (ways - 1) + [shape(late, width)] * (late > 0)
+    copies = (ways - 1) * (2 if early else 1) + (late > 0)
+    return pl.pallas_call(
+        functools.partial(block_kernel, ways, split, early),
+        out_shape=outs,
+        in_specs=[HBM, VMEM],
+        out_specs=[VMEM] * len(outs),
+        scratch_shapes=[pltpu.SemaphoreType.DMA((copies,))],
         compiler_params=params(),
         name="prepare_blocks",
-    )(edge_feats)
-
-
-def unpack_kernel(ways, halo_count, rows_ref, nodes, *refs):
-    messages, outs = refs[: ways - 1], list(refs[ways - 1 :])
-    halos = [outs.pop(0) for _ in range(halo_count)]
-    others, gains = outs[::2], outs[1::2]
-    count, width = nodes.shape
-    for d in range(1, ways):
-        message = messages[d - 1]
-        others[d - 1][...] = message[:count, :]
-        parts = message[count:, :].astype(f32)
-        gains[d - 1][...] = parts[0:1, :] + parts[1:2, :] + parts[2:3, :]
-    for j in range(halo_count):
+    )(edge_feats, gain)
+
+
+def halo_kernel(ways, rows_ref, *refs):
+    nodes, halos = refs[:ways], refs[ways:]
+    count, width = nodes[0].shape
+    for j, halo in enumerate(halos):
         hits = onehot(column(rows_ref[0, j : j + 1, :]), count)
         for d in range(ways):
-            table = nodes[...] if d == 0 else others[d - 1][...]
-            halos[j][:, d * width : (d + 1) * width] = dot(hits, table).astype(bf16)
-
-
-def unpack(halo_rows, nodes, messages, ways):
+            halo[:, d * width : (d + 1) * width] = dot(hits, nodes[d][...]).astype(bf16)
+
+
+def halo_gather(halo_rows, nodes):
+    ways = len(nodes)
     _, offsets, size = halo_rows.shape
-    count, width = nodes.shape
-    each = [shape(count, width), shape(1, width, dtype=f32)]
-    outs = pl.pallas_call(
-        functools.partial(unpack_kernel, ways, offsets),
-        out_shape=[shape(size, ways * width)] * offsets + each * (ways - 1),
-        compiler_params=params(),
-        cost_estimate=pl.CostEstimate(flops=6000000 * 1000, bytes_accessed=4 * 1024 * 1024, transcendentals=0),
-        name="unpack",
-    )(halo_rows, nodes, *messages)
-    return outs[:offsets], outs[offsets::2], outs[offsets + 1 :: 2]
+    return pl.pallas_call(
+        functools.partial(halo_kernel, ways),
+        out_shape=[shape(size, ways * nodes[0].shape[1])] * offsets,
+        compiler_params=params(),
+        cost_estimate=pl.CostEstimate(flops=6 * 10**9, bytes_accessed=4 * 1024 * 1024, transcendentals=0),
+        name="halo_gather",
+    )(halo_rows, *nodes)
 
 
 def join_kernel(first, second, out):
@@ -238,18 +236,38 @@
     )(*pieces)
 
 
-def split_rows(slot_count, ways):
-    tiles = slot_count // (ways * TILE)
-    first = -(-tiles // 3)
-    second = (tiles - first + 1) // 2
-    return [size * TILE for size in (first, second, tiles - first - second) if size]
+def stage_kernel(w_in, w_out, inner, outer, sems):
+    copy, finish = copier(sems)
+    copy(w_in, inner)
+    copy(w_out, outer)
+    finish()
+
+
+def stage(weight_in, weight_out):
+    return pl.pallas_call(
+        stage_kernel,
+        out_shape=[shape(*weight_in.shape), shape(*weight_out.shape)],
+        in_specs=[HBM] * 2,
+        out_specs=[VMEM] * 2,
+        scratch_shapes=[pltpu.SemaphoreType.DMA((2,))],
+        compiler_params=params(),
+        name="stage",
+    )(weight_in, weight_out)
+
+
+def plan_rows(slot_count, ways):
+    tiles = slot_count // TILE
+    shared = [2, 2] if ways == 2 and tiles >= 8 and tiles % 2 == 0 else []
+    alone = (tiles - sum(shared)) // ways
+    chunks = [alone - alone // 2, alone // 2]
+    return [size * TILE for size in chunks if size], [size * TILE for size in shared]
 
 
 def starts_of(sizes):
     return [sum(sizes[:k]) for k in range(len(sizes))]
 
 
-def edge_kernel(ways, before, mine, counts, sender_ref, slot_ref, *refs):
+def edge_kernel(ways, place, mine, late, counts, sender_ref, slot_ref, *refs):
     refs = list(refs)
 
     def take(count):
@@ -257,15 +275,21 @@
         del refs[:count]
         return taken
 
-    own, nodes, gains, halos = take(ways), take(ways), take(ways), take(2 * RADIUS)
+    (own, own_gain), mains, others = take(2), take(ways - 1), take(ways - 1 if late else 0)
+    nodes, halos = take(ways), take(2 * RADIUS)
     w_in, w_out = take(2)
     others_a, others_b = take(ways - 1), take(ways - 1)
     outs = refs
-    width = own[0].shape[1]
+    width = own.shape[1]
     channels = ways * width
     me = lax.axis_index("chan")
-    first = pl.multiple_of(me * (own[0].shape[0] // ways) + before, TILE)
-    edges = [own[0][pl.ds(first, mine), :]] + [e[before : before + mine, :] for e in own[1:]]
+    split, base, start = place
+    first = pl.multiple_of(me * split + base, TILE)
+    edges = [own[pl.ds(first, mine), :]]
+    for d, block in enumerate(mains):
+        here = mine - others[d].shape[0] if late else mine
+        rows = block[start : start + here, :]
+        edges.append(jnp.concatenate([rows, others[d][...]], axis=0) if late else rows)
     local_nodes = nodes[0].shape[0]
     halo_count = sum(h.shape[0] for h in halos)
     to_sender = onehot(column(sender_ref[:, pl.ds(first, mine)]), local_nodes)
@@ -293,21 +317,26 @@
     part = lax.axis_index("dom") * lax.axis_size("rep") + lax.axis_index("rep")
     live_rows = TILE * counts[part] - first
     live = lax.broadcasted_iota(i32, (mine, width), 0) < live_rows
-    for d in range(ways):
-        normed = (projected[d] - mean) * scale * gains[d][...]
+    for d in range(len(outs)):
+        if d == 0:
+            gain = own_gain[...]
+        else:
+            terms = mains[d - 1][mains[d - 1].shape[0] - GAIN_ROWS :, :].astype(f32)
+            gain = terms[0:1, :] + terms[1:2, :] + terms[2:3, :]
+        normed = (projected[d] - mean) * scale * gain
         outs[d][...] = jnp.where(live, (edges[d].astype(f32) + normed).astype(bf16), edges[d])
 
 
-def edge_update(k, before, mine, counts, senders, slots, edges, nodes, gains, halos, w_in, w_out, others_a, others_b):
+def edge_update(k, place, mine, results, counts, senders, slots, own, gain, blocks, others, nodes, halos, w_in, w_out, others_a, others_b):
     ways = len(nodes)
-    width = edges[0].shape[1]
+    width = own.shape[1]
     channels = ways * width
-    operands = [*edges, *nodes, *gains, *halos, w_in, w_out, *others_a, *others_b]
-    return pl.pallas_call(
-        functools.partial(edge_kernel, ways, before, mine),
-        out_shape=[shape(mine, width)] * ways,
+    operands = [own, gain, *blocks, *others, *nodes, *halos, w_in, w_out, *others_a, *others_b]
+    return pl.pallas_call(
+        functools.partial(edge_kernel, ways, place, mine, bool(others)),
+        out_shape=[shape(mine, width)] * results,
         in_specs=[SMEM] + [VMEM] * (2 + len(operands)),
-        out_specs=[VMEM] * ways,
+        out_specs=[VMEM] * results,
         compiler_params=params(),
         cost_estimate=pl.CostEstimate(
             flops=2 * mine * channels * (4 * channels + 768),
@@ -325,11 +354,10 @@
     me = lax.axis_index("chan")
     part = lax.axis_index("dom") * lax.axis_size("rep") + lax.axis_index("rep")
     live_rows = TILE * counts[part]
-    whole = slot_ref.shape[1] // ways
     table_rows = refs[0].shape[0] + (sum(r.shape[0] for r in refs[1:]) if last else 0)
-    for (d, before), block in zip(places, parts):
+    for (d, split, base), block in zip(places, parts):
         mine = block.shape[0]
-        first = pl.multiple_of(lax.rem(me + d, ways) * whole + before, TILE)
+        first = pl.multiple_of(lax.rem(me + d, ways) * split + base, TILE)
         slots = slot_ref[:, pl.ds(first, mine)]
         ids = first + lax.broadcasted_iota(i32, (1, mine), 1)
         slots = jnp.where(ids < live_rows, slots, -1)
@@ -366,6 +394,23 @@
     )(counts, slots, *parts, *before)
 
 
+def write_kernel(ways, places, *refs):
+    parts, out = refs[:-1], refs[-1]
+    me = lax.axis_index("chan")
+    for (d, split, base), block in zip(places, parts):
+        first = pl.multiple_of(lax.rem(me + d, ways) * split + base, TILE)
+        out[pl.ds(first, block.shape[0]), :] = block[...]
+
+
+def write(places, parts, slot_count, ways):
+    return pl.pallas_call(
+        functools.partial(write_kernel, ways, places),
+        out_shape=shape(slot_count, parts[0].shape[1]),
+        compiler_params=params(),
+        name="write",
+    )(*parts)
+
+
 def finish_kernel(rows_ref, own, *refs):
     returned, out = refs[:-1], refs[-1]
     total = own[...]
@@ -398,59 +443,67 @@
     norm_gain,
 ):
     ways = lax.axis_size("chan")
-    me = lax.axis_index("chan")
     offsets = [shift_by for shift_by in range(-RADIUS, RADIUS + 1) if shift_by != 0]
     local_nodes, width = node_feats.shape
     halo_size = halo_rows.shape[2]
     slot_count = edge_feats.shape[0]
-    sizes = split_rows(slot_count, ways)
-    whole = slot_count // ways
+    alone, shared = plan_rows(slot_count, ways)
+    split, early, late = sum(alone), sum(shared[:1]), sum(shared[1:])
     distances = range(1, ways)
     axes_a, axes_b = even(SHARERS_A), even(SHARERS_B)
 
     gain = norm_gain.reshape(1, width)
     sender_row, slot_row = senders.reshape(1, -1), receiver_slot.reshape(1, -1)
-    packed, message_a = prepare_first(weight_in, node_feats, gain, ways, axes_a)
+    message_a = prepare_first(weight_in, axes_a)
     message_b = prepare_second(weight_in, weight_out, ways, axes_b)
-    blocks = prepare_blocks(edge_feats, ways)
+    blocks = prepare_blocks(edge_feats, gain, ways, split, early, late)
     blocks = [tie(block, sender_row, slot_row) for block in blocks]
-    received = [shifted(packed, "chan", d) for d in distances]
+    nodes = [node_feats] + [shifted(node_feats, "chan", d) for d in distances]
     crossed_a = [shifted(message_a, "chan", d) for d in distances]
     crossed_b = [shifted(message_b, "chan", d) for d in distances]
-    outgoing, nodes, gains = unpack(halo_rows, node_feats, received, ways)
-    nodes, gains = [node_feats, *nodes], [gain, *gains]
+    outgoing = halo_gather(halo_rows, nodes)
     halos = [shifted(rows, ("dom", "rep"), by) for rows, by in zip(outgoing, offsets)]
-    edges = [edge_feats] + [shifted(blocks[d - 1], "chan", d) for d in distances]
+    edges = [shifted(blocks[d - 1], "chan", d) for d in distances]
+    late_edges = [shifted(blocks[-1], "chan", d) for d in distances if late]
     pieces = [tie(piece, *halos[:3]) for piece in crossed_a]
     pieces = [join(piece, swapped(piece, axes_a[0])) for piece in pieces]
     pieces = [tie(piece, *halos[3:]) for piece in pieces]
     crossed_b = [tie(piece, *pieces) for piece in crossed_b]
-    others_a = [assemble(gather_shares(piece, axes_a[1:], edges[1:]), axes_a) for piece in pieces]
-    others_b = [assemble(gather_shares(piece, axes_b, ()), axes_b) for piece in crossed_b]
+    others_a = [assemble(gather_shares(piece, axes_a[1:], edges), axes_a) for piece in pieces]
+    inner, outer = stage(tie(weight_in, *outgoing), weight_out)
+    others_b = [assemble(gather_shares(piece, axes_b, [inner, outer]), axes_b) for piece in crossed_b]
 
     def collected(places, parts, sums, last=False):
         return collect(places, parts, sums, tile_counts, slot_row, ways, local_nodes, halo_size, last)
 
-    finished = jnp.zeros((slot_count, width), bf16)
-    kept, arrived = [], []
-    for k, (before, mine) in enumerate(zip(starts_of(sizes), sizes)):
-        parts = edge_update(
-            k, before, mine, tile_counts, sender_row, slot_row, edges, nodes, gains, halos,
-            weight_in, weight_out, others_a, others_b,
+    jobs = [(split, before, before, mine, ways) for before, mine in zip(starts_of(alone), alone)]
+    if shared:
+        jobs.append((0, ways * split, split, early + late, 1))
+    parts, places, order = [], [], edge_feats
+    for k, (stride, base, start, mine, results) in enumerate(jobs):
+        others = late_edges if k == len(alone) else []
+        outs = edge_update(
+            k, (stride, base, start), mine, results, tile_counts, sender_row, slot_row, order, gain, edges, others,
+            nodes, halos, inner, outer, others_a, others_b,
         )
-        edges[0] = tie(edges[0], *parts)
-        kept.append(parts[0])
-        arrived.append([shifted(parts[d], "chan", -d) for d in distances])
-        for d, part in enumerate([parts[0], *arrived[-1]]):
-            first = ((me + d) % ways) * whole + before
-            finished = lax.dynamic_update_slice_in_dim(finished, part, first, 0)
-    starts = starts_of(sizes)
-    (sums,) = collected([(0, b) for b in starts], kept, None)
-    for k in range(len(sizes) - 1):
-        (sums,) = collected([(d, starts[k]) for d in distances], arrived[k], sums)
-    own, *pieces = collected([(d, starts[-1]) for d in distances], arrived[-1], sums, True)
+        order = tie(order, *outs)
+        outs = [outs[0]] + [shifted(outs[d], "chan", -d) for d in range(1, results)]
+        parts.append(outs)
+        places.append([(d, stride, base) for d in range(results)])
+
+    def chosen(which):
+        return [places[k][d] for k, d in which], [parts[k][d] for k, d in which]
+
+    count = len(alone)
+    final = [(count - 1, d) for d in distances]
+    own_parts = [(k, 0) for k in range(len(jobs))]
+    (sums,) = collected(*chosen(own_parts), None)
+    for k in range(count - 1):
+        (sums,) = collected(*chosen([(k, d) for d in distances]), sums)
+    own, *pieces = collected(*chosen(final), sums, True)
     returned = [shifted(piece, ("dom", "rep"), -by) for piece, by in zip(pieces, offsets)]
-    return (finished, finish(halo_rows, own, returned))
+    everything = chosen([(k, d) for k, outs in enumerate(parts) for d in range(len(outs))])
+    return (write(*everything, slot_count, ways), finish(halo_rows, own, returned))
 
 
 def solution(mesh):

time: 85.2 us -> 77 us (0.904)
  waiting for transfers between devices: 38.6 us -> 27.1 us
  Pallas kernels: 21.3 us -> 24 us
  starting transfers between devices: 22.5 us -> 24.6 us
  local copies, waits for them, and re-layouts: 1.73 us -> 0.33 us
    ppermute x7, waiting for transfers between devices: 15.7 us -> 5.07 us  [swapped(): return lax.ppermute(block, axis, [(i, i ^ 1) for i in range(size)])]
    pallas_call x6 -> x8, Pallas kernels: 14.2 us -> 17.6 us  [the longest x3 13.7 us: edge_update(): pl.pallas_call(functools.partial(edge_kernel, ways, place, mine, bool(oth...]
    ppermute x15, starting transfers between devices: 19.8 us -> 21.5 us  [shifted(): lax.ppermute(block, axis, [(i, (i + distance) % size) for i in range(size)])]
    unnamed x20 -> x18, local copies, waits for them, and re-layouts: 1.47 us -> 0.32 us
    ppermute x15, waiting for transfers between devices: 23 us -> 22 us  [shifted(): lax.ppermute(block, axis, [(i, (i + distance) % size) for i in range(size)])]
    pallas_call x4 -> x3, Pallas kernels: 3.63 us -> 2.93 us  [collect(): pl.pallas_call(functools.partial(collect_kernel, ways, places, local_node...]
  transfers between devices with their start and end apart: 22 -> 22, of which waited for: 16 -> 11; matrix products, arithmetic and copies ran while one was open for 0% -> 0% of each run, Pallas kernels for 15% -> 29%
where the time goes in v4:
time: 77 us; the launch traced here: 76.8 us
  waiting for transfers between devices  27.1 us (35%)
  starting transfers between devices  24.6 us (32%)
  Pallas kernels  24 us (31%)
  between operations  0.88 us (1%)
    ppermute x15, waiting for transfers between devices, shifted(): lax.ppermute(block, axis, [(i, (i + distance) % size) for i in range(size)])  22 us
    ppermute x15, starting transfers between devices, shifted(): lax.ppermute(block, axis, [(i, (i + distance) % size) for i in range(size)])  21.5 us
    pallas_call x3, Pallas kernels, edge_update(): pl.pallas_call(functools.partial(edge_kernel, ways, place, mine, bool(oth...  13.7 us
    ppermute x7, waiting for transfers between devices, swapped(): return lax.ppermute(block, axis, [(i, i ^ 1) for i in range(size)])  5.07 us
    ppermute x7, starting transfers between devices, swapped(): return lax.ppermute(block, axis, [(i, i ^ 1) for i in range(size)])  3.11 us
    pallas_call x3, Pallas kernels, collect(): pl.pallas_call(functools.partial(collect_kernel, ways, places, local_node...  2.93 us
    pallas_call x1, Pallas kernels, prepare_second(): pl.pallas_call(functools.partial(second_kernel, ways, axes), out_shape=sh...  1.86 us
    pallas_call x1, Pallas kernels, prepare_first(): pl.pallas_call(functools.partial(first_kernel, axes), out_shape=shape(2,...  1.68 us
  transfers between devices with their start and end apart: 22, of which 11 were waited for; matrix products, arithmetic and copies ran while one was open for 0% of the time, Pallas kernels for 29%

profile of v4, /device:TPU:0, one launch (start us, length us, event | category | flops | bytes accessed | tf_op | source)
XLA Modules:
  0.0 76.8 jit_solution(5454060846802997652)
XLA Ops:
  0.6 3.0 %collective-permute-start.1 = (bf16[256,512]{1,0:T(8,128)(2,1)}, bf16[256,512]{1,0:T(8,128)(2,1)S(1)}, u32[]{:S(2)}, u32[]{:S(2)}) collective-permute-start(bf16[256,512]{1,0:T(8,128)(2,1)} %refs_4_.1), channel_id=1, source_target_pairs={{0,2},{2,0},{1,3},{3,1},{4,6},{6,4},{5,7},{7,5},{8,10},{10,8},{9,1... | collective-permute-start | bytes 786440 | tf_op jit(solution)/shard_map/ppermute | solution.py:35
  3.6 1.7 %prepare_first.1 = bf16[2,64,1024]{2,1,0:T(8,128)(2,1)} custom-call(bf16[3,512,1024]{2,1,0:T(8,128)(2,1)} %w_in.4), custom_call_target="tpu_custom_call" | custom-call | tf_op jit(solution)/shard_map/prepare_first/pallas_call | solution.py:94
  5.3 0.0 copy-start.3
  5.3 0.0 copy-start.6
  5.3 0.1 collective-permute-start.6
  5.5 1.9 %prepare_second.1 = bf16[2,128,1024]{2,1,0:T(8,128)(2,1)} custom-call(bf16[3,512,1024]{2,1,0:T(8,128)(2,1)} %w_in.4, bf16[1024,512]{1,0:T(8,128)(2,1)} %w_out.3), custom_call_target="tpu_custom_call" | custom-call | tf_op jit(solution)/shard_map/prepare_second/pallas_call | solution.py:118
  7.3 0.0 copy-start.7
  7.3 0.0 copy-start.8
  7.3 0.0 copy-start.1
  7.4 0.0 copy-start.4
  7.4 2.1 %collective-permute-start.11 = (bf16[2,128,1024]{2,1,0:T(8,128)(2,1)}, bf16[2,128,1024]{2,1,0:T(8,128)(2,1)S(1)}, u32[]{:S(2)}, u32[]{:S(2)}) collective-permute-start(bf16[2,128,1024]{2,1,0:T(8,128)(2,1)} %prepare_second.1), channel_id=1, source_target_pairs={{0,2},{2,0},{1,3},{3,1},{4,6},{6,4},{5,7},{7,5},{8,10},{10,8},{9,1... | collective-permute-start | bytes 1572872 | tf_op jit(solution)/shard_map/ppermute | solution.py:35
  9.4 1.6 %collective-permute-done.1.refs_1_.refs_4_.refs_5_ = bf16[256,512]{1,0:T(8,128)(2,1)S(1)} collective-permute-done((bf16[256,512]{1,0:T(8,128)(2,1)}, bf16[256,512]{1,0:T(8,128)(2,1)S(1)}, u32[]{:S(2)}, u32[]{:S(2)}) %collective-permute-start.1) | collective-permute-done | bytes 262176 | tf_op jit(solution)/shard_map/ppermute | solution.py:35
  11.0 0.5 halo_gather.1
  11.5 0.0 copy-start.2
  11.5 4.2 %collective-permute-start.2 = (bf16[64,1024]{1,0:T(8,128)(2,1)S(1)}, bf16[64,1024]{1,0:T(8,128)(2,1)S(1)}, u32[]{:S(2)}, u32[]{:S(2)}) collective-permute-start(bf16[64,1024]{1,0:T(8,128)(2,1)S(1)} %get-tuple-element.31), channel_id=1, source_target_pairs={{0,12},{1,13},{4,0},{5,1},{8,4},{9,5},{12,8},{13,9},{2,14},{3,15},... | collective-permute-start | bytes 393224 | tf_op jit(solution)/shard_map/ppermute | solution.py:35
  15.7 0.5 collective-permute-start.4
  16.3 0.1 prepare_blocks.1
  16.5 0.1 collective-permute-done.6.first
  16.6 2.1 %collective-permute-start = (bf16[784,512]{1,0:T(8,128)(2,1)S(1)}, bf16[784,512]{1,0:T(8,128)(2,1)S(1)}, u32[]{:S(2)}, u32[]{:S(2)}) collective-permute-start(bf16[784,512]{1,0:T(8,128)(2,1)S(1)} %get-tuple-element.30), channel_id=1, source_target_pairs={{0,2},{2,0},{1,3},{3,1},{4,6},{6,4},{5,7},{7,5},{8,10},{10,8},{9,1... | collective-permute-start | bytes 2408456 | tf_op jit(solution)/shard_map/ppermute | solution.py:35
  18.7 0.8 %collective-permute-done.2.refs_5_.refs_6_ = bf16[64,1024]{1,0:T(8,128)(2,1)S(1)} collective-permute-done((bf16[64,1024]{1,0:T(8,128)(2,1)S(1)}, bf16[64,1024]{1,0:T(8,128)(2,1)S(1)}, u32[]{:S(2)}, u32[]{:S(2)}) %collective-permute-start.2) | collective-permute-done | bytes 131104 | tf_op jit(solution)/shard_map/ppermute | solution.py:35
  19.5 1.4 %collective-permute-done.3.refs_6_.refs_7_ = bf16[64,1024]{1,0:T(8,128)(2,1)S(1)} collective-permute-done((bf16[64,1024]{1,0:T(8,128)(2,1)S(1)}, bf16[64,1024]{1,0:T(8,128)(2,1)S(1)}, u32[]{:S(2)}, u32[]{:S(2)}) %collective-permute-start.3) | collective-permute-done | bytes 131104 | tf_op jit(solution)/shard_map/ppermute | solution.py:35
  20.9 1.1 %collective-permute-done.4.refs_7_.refs_8_ = bf16[64,1024]{1,0:T(8,128)(2,1)S(1)} collective-permute-done((bf16[64,1024]{1,0:T(8,128)(2,1)S(1)}, bf16[64,1024]{1,0:T(8,128)(2,1)S(1)}, u32[]{:S(2)}, u32[]{:S(2)}) %collective-permute-start.4) | collective-permute-done | bytes 131104 | tf_op jit(solution)/shard_map/ppermute | solution.py:35
  21.9 1.5 %collective-permute-start.7 = (bf16[2,64,1024]{2,1,0:T(8,128)(2,1)S(1)}, bf16[2,64,1024]{2,1,0:T(8,128)(2,1)S(1)}, u32[]{:S(2)}, u32[]{:S(2)}) collective-permute-start(bf16[2,64,1024]{2,1,0:T(8,128)(2,1)S(1)} %collective-permute-done.6.first), channel_id=1, source_target_pairs={{0,16},{16,0},{1,17},{17,1},{2,18},{18,2},{3,19},{19,3},{4,20},{20... | collective-permute-start | bytes 786440 | tf_op jit(solution)/shard_map/ppermute | solution.py:40
  23.5 4.8 %collective-permute-done.7.second = bf16[2,64,1024]{2,1,0:T(8,128)(2,1)S(1)} collective-permute-done((bf16[2,64,1024]{2,1,0:T(8,128)(2,1)S(1)}, bf16[2,64,1024]{2,1,0:T(8,128)(2,1)S(1)}, u32[]{:S(2)}, u32[]{:S(2)}) %collective-permute-start.7) | collective-permute-done | bytes 262176 | tf_op jit(solution)/shard_map/ppermute | solution.py:40
  28.4 1.9 %collective-permute-done.5.refs_8_.refs_9_ = bf16[64,1024]{1,0:T(8,128)(2,1)S(1)} collective-permute-done((bf16[64,1024]{1,0:T(8,128)(2,1)S(1)}, bf16[64,1024]{1,0:T(8,128)(2,1)S(1)}, u32[]{:S(2)}, u32[]{:S(2)}) %collective-permute-start.5) | collective-permute-done | bytes 131104 | tf_op jit(solution)/shard_map/ppermute | solution.py:35
  30.2 0.0 collective-permute-start.8
  30.2 0.0 collective-permute-done.11.refs_0_
  30.2 0.5 collective-permute-start.12
  30.8 0.3 stage.1
  31.1 0.1 collective-permute-start.9
  31.1 0.5 collective-permute-start.13
  31.6 12.6 %collective-permute-done.refs_2_ = bf16[784,512]{1,0:T(8,128)(2,1)S(1)} collective-permute-done((bf16[784,512]{1,0:T(8,128)(2,1)S(1)}, bf16[784,512]{1,0:T(8,128)(2,1)S(1)}, u32[]{:S(2)}, u32[]{:S(2)}) %collective-permute-start) | collective-permute-done | bytes 802848 | tf_op jit(solution)/shard_map/ppermute | solution.py:35
  44.2 0.0 collective-permute-done.8.refs_1_
  44.2 0.0 collective-permute-start.10
  44.2 0.0 collective-permute-done.12.refs_1_
  44.2 0.5 collective-permute-start.14
  44.7 1.7 %collective-permute-start.17 = (bf16[256,512]{1,0:T(8,128)(2,1)S(1)}, bf16[256,512]{1,0:T(8,128)(2,1)S(1)}, u32[]{:S(2)}, u32[]{:S(2)}) collective-permute-start(bf16[256,512]{1,0:T(8,128)(2,1)S(1)} %get-tuple-element.50), channel_id=1, source_target_pairs={{0,2},{2,0},{1,3},{3,1},{4,6},{6,4},{5,7},{7,5},{8,10},{10,8},{9,1... | collective-permute-start | bytes 786440 | tf_op jit(solution)/shard_map/ppermute | solution.py:35
  46.5 0.0 collective-permute-done.10.refs_3_
  46.5 0.2 assemble.2.refs_11_.refs_12_
  46.6 0.0 copy-start.5
  46.7 0.0 collective-permute-done.13.refs_2_
  46.7 0.2 collective-permute-done.14.refs_3_
  46.9 0.2 assemble.3.refs_12_.refs_13_
  47.0 0.3 copy-done.5
  47.3 3.7 %edge_update_0.1 = (bf16[256,512]{1,0:T(8,128)(2,1)S(1)}, bf16[256,512]{1,0:T(8,128)(2,1)S(1)}) custom-call(s32[8]{0:T(128)S(1)} %copy-done.5, s32[1,1536]{1,0:T(1,128)S(1)} %reshape.13.sender_ref, s32[1,1536]{1,0:T(1,128)S(1)} %reshape.14.slot_ref, bf16[1536,512]{1,0:T(8,128)(2,1)S(1)} %copy-done.1, f32[1,512]{1,0:T(1,128)S(1)} %bitcast.2, ...), custom_call_target="tpu_custom_call" | custom-call | flops 2550136832 | bytes 8388608 | tf_op jit(solution)/shard_map/edge_update_0/pallas_call | solution.py:335
  51.0 1.6 %collective-permute-start.15 = (bf16[256,512]{1,0:T(8,128)(2,1)S(1)}, bf16[256,512]{1,0:T(8,128)(2,1)S(1)}, u32[]{:S(2)}, u32[]{:S(2)}) collective-permute-start(bf16[256,512]{1,0:T(8,128)(2,1)S(1)} %get-tuple-element.44), channel_id=1, source_target_pairs={{0,2},{2,0},{1,3},{3,1},{4,6},{6,4},{5,7},{7,5},{8,10},{10,8},{9,1... | collective-permute-start | bytes 786440 | tf_op jit(solution)/shard_map/ppermute | solution.py:35
  52.6 3.7 %edge_update_1.1 = (bf16[256,512]{1,0:T(8,128)(2,1)S(1)}, bf16[256,512]{1,0:T(8,128)(2,1)S(1)}) custom-call(s32[8]{0:T(128)S(1)} %copy-done.5, s32[1,1536]{1,0:T(1,128)S(1)} %reshape.13.sender_ref, s32[1,1536]{1,0:T(1,128)S(1)} %reshape.14.slot_ref, bf16[1536,512]{1,0:T(8,128)(2,1)S(1)} %copy-done.1, f32[1,512]{1,0:T(1,128)S(1)} %bitcast.3, ...), custom_call_target="tpu_custom_call" | custom-call | flops 2550136832 | bytes 8388608 | tf_op jit(solution)/shard_map/edge_update_1/pallas_call | solution.py:335
  56.2 0.6 collective-permute-start.16
  56.8 0.0 collective-permute-done.17.refs_3_
  56.8 6.3 %edge_update_2.1.refs_4_.refs_2_ = bf16[512,512]{1,0:T(8,128)(2,1)S(1)} custom-call(s32[8]{0:T(128)S(1)} %copy-done.5, s32[1,1536]{1,0:T(1,128)S(1)} %reshape.13.sender_ref, s32[1,1536]{1,0:T(1,128)S(1)} %reshape.14.slot_ref, bf16[1536,512]{1,0:T(8,128)(2,1)S(1)} %copy-done.1, f32[1,512]{1,0:T(1,128)S(1)} %bitcast.4, ...), custom_call_target="tpu_custom_call" | custom-call | flops 5100273664 | bytes 8388608 | tf_op jit(solution)/shard_map/edge_update_2/pallas_call | solution.py:335
  63.2 1.2 %collect.3.refs_1_ = f32[512,512]{1,0:T(8,128)S(1)} custom-call(s32[8]{0:T(128)S(1)} %copy-done.5, s32[1,1536]{1,0:T(1,128)S(1)} %reshape.14.slot_ref, bf16[256,512]{1,0:T(8,128)(2,1)S(1)} %get-tuple-element.43.refs_0_, bf16[256,512]{1,0:T(8,128)(2,1)S(1)} %get-tuple-element.46.refs_2_.refs_1_, bf16[512,512]{1,0:T(8,128)(2,1)S(1)} %edge_update_2.1.refs_4_.refs_2_), custom_call_target="tpu_custom_call" | custom-call | tf_op jit(solution)/shard_map/collect/pallas_call | solution.py:387
  64.4 0.0 collective-permute-done.15.refs_1_.refs_0_
  64.4 0.8 %collect.4.refs_1_ = f32[512,512]{1,0:T(8,128)S(1)} custom-call(s32[8]{0:T(128)S(1)} %copy-done.5, s32[1,1536]{1,0:T(1,128)S(1)} %reshape.14.slot_ref, bf16[256,512]{1,0:T(8,128)(2,1)S(1)} %collective-permute-done.15.refs_1_.refs_0_, f32[512,512]{1,0:T(8,128)S(1)} %collect.3.refs_1_), custom_call_target="tpu_custom_call" | custom-call | tf_op jit(solution)/shard_map/collect/pallas_call | solution.py:387
  65.3 0.0 collective-permute-done.16.refs_3_.refs_0_
  65.3 0.8 %collect.5 = (f32[256,512]{1,0:T(8,128)S(1)}, bf16[64,512]{1,0:T(8,128)(2,1)S(1)}, bf16[64,512]{1,0:T(8,128)(2,1)S(1)}, bf16[64,512]{1,0:T(8,128)(2,1)S(1)}, bf16[64,512]{1,0:T(8,128)(2,1)S(1)}) custom-call(s32[8]{0:T(128)S(1)} %copy-done.5, s32[1,1536]{1,0:T(1,128)S(1)} %reshape.14.slot_ref, bf16[256,512]{1,0:T(8,128)(2,1)S(1)} %collective-permute-done.16.refs_3_.refs_0_, ...), custom_call_target="tpu_custom_call" | custom-call | tf_op jit(solution)/shard_map/collect/pallas_call | solution.py:387
  66.2 1.6 %collective-permute-start.18 = (bf16[64,512]{1,0:T(8,128)(2,1)S(1)}, bf16[64,512]{1,0:T(8,128)(2,1)S(1)}, u32[]{:S(2)}, u32[]{:S(2)}) collective-permute-start(bf16[64,512]{1,0:T(8,128)(2,1)S(1)} %get-tuple-element.52), channel_id=1, source_target_pairs={{0,4},{1,5},{4,8},{5,9},{8,12},{9,13},{12,0},{13,1},{2,6},{3,7},{6... | collective-permute-start | bytes 196616 | tf_op jit(solution)/shard_map/ppermute | solution.py:35
  67.8 0.0 collective-permute-start.19
  67.8 3.5 %collective-permute-start.20 = (bf16[64,512]{1,0:T(8,128)(2,1)S(1)}, bf16[64,512]{1,0:T(8,128)(2,1)S(1)}, u32[]{:S(2)}, u32[]{:S(2)}) collective-permute-start(bf16[64,512]{1,0:T(8,128)(2,1)S(1)} %get-tuple-element.54), channel_id=1, source_target_pairs={{0,13},{1,0},{4,1},{5,4},{8,5},{9,8},{12,9},{13,12},{2,15},{3,2},{... | collective-permute-start | bytes 196616 | tf_op jit(solution)/shard_map/ppermute | solution.py:35
  71.3 0.4 collective-permute-start.21
  71.8 1.3 %write.1 = bf16[1536,512]{1,0:T(8,128)(2,1)} custom-call(bf16[256,512]{1,0:T(8,128)(2,1)S(1)} %get-tuple-element.43.refs_0_, bf16[256,512]{1,0:T(8,128)(2,1)S(1)} %collective-permute-done.15.refs_1_.refs_0_, bf16[256,512]{1,0:T(8,128)(2,1)S(1)} %get-tuple-element.46.refs_2_.refs_1_, bf16[256,512]{1,0:T(8,128)(2,1)S(1)} %collective-permute-done.16.refs_3_.refs_0_, ...), custom_call_target="tpu_custom_call" | custom-call | tf_op jit(solution)/shard_map/write/pallas_call | solution.py:406
  73.0 0.3 collective-permute-done.19.refs_1_
  73.3 0.0 collective-permute-done.20.refs_2_
  73.4 2.2 %collective-permute-done.21.refs_3_ = bf16[64,512]{1,0:T(8,128)(2,1)S(1)} collective-permute-done((bf16[64,512]{1,0:T(8,128)(2,1)S(1)}, bf16[64,512]{1,0:T(8,128)(2,1)S(1)}, u32[]{:S(2)}, u32[]{:S(2)}) %collective-permute-start.21) | collective-permute-done | bytes 65568 | tf_op jit(solution)/shard_map/ppermute | solution.py:35
  75.6 1.2 %finish.1 = f32[256,512]{1,0:T(8,128)} custom-call(s32[1,4,64]{2,1,0:T(4,128)S(1)} %copy-done.6, f32[256,512]{1,0:T(8,128)S(1)} %get-tuple-element.51.own, bf16[64,512]{1,0:T(8,128)(2,1)S(1)} %collective-permute-done.18.refs_0_, bf16[64,512]{1,0:T(8,128)(2,1)S(1)} %collective-permute-done.19.refs_1_, bf16[64,512]{1,0:T(8,128)(2,1)S(1)} %collective-permute-done.20.refs_2_, ...), custom_call_target="tpu_custom_call" | custom-call | tf_op jit(solution)/shard_map/finish/pallas_call | solution.py:426
  (16 shorter events, 0.1 us)
Async XLA Ops:
  0.6 10.4 %collective-permute-start.1 = (bf16[256,512]{1,0:T(8,128)(2,1)}, bf16[256,512]{1,0:T(8,128)(2,1)S(1)}, u32[]{:S(2)}, u32[]{:S(2)}) collective-permute-start(bf16[256,512]{1,0:T(8,128)(2,1)} %refs_4_.1), channel_id=1, source_target_pairs={{0,2},{2,0},{1,3},{3,1},{4,6},{6,4},{5,7},{7,5},{8,10},{10,8},{9,1... | collective-permute-start | bytes 786440 | tf_op jit(solution)/shard_map/ppermute | solution.py:35
  5.3 5.7 %copy-start.3 = (bf16[256,512]{1,0:T(8,128)(2,1)S(1)}, bf16[256,512]{1,0:T(8,128)(2,1)}, u32[]{:S(2)}) copy-start(bf16[256,512]{1,0:T(8,128)(2,1)} %refs_4_.1) | copy-start | bytes 786436
  5.3 5.6 %copy-start.6 = (s32[1,4,64]{2,1,0:T(4,128)S(1)}, s32[1,4,64]{2,1,0:T(4,128)}, u32[]{:S(2)}) copy-start(s32[1,4,64]{2,1,0:T(4,128)} %rows_ref.3) | copy-start | bytes 3076
  5.3 11.2 %collective-permute-start.6 = (bf16[2,64,1024]{2,1,0:T(8,128)(2,1)}, bf16[2,64,1024]{2,1,0:T(8,128)(2,1)S(1)}, u32[]{:S(2)}, u32[]{:S(2)}) collective-permute-start(bf16[2,64,1024]{2,1,0:T(8,128)(2,1)} %prepare_first.1), channel_id=1, source_target_pairs={{0,2},{2,0},{1,3},{3,1},{4,6},{6,4},{5,7},{7,5},{8,10},{10,8},{9,1... | collective-permute-start | bytes 786440 | tf_op jit(solution)/shard_map/ppermute | solution.py:35
  7.3 8.9 %copy-start.7 = (s32[1536]{0:T(1024)S(1)}, s32[1536]{0:T(1024)}, u32[]{:S(2)}) copy-start(s32[1536]{0:T(1024)} %param.12) | copy-start | bytes 18436
  7.3 8.9 %copy-start.8 = (s32[1536]{0:T(1024)S(1)}, s32[1536]{0:T(1024)}, u32[]{:S(2)}) copy-start(s32[1536]{0:T(1024)} %param.11) | copy-start | bytes 18436
  7.3 8.9 %copy-start.1 = (bf16[1536,512]{1,0:T(8,128)(2,1)S(1)}, bf16[1536,512]{1,0:T(8,128)(2,1)}, u32[]{:S(2)}) copy-start(bf16[1536,512]{1,0:T(8,128)(2,1)} %refs_0_.5) | copy-start | bytes 4718596
  7.4 8.9 %copy-start.4 = (f32[512]{0:T(512)S(1)}, f32[512]{0:T(512)}, u32[]{:S(2)}) copy-start(f32[512]{0:T(512)} %param.17) | copy-start | bytes 6148
  7.4 22.9 %collective-permute-start.11 = (bf16[2,128,1024]{2,1,0:T(8,128)(2,1)}, bf16[2,128,1024]{2,1,0:T(8,128)(2,1)S(1)}, u32[]{:S(2)}, u32[]{:S(2)}) collective-permute-start(bf16[2,128,1024]{2,1,0:T(8,128)(2,1)} %prepare_second.1), channel_id=1, source_target_pairs={{0,2},{2,0},{1,3},{3,1},{4,6},{6,4},{5,7},{7,5},{8,10},{10,8},{9,1... | collective-permute-start | bytes 1572872 | tf_op jit(solution)/shard_map/ppermute | solution.py:35
  11.0 19.8 %copy-start = (bf16[3,512,1024]{2,1,0:T(8,128)(2,1)S(1)}, bf16[3,512,1024]{2,1,0:T(8,128)(2,1)}, u32[]{:S(2)}) copy-start(bf16[3,512,1024]{2,1,0:T(8,128)(2,1)} %w_in.4) | copy-start | bytes 9437188
  11.5 19.2 %copy-start.2 = (bf16[1024,512]{1,0:T(8,128)(2,1)S(1)}, bf16[1024,512]{1,0:T(8,128)(2,1)}, u32[]{:S(2)}) copy-start(bf16[1024,512]{1,0:T(8,128)(2,1)} %w_out.3) | copy-start | bytes 3145732
  11.5 7.9 %collective-permute-start.2 = (bf16[64,1024]{1,0:T(8,128)(2,1)S(1)}, bf16[64,1024]{1,0:T(8,128)(2,1)S(1)}, u32[]{:S(2)}, u32[]{:S(2)}) collective-permute-start(bf16[64,1024]{1,0:T(8,128)(2,1)S(1)} %get-tuple-element.31), channel_id=1, source_target_pairs={{0,12},{1,13},{4,0},{5,1},{8,4},{9,5},{12,8},{13,9},{2,14},{3,15},... | collective-permute-start | bytes 393224 | tf_op jit(solution)/shard_map/ppermute | solution.py:35
  15.7 5.1 %collective-permute-start.3 = (bf16[64,1024]{1,0:T(8,128)(2,1)S(1)}, bf16[64,1024]{1,0:T(8,128)(2,1)S(1)}, u32[]{:S(2)}, u32[]{:S(2)}) collective-permute-start(bf16[64,1024]{1,0:T(8,128)(2,1)S(1)} %get-tuple-element.32), channel_id=1, source_target_pairs={{0,13},{1,0},{4,1},{5,4},{8,5},{9,8},{12,9},{13,12},{2,15},{3,2},{... | collective-permute-start | bytes 393224 | tf_op jit(solution)/shard_map/ppermute | solution.py:35
  15.7 6.2 %collective-permute-start.4 = (bf16[64,1024]{1,0:T(8,128)(2,1)S(1)}, bf16[64,1024]{1,0:T(8,128)(2,1)S(1)}, u32[]{:S(2)}, u32[]{:S(2)}) collective-permute-start(bf16[64,1024]{1,0:T(8,128)(2,1)S(1)} %get-tuple-element.33), channel_id=1, source_target_pairs={{0,1},{1,4},{4,5},{5,8},{8,9},{9,12},{12,13},{13,0},{2,3},{3,6},{6... | collective-permute-start | bytes 393224 | tf_op jit(solution)/shard_map/ppermute | solution.py:35
  16.6 27.6 %collective-permute-start = (bf16[784,512]{1,0:T(8,128)(2,1)S(1)}, bf16[784,512]{1,0:T(8,128)(2,1)S(1)}, u32[]{:S(2)}, u32[]{:S(2)}) collective-permute-start(bf16[784,512]{1,0:T(8,128)(2,1)S(1)} %get-tuple-element.30), channel_id=1, source_target_pairs={{0,2},{2,0},{1,3},{3,1},{4,6},{6,4},{5,7},{7,5},{8,10},{10,8},{9,1... | collective-permute-start | bytes 2408456 | tf_op jit(solution)/shard_map/ppermute | solution.py:35
  21.9 6.4 %collective-permute-start.7 = (bf16[2,64,1024]{2,1,0:T(8,128)(2,1)S(1)}, bf16[2,64,1024]{2,1,0:T(8,128)(2,1)S(1)}, u32[]{:S(2)}, u32[]{:S(2)}) collective-permute-start(bf16[2,64,1024]{2,1,0:T(8,128)(2,1)S(1)} %collective-permute-done.6.first), channel_id=1, source_target_pairs={{0,16},{16,0},{1,17},{17,1},{2,18},{18,2},{3,19},{19,3},{4,20},{20... | collective-permute-start | bytes 786440 | tf_op jit(solution)/shard_map/ppermute | solution.py:40
  23.5 6.8 %collective-permute-start.5 = (bf16[64,1024]{1,0:T(8,128)(2,1)S(1)}, bf16[64,1024]{1,0:T(8,128)(2,1)S(1)}, u32[]{:S(2)}, u32[]{:S(2)}) collective-permute-start(bf16[64,1024]{1,0:T(8,128)(2,1)S(1)} %get-tuple-element.34), channel_id=1, source_target_pairs={{0,4},{1,5},{4,8},{5,9},{8,12},{9,13},{12,0},{13,1},{2,6},{3,7},{6... | collective-permute-start | bytes 393224 | tf_op jit(solution)/shard_map/ppermute | solution.py:35
  30.2 14.0 %collective-permute-start.8 = (bf16[2,128,1024]{2,1,0:T(8,128)(2,1)S(1)}, bf16[2,128,1024]{2,1,0:T(8,128)(2,1)S(1)}, u32[]{:S(2)}, u32[]{:S(2)}) collective-permute-start(bf16[2,128,1024]{2,1,0:T(8,128)(2,1)S(1)} %join.1.refs_0_), channel_id=1, source_target_pairs={{0,4},{4,0},{8,12},{12,8},{1,5},{5,1},{9,13},{13,9},{2,6},{6,2},{1... | collective-permute-start | bytes 1572872 | tf_op jit(solution)/shard_map/ppermute | solution.py:40
  30.2 14.0 %collective-permute-start.12 = (bf16[2,128,1024]{2,1,0:T(8,128)(2,1)S(1)}, bf16[2,128,1024]{2,1,0:T(8,128)(2,1)S(1)}, u32[]{:S(2)}, u32[]{:S(2)}) collective-permute-start(bf16[2,128,1024]{2,1,0:T(8,128)(2,1)S(1)} %collective-permute-done.11.refs_0_), channel_id=1, source_target_pairs={{0,16},{16,0},{1,17},{17,1},{2,18},{18,2},{3,19},{19,3},{4,20},{20... | collective-permute-start | bytes 1572872 | tf_op jit(solution)/shard_map/ppermute | solution.py:40
  31.1 15.4 %collective-permute-start.9 = (bf16[2,128,1024]{2,1,0:T(8,128)(2,1)S(1)}, bf16[2,128,1024]{2,1,0:T(8,128)(2,1)S(1)}, u32[]{:S(2)}, u32[]{:S(2)}) collective-permute-start(bf16[2,128,1024]{2,1,0:T(8,128)(2,1)S(1)} %join.1.refs_0_), channel_id=1, source_target_pairs={{0,1},{1,0},{2,3},{3,2},{4,5},{5,4},{6,7},{7,6},{8,9},{9,8},{10,11... | collective-permute-start | bytes 1572872 | tf_op jit(solution)/shard_map/ppermute | solution.py:40
  31.1 15.5 %collective-permute-start.13 = (bf16[2,128,1024]{2,1,0:T(8,128)(2,1)S(1)}, bf16[2,128,1024]{2,1,0:T(8,128)(2,1)S(1)}, u32[]{:S(2)}, u32[]{:S(2)}) collective-permute-start(bf16[2,128,1024]{2,1,0:T(8,128)(2,1)S(1)} %collective-permute-done.11.refs_0_), channel_id=1, source_target_pairs={{0,1},{1,0},{2,3},{3,2},{4,5},{5,4},{6,7},{7,6},{8,9},{9,8},{10,11... | collective-permute-start | bytes 1572872 | tf_op jit(solution)/shard_map/ppermute | solution.py:40
  44.2 2.3 %collective-permute-start.10 = (bf16[2,128,1024]{2,1,0:T(8,128)(2,1)S(1)}, bf16[2,128,1024]{2,1,0:T(8,128)(2,1)S(1)}, u32[]{:S(2)}, u32[]{:S(2)}) collective-permute-start(bf16[2,128,1024]{2,1,0:T(8,128)(2,1)S(1)} %collective-permute-done.8.refs_1_), channel_id=1, source_target_pairs={{0,1},{1,0},{2,3},{3,2},{4,5},{5,4},{6,7},{7,6},{8,9},{9,8},{10,11... | collective-permute-start | bytes 1572872 | tf_op jit(solution)/shard_map/ppermute | solution.py:40
  44.2 2.7 %collective-permute-start.14 = (bf16[2,128,1024]{2,1,0:T(8,128)(2,1)S(1)}, bf16[2,128,1024]{2,1,0:T(8,128)(2,1)S(1)}, u32[]{:S(2)}, u32[]{:S(2)}) collective-permute-start(bf16[2,128,1024]{2,1,0:T(8,128)(2,1)S(1)} %collective-permute-done.12.refs_1_), channel_id=1, source_target_pairs={{0,1},{1,0},{2,3},{3,2},{4,5},{5,4},{6,7},{7,6},{8,9},{9,8},{10,11... | collective-permute-start | bytes 1572872 | tf_op jit(solution)/shard_map/ppermute | solution.py:40
  44.7 12.1 %collective-permute-start.17 = (bf16[256,512]{1,0:T(8,128)(2,1)S(1)}, bf16[256,512]{1,0:T(8,128)(2,1)S(1)}, u32[]{:S(2)}, u32[]{:S(2)}) collective-permute-start(bf16[256,512]{1,0:T(8,128)(2,1)S(1)} %get-tuple-element.50), channel_id=1, source_target_pairs={{0,2},{2,0},{1,3},{3,1},{4,6},{6,4},{5,7},{7,5},{8,10},{10,8},{9,1... | collective-permute-start | bytes 786440 | tf_op jit(solution)/shard_map/ppermute | solution.py:35
  46.6 0.7 copy-start.5
  51.0 13.4 %collective-permute-start.15 = (bf16[256,512]{1,0:T(8,128)(2,1)S(1)}, bf16[256,512]{1,0:T(8,128)(2,1)S(1)}, u32[]{:S(2)}, u32[]{:S(2)}) collective-permute-start(bf16[256,512]{1,0:T(8,128)(2,1)S(1)} %get-tuple-element.44), channel_id=1, source_target_pairs={{0,2},{2,0},{1,3},{3,1},{4,6},{6,4},{5,7},{7,5},{8,10},{10,8},{9,1... | collective-permute-start | bytes 786440 | tf_op jit(solution)/shard_map/ppermute | solution.py:35
  56.2 9.1 %collective-permute-start.16 = (bf16[256,512]{1,0:T(8,128)(2,1)S(1)}, bf16[256,512]{1,0:T(8,128)(2,1)S(1)}, u32[]{:S(2)}, u32[]{:S(2)}) collective-permute-start(bf16[256,512]{1,0:T(8,128)(2,1)S(1)} %get-tuple-element.47), channel_id=1, source_target_pairs={{0,2},{2,0},{1,3},{3,1},{4,6},{6,4},{5,7},{7,5},{8,10},{10,8},{9,1... | collective-permute-start | bytes 786440 | tf_op jit(solution)/shard_map/ppermute | solution.py:35
  66.2 6.9 %collective-permute-start.18 = (bf16[64,512]{1,0:T(8,128)(2,1)S(1)}, bf16[64,512]{1,0:T(8,128)(2,1)S(1)}, u32[]{:S(2)}, u32[]{:S(2)}) collective-permute-start(bf16[64,512]{1,0:T(8,128)(2,1)S(1)} %get-tuple-element.52), channel_id=1, source_target_pairs={{0,4},{1,5},{4,8},{5,9},{8,12},{9,13},{12,0},{13,1},{2,6},{3,7},{6... | collective-permute-start | bytes 196616 | tf_op jit(solution)/shard_map/ppermute | solution.py:35
  67.8 5.6 %collective-permute-start.19 = (bf16[64,512]{1,0:T(8,128)(2,1)S(1)}, bf16[64,512]{1,0:T(8,128)(2,1)S(1)}, u32[]{:S(2)}, u32[]{:S(2)}) collective-permute-start(bf16[64,512]{1,0:T(8,128)(2,1)S(1)} %get-tuple-element.53), channel_id=1, source_target_pairs={{0,1},{1,4},{4,5},{5,8},{8,9},{9,12},{12,13},{13,0},{2,3},{3,6},{6... | collective-permute-start | bytes 196616 | tf_op jit(solution)/shard_map/ppermute | solution.py:35
  67.8 5.6 %collective-permute-start.20 = (bf16[64,512]{1,0:T(8,128)(2,1)S(1)}, bf16[64,512]{1,0:T(8,128)(2,1)S(1)}, u32[]{:S(2)}, u32[]{:S(2)}) collective-permute-start(bf16[64,512]{1,0:T(8,128)(2,1)S(1)} %get-tuple-element.54), channel_id=1, source_target_pairs={{0,13},{1,0},{4,1},{5,4},{8,5},{9,8},{12,9},{13,12},{2,15},{3,2},{... | collective-permute-start | bytes 196616 | tf_op jit(solution)/shard_map/ppermute | solution.py:35
  71.3 4.3 %collective-permute-start.21 = (bf16[64,512]{1,0:T(8,128)(2,1)S(1)}, bf16[64,512]{1,0:T(8,128)(2,1)S(1)}, u32[]{:S(2)}, u32[]{:S(2)}) collective-permute-start(bf16[64,512]{1,0:T(8,128)(2,1)S(1)} %get-tuple-element.55), channel_id=1, source_target_pairs={{0,12},{1,13},{4,0},{5,1},{8,4},{9,5},{12,8},{13,9},{2,14},{3,15},... | collective-permute-start | bytes 196616 | tf_op jit(solution)/shard_map/ppermute | solution.py:35

commit v5 on v4

--- a/solution.py
+++ b/solution.py
@@ -124,6 +124,23 @@
         compiler_params=params(PREPARE_VMEM_BYTES),
         name="prepare_second",
     )(weight_in, weight_out)
+
+
+def mask_kernel(counts, slots, out):
+    part = lax.axis_index("dom") * lax.axis_size("rep") + lax.axis_index("rep")
+    ids = lax.broadcasted_iota(i32, slots.shape, 1)
+    out[...] = jnp.where(ids < TILE * counts[part], slots[...], -1)
+
+
+def mask_slots(counts, slots):
+    return pl.pallas_call(
+        mask_kernel,
+        out_shape=shape(*slots.shape, dtype=i32),
+        in_specs=[SMEM, VMEM],
+        out_specs=VMEM,
+        compiler_params=params(),
+        name="mask_slots",
+    )(counts, slots)
 
 
 def gain_terms(gain, width):
@@ -267,7 +284,7 @@
     return [sum(sizes[:k]) for k in range(len(sizes))]
 
 
-def edge_kernel(ways, place, mine, late, counts, sender_ref, slot_ref, *refs):
+def edge_kernel(ways, place, mine, late, sender_ref, slot_ref, *refs):
     refs = list(refs)
 
     def take(count):
@@ -293,7 +310,8 @@
     local_nodes = nodes[0].shape[0]
     halo_count = sum(h.shape[0] for h in halos)
     to_sender = onehot(column(sender_ref[:, pl.ds(first, mine)]), local_nodes)
-    to_slot = onehot(column(slot_ref[:, pl.ds(first, mine)]), local_nodes + halo_count)
+    slots = column(slot_ref[:, pl.ds(first, mine)])
+    to_slot = onehot(slots, local_nodes + halo_count)
     table = jnp.concatenate([h[...] for h in halos], axis=0)
     preact = None
     for d in range(ways):
@@ -306,7 +324,7 @@
         got = (got + dot(to_slot[:, local_nodes:], table[:, d * width : (d + 1) * width])).astype(bf16)
         term = dot(edges[d], weights[0]) + dot(sent, weights[1]) + dot(got, weights[2])
         preact = term if preact is None else preact + term
-    hidden = (preact / (1.0 + jnp.exp(-preact))).astype(bf16)
+    hidden = (0.5 * preact * (1.0 + jnp.tanh(0.5 * preact))).astype(bf16)
     projected = [dot(hidden, w_out[...])]
     for d in range(1, ways):
         blocks = [slice(h * width, (h + 1) * width) for h in range(ways)]
@@ -314,9 +332,7 @@
     mean = sum(jnp.sum(p, axis=1, keepdims=True) for p in projected) / channels
     square = sum(jnp.sum(p * p, axis=1, keepdims=True) for p in projected) / channels
     scale = lax.rsqrt(square - mean * mean + 1e-05)
-    part = lax.axis_index("dom") * lax.axis_size("rep") + lax.axis_index("rep")
-    live_rows = TILE * counts[part] - first
-    live = lax.broadcasted_iota(i32, (mine, width), 0) < live_rows
+    live = jnp.concatenate([slots] * (width // 128), axis=1) >= 0
     for d in range(len(outs)):
         if d == 0:
             gain = own_gain[...]
@@ -327,7 +343,7 @@
         outs[d][...] = jnp.where(live, (edges[d].astype(f32) + normed).astype(bf16), edges[d])
 
 
-def edge_update(k, place, mine, results, counts, senders, slots, own, gain, blocks, others, nodes, halos, w_in, w_out, others_a, others_b):
+def edge_update(k, place, mine, results, senders, slots, own, gain, blocks, others, nodes, halos, w_in, w_out, others_a, others_b):
     ways = len(nodes)
     width = own.shape[1]
     channels = ways * width
@@ -335,7 +351,7 @@
     return pl.pallas_call(
         functools.partial(edge_kernel, ways, place, mine, bool(others)),
         out_shape=[shape(mine, width)] * results,
-        in_specs=[SMEM] + [VMEM] * (2 + len(operands)),
+        in_specs=[VMEM] * (2 + len(operands)),
         out_specs=[VMEM] * results,
         compiler_params=params(),
         cost_estimate=pl.CostEstimate(
@@ -344,23 +360,19 @@
             transcendentals=mine * channels,
         ),
         name=f"edge_update_{k}",
-    )(counts, senders, slots, *operands)
-
-
-def collect_kernel(ways, places, local_nodes, last, counts, slot_ref, *refs):
+    )(senders, slots, *operands)
+
+
+def collect_kernel(ways, places, local_nodes, last, slot_ref, *refs):
     refs = list(refs)
     parts = [refs.pop(0) for _ in places]
     sums = refs.pop(0)[...] if len(refs) > (1 + 2 * RADIUS if last else 1) else None
     me = lax.axis_index("chan")
-    part = lax.axis_index("dom") * lax.axis_size("rep") + lax.axis_index("rep")
-    live_rows = TILE * counts[part]
     table_rows = refs[0].shape[0] + (sum(r.shape[0] for r in refs[1:]) if last else 0)
     for (d, split, base), block in zip(places, parts):
         mine = block.shape[0]
         first = pl.multiple_of(lax.rem(me + d, ways) * split + base, TILE)
         slots = slot_ref[:, pl.ds(first, mine)]
-        ids = first + lax.broadcasted_iota(i32, (1, mine), 1)
-        slots = jnp.where(ids < live_rows, slots, -1)
         rows = lax.broadcasted_iota(i32, (table_rows, mine), 0)
         hits = (rows == jnp.broadcast_to(slots, (table_rows, mine))).astype(f32).astype(bf16)
         term = dot(hits, block[...])
@@ -376,7 +388,7 @@
         start += size
 
 
-def collect(places, parts, sums, counts, slots, ways, local_nodes, halo_size, last):
+def collect(places, parts, sums, slots, ways, local_nodes, halo_size, last):
     width = parts[0].shape[1]
     table_rows = local_nodes + 2 * RADIUS * halo_size
     before = [] if sums is None else [sums]
@@ -387,11 +399,11 @@
     return pl.pallas_call(
         functools.partial(collect_kernel, ways, places, local_nodes, last),
         out_shape=outs,
-        in_specs=[SMEM] + [VMEM] * (1 + len(parts) + len(before)),
+        in_specs=[VMEM] * (1 + len(parts) + len(before)),
         out_specs=[VMEM] * len(outs),
         compiler_params=params(),
         name="collect",
-    )(counts, slots, *parts, *before)
+    )(slots, *parts, *before)
 
 
 def write_kernel(ways, places, *refs):
@@ -413,13 +425,12 @@
 
 def finish_kernel(rows_ref, own, *refs):
     returned, out = refs[:-1], refs[-1]
-    total = own[...]
+    hits = []
     for j, rows in enumerate(returned):
-        size = rows.shape[0]
-        ids = lax.broadcasted_iota(i32, (own.shape[0], size), 0)
-        hits = (ids == jnp.broadcast_to(rows_ref[0, j : j + 1, :], ids.shape)).astype(f32).astype(bf16)
-        total = total + dot(hits, rows[...])
-    out[...] = total
+        ids = lax.broadcasted_iota(i32, (own.shape[0], rows.shape[0]), 0)
+        hits.append((ids == jnp.broadcast_to(rows_ref[0, j : j + 1, :], ids.shape)).astype(f32).astype(bf16))
+    rows = jnp.concatenate([r[...] for r in returned], axis=0)
+    out[...] = own[...] + dot(jnp.concatenate(hits, axis=1), rows)
 
 
 def finish(halo_rows, own, returned):
@@ -453,7 +464,7 @@
     axes_a, axes_b = even(SHARERS_A), even(SHARERS_B)
 
     gain = norm_gain.reshape(1, width)
-    sender_row, slot_row = senders.reshape(1, -1), receiver_slot.reshape(1, -1)
+    sender_row, slot_row = senders.reshape(1, -1), mask_slots(tile_counts, receiver_slot.reshape(1, -1))
     message_a = prepare_first(weight_in, axes_a)
     message_b = prepare_second(weight_in, weight_out, ways, axes_b)
     blocks = prepare_blocks(edge_feats, gain, ways, split, early, late)
@@ -474,7 +485,7 @@
     others_b = [assemble(gather_shares(piece, axes_b, [inner, outer]), axes_b) for piece in crossed_b]
 
     def collected(places, parts, sums, last=False):
-        return collect(places, parts, sums, tile_counts, slot_row, ways, local_nodes, halo_size, last)
+        return collect(places, parts, sums, slot_row, ways, local_nodes, halo_size, last)
 
     jobs = [(split, before, before, mine, ways) for before, mine in zip(starts_of(alone), alone)]
     if shared:
@@ -483,7 +494,7 @@
     for k, (stride, base, start, mine, results) in enumerate(jobs):
         others = late_edges if k == len(alone) else []
         outs = edge_update(
-            k, (stride, base, start), mine, results, tile_counts, sender_row, slot_row, order, gain, edges, others,
+            k, (stride, base, start), mine, results, sender_row, slot_row, order, gain, edges, others,
             nodes, halos, inner, outer, others_a, others_b,
         )
         order = tie(order, *outs)
@@ -497,9 +508,7 @@
     count = len(alone)
     final = [(count - 1, d) for d in distances]
     own_parts = [(k, 0) for k in range(len(jobs))]
-    (sums,) = collected(*chosen(own_parts), None)
-    for k in range(count - 1):
-        (sums,) = collected(*chosen([(k, d) for d in distances]), sums)
+    (sums,) = collected(*chosen(own_parts + [(k, d) for k in range(count - 1) for d in distances]), None)
     own, *pieces = collected(*chosen(final), sums, True)
     returned = [shifted(piece, ("dom", "rep"), -by) for piece, by in zip(pieces, offsets)]
     everything = chosen([(k, d) for k, outs in enumerate(parts) for d in range(len(outs))])

time: 77 us -> 75.5 us (0.981)
  Pallas kernels: 24 us -> 20.9 us
  waiting for transfers between devices: 27.1 us -> 29.2 us
    ppermute x15, waiting for transfers between devices: 22 us -> 24.1 us  [shifted(): lax.ppermute(block, axis, [(i, (i + distance) % size) for i in range(size)])]
    pallas_call x3 -> x2, Pallas kernels: 2.93 us -> 1.13 us  [collect(): pl.pallas_call(functools.partial(collect_kernel, ways, places, local_node...]
    pallas_call x3, Pallas kernels: 13.7 us -> 12.1 us  [edge_update(): pl.pallas_call(functools.partial(edge_kernel, ways, place, mine, bool(oth...]
  transfers between devices with their start and end apart: 22 -> 22, of which waited for: 11 -> 11; matrix products, arithmetic and copies ran while one was open for 0% -> 0% of each run, Pallas kernels for 29% -> 26%
where the time goes in v5:
time: 75.5 us; the launch traced here: 75.3 us
  waiting for transfers between devices  29.2 us (39%)
  starting transfers between devices  24.2 us (32%)
  Pallas kernels  20.9 us (28%)
  between operations  0.88 us (1%)
    ppermute x15, waiting for transfers between devices, shifted(): lax.ppermute(block, axis, [(i, (i + distance) % size) for i in range(size)])  24.1 us
    ppermute x15, starting transfers between devices, shifted(): lax.ppermute(block, axis, [(i, (i + distance) % size) for i in range(size)])  21.1 us
    pallas_call x3, Pallas kernels, edge_update(): pl.pallas_call(functools.partial(edge_kernel, ways, place, mine, bool(oth...  12.1 us
    ppermute x7, waiting for transfers between devices, swapped(): return lax.ppermute(block, axis, [(i, i ^ 1) for i in range(size)])  5.08 us
    ppermute x7, starting transfers between devices, swapped(): return lax.ppermute(block, axis, [(i, i ^ 1) for i in range(size)])  3.11 us
    pallas_call x1, Pallas kernels, prepare_second(): pl.pallas_call(functools.partial(second_kernel, ways, axes), out_shape=sh...  1.86 us
    pallas_call x1, Pallas kernels, prepare_first(): pl.pallas_call(functools.partial(first_kernel, axes), out_shape=shape(2,...  1.68 us
  transfers between devices with their start and end apart: 22, of which 11 were waited for; matrix products, arithmetic and copies ran while one was open for 0% of the time, Pallas kernels for 26%

profile of v5, /device:TPU:0, one launch (start us, length us, event | category | flops | bytes accessed | tf_op | source)
XLA Modules:
  0.0 75.3 jit_solution(1249944094478515277)
XLA Ops:
  0.6 3.0 %collective-permute-start.1 = (bf16[256,512]{1,0:T(8,128)(2,1)}, bf16[256,512]{1,0:T(8,128)(2,1)S(1)}, u32[]{:S(2)}, u32[]{:S(2)}) collective-permute-start(bf16[256,512]{1,0:T(8,128)(2,1)} %refs_4_.1), channel_id=1, source_target_pairs={{0,2},{2,0},{1,3},{3,1},{4,6},{6,4},{5,7},{7,5},{8,10},{10,8},{9,1... | collective-permute-start | bytes 786440 | tf_op jit(solution)/shard_map/ppermute | solution.py:35
  3.6 1.7 %prepare_first.1 = bf16[2,64,1024]{2,1,0:T(8,128)(2,1)} custom-call(bf16[3,512,1024]{2,1,0:T(8,128)(2,1)} %w_in.4), custom_call_target="tpu_custom_call" | custom-call | tf_op jit(solution)/shard_map/prepare_first/pallas_call | solution.py:94
  5.3 0.0 copy-start.3
  5.3 0.0 copy-start.5
  5.3 0.1 collective-permute-start.6
  5.5 1.9 %prepare_second.1 = bf16[2,128,1024]{2,1,0:T(8,128)(2,1)} custom-call(bf16[3,512,1024]{2,1,0:T(8,128)(2,1)} %w_in.4, bf16[1024,512]{1,0:T(8,128)(2,1)} %w_out.3), custom_call_target="tpu_custom_call" | custom-call | tf_op jit(solution)/shard_map/prepare_second/pallas_call | solution.py:118
  7.3 0.0 copy-start.7
  7.3 0.0 copy-start.8
  7.3 0.0 copy-start.6
  7.4 0.0 copy-start.1
  7.4 0.0 copy-start.4
  7.4 2.1 %collective-permute-start.11 = (bf16[2,128,1024]{2,1,0:T(8,128)(2,1)}, bf16[2,128,1024]{2,1,0:T(8,128)(2,1)S(1)}, u32[]{:S(2)}, u32[]{:S(2)}) collective-permute-start(bf16[2,128,1024]{2,1,0:T(8,128)(2,1)} %prepare_second.1), channel_id=1, source_target_pairs={{0,2},{2,0},{1,3},{3,1},{4,6},{6,4},{5,7},{7,5},{8,10},{10,8},{9,1... | collective-permute-start | bytes 1572872 | tf_op jit(solution)/shard_map/ppermute | solution.py:35
  9.4 1.5 %collective-permute-done.1.refs_1_.refs_4_.refs_5_ = bf16[256,512]{1,0:T(8,128)(2,1)S(1)} collective-permute-done((bf16[256,512]{1,0:T(8,128)(2,1)}, bf16[256,512]{1,0:T(8,128)(2,1)S(1)}, u32[]{:S(2)}, u32[]{:S(2)}) %collective-permute-start.1) | collective-permute-done | bytes 262176 | tf_op jit(solution)/shard_map/ppermute | solution.py:35
  11.0 0.5 halo_gather.1
  11.5 0.0 copy-start.2
  11.5 4.2 %collective-permute-start.2 = (bf16[64,1024]{1,0:T(8,128)(2,1)S(1)}, bf16[64,1024]{1,0:T(8,128)(2,1)S(1)}, u32[]{:S(2)}, u32[]{:S(2)}) collective-permute-start(bf16[64,1024]{1,0:T(8,128)(2,1)S(1)} %get-tuple-element.31), channel_id=1, source_target_pairs={{0,12},{1,13},{4,0},{5,1},{8,4},{9,5},{12,8},{13,9},{2,14},{3,15},... | collective-permute-start | bytes 393224 | tf_op jit(solution)/shard_map/ppermute | solution.py:35
  15.7 0.0 collective-permute-start.3
  15.7 0.5 collective-permute-start.4
  16.3 0.6 mask_slots.1.slot_ref
  16.9 0.1 prepare_blocks.1
  17.0 0.0 collective-permute-done.6.first
  17.1 1.6 %collective-permute-start = (bf16[784,512]{1,0:T(8,128)(2,1)S(1)}, bf16[784,512]{1,0:T(8,128)(2,1)S(1)}, u32[]{:S(2)}, u32[]{:S(2)}) collective-permute-start(bf16[784,512]{1,0:T(8,128)(2,1)S(1)} %get-tuple-element.30), channel_id=1, source_target_pairs={{0,2},{2,0},{1,3},{3,1},{4,6},{6,4},{5,7},{7,5},{8,10},{10,8},{9,1... | collective-permute-start | bytes 2408456 | tf_op jit(solution)/shard_map/ppermute | solution.py:35
  18.7 0.8 %collective-permute-done.2.refs_5_.refs_6_ = bf16[64,1024]{1,0:T(8,128)(2,1)S(1)} collective-permute-done((bf16[64,1024]{1,0:T(8,128)(2,1)S(1)}, bf16[64,1024]{1,0:T(8,128)(2,1)S(1)}, u32[]{:S(2)}, u32[]{:S(2)}) %collective-permute-start.2) | collective-permute-done | bytes 131104 | tf_op jit(solution)/shard_map/ppermute | solution.py:35
  19.5 1.4 %collective-permute-done.3.refs_6_.refs_7_ = bf16[64,1024]{1,0:T(8,128)(2,1)S(1)} collective-permute-done((bf16[64,1024]{1,0:T(8,128)(2,1)S(1)}, bf16[64,1024]{1,0:T(8,128)(2,1)S(1)}, u32[]{:S(2)}, u32[]{:S(2)}) %collective-permute-start.3) | collective-permute-done | bytes 131104 | tf_op jit(solution)/shard_map/ppermute | solution.py:35
  20.9 1.1 %collective-permute-done.4.refs_7_.refs_8_ = bf16[64,1024]{1,0:T(8,128)(2,1)S(1)} collective-permute-done((bf16[64,1024]{1,0:T(8,128)(2,1)S(1)}, bf16[64,1024]{1,0:T(8,128)(2,1)S(1)}, u32[]{:S(2)}, u32[]{:S(2)}) %collective-permute-start.4) | collective-permute-done | bytes 131104 | tf_op jit(solution)/shard_map/ppermute | solution.py:35
  21.9 1.5 %collective-permute-start.7 = (bf16[2,64,1024]{2,1,0:T(8,128)(2,1)S(1)}, bf16[2,64,1024]{2,1,0:T(8,128)(2,1)S(1)}, u32[]{:S(2)}, u32[]{:S(2)}) collective-permute-start(bf16[2,64,1024]{2,1,0:T(8,128)(2,1)S(1)} %collective-permute-done.6.first), channel_id=1, source_target_pairs={{0,16},{16,0},{1,17},{17,1},{2,18},{18,2},{3,19},{19,3},{4,20},{20... | collective-permute-start | bytes 786440 | tf_op jit(solution)/shard_map/ppermute | solution.py:40
  23.5 0.0 collective-permute-start.5
  23.5 4.8 %collective-permute-done.7.second = bf16[2,64,1024]{2,1,0:T(8,128)(2,1)S(1)} collective-permute-done((bf16[2,64,1024]{2,1,0:T(8,128)(2,1)S(1)}, bf16[2,64,1024]{2,1,0:T(8,128)(2,1)S(1)}, u32[]{:S(2)}, u32[]{:S(2)}) %collective-permute-start.7) | collective-permute-done | bytes 262176 | tf_op jit(solution)/shard_map/ppermute | solution.py:40
  28.4 1.9 %collective-permute-done.5.refs_8_.refs_9_ = bf16[64,1024]{1,0:T(8,128)(2,1)S(1)} collective-permute-done((bf16[64,1024]{1,0:T(8,128)(2,1)S(1)}, bf16[64,1024]{1,0:T(8,128)(2,1)S(1)}, u32[]{:S(2)}, u32[]{:S(2)}) %collective-permute-start.5) | collective-permute-done | bytes 131104 | tf_op jit(solution)/shard_map/ppermute | solution.py:35
  30.2 0.0 collective-permute-start.8
  30.2 0.0 collective-permute-done.11.refs_0_
  30.2 0.5 collective-permute-start.12
  30.8 0.3 stage.1
  31.1 0.1 collective-permute-start.9
  31.1 0.5 collective-permute-start.13
  31.6 12.6 %collective-permute-done.refs_2_ = bf16[784,512]{1,0:T(8,128)(2,1)S(1)} collective-permute-done((bf16[784,512]{1,0:T(8,128)(2,1)S(1)}, bf16[784,512]{1,0:T(8,128)(2,1)S(1)}, u32[]{:S(2)}, u32[]{:S(2)}) %collective-permute-start) | collective-permute-done | bytes 802848 | tf_op jit(solution)/shard_map/ppermute | solution.py:35
  44.2 0.0 collective-permute-done.8.refs_1_
  44.2 0.0 collective-permute-start.10
  44.2 0.0 collective-permute-done.12.refs_1_
  44.2 0.5 collective-permute-start.14
  44.7 1.7 %collective-permute-start.17 = (bf16[256,512]{1,0:T(8,128)(2,1)S(1)}, bf16[256,512]{1,0:T(8,128)(2,1)S(1)}, u32[]{:S(2)}, u32[]{:S(2)}) collective-permute-start(bf16[256,512]{1,0:T(8,128)(2,1)S(1)} %get-tuple-element.50), channel_id=1, source_target_pairs={{0,2},{2,0},{1,3},{3,1},{4,6},{6,4},{5,7},{7,5},{8,10},{10,8},{9,1... | collective-permute-start | bytes 786440 | tf_op jit(solution)/shard_map/ppermute | solution.py:35
  46.5 0.0 collective-permute-done.9.refs_2_
  46.5 0.0 collective-permute-done.10.refs_3_
  46.5 0.2 assemble.2.refs_11_.refs_12_
  46.6 0.0 collective-permute-done.13.refs_2_
  46.7 0.2 collective-permute-done.14.refs_3_
  46.9 0.2 assemble.3.refs_12_.refs_13_
  47.0 3.2 %edge_update_0.1 = (bf16[256,512]{1,0:T(8,128)(2,1)S(1)}, bf16[256,512]{1,0:T(8,128)(2,1)S(1)}) custom-call(s32[1,1536]{1,0:T(1,128)S(1)} %reshape.13.sender_ref, s32[1,1536]{1,0:T(1,128)S(1)} %mask_slots.1.slot_ref, bf16[1536,512]{1,0:T(8,128)(2,1)S(1)} %copy-done.1, f32[1,512]{1,0:T(1,128)S(1)} %bitcast.2, ...), custom_call_target="tpu_custom_call" | custom-call | flops 2550136832 | bytes 8388608 | tf_op jit(solution)/shard_map/edge_update_0/pallas_call | solution.py:351
  50.2 1.8 %collective-permute-start.15 = (bf16[256,512]{1,0:T(8,128)(2,1)S(1)}, bf16[256,512]{1,0:T(8,128)(2,1)S(1)}, u32[]{:S(2)}, u32[]{:S(2)}) collective-permute-start(bf16[256,512]{1,0:T(8,128)(2,1)S(1)} %get-tuple-element.44), channel_id=1, source_target_pairs={{0,2},{2,0},{1,3},{3,1},{4,6},{6,4},{5,7},{7,5},{8,10},{10,8},{9,1... | collective-permute-start | bytes 786440 | tf_op jit(solution)/shard_map/ppermute | solution.py:35
  52.0 3.1 %edge_update_1.1 = (bf16[256,512]{1,0:T(8,128)(2,1)S(1)}, bf16[256,512]{1,0:T(8,128)(2,1)S(1)}) custom-call(s32[1,1536]{1,0:T(1,128)S(1)} %reshape.13.sender_ref, s32[1,1536]{1,0:T(1,128)S(1)} %mask_slots.1.slot_ref, bf16[1536,512]{1,0:T(8,128)(2,1)S(1)} %copy-done.1, f32[1,512]{1,0:T(1,128)S(1)} %bitcast.3, ...), custom_call_target="tpu_custom_call" | custom-call | flops 2550136832 | bytes 8388608 | tf_op jit(solution)/shard_map/edge_update_1/pallas_call | solution.py:351
  55.2 0.4 collective-permute-start.16
  55.5 5.8 %edge_update_2.1.refs_4_.refs_2_ = bf16[512,512]{1,0:T(8,128)(2,1)S(1)} custom-call(s32[1,1536]{1,0:T(1,128)S(1)} %reshape.13.sender_ref, s32[1,1536]{1,0:T(1,128)S(1)} %mask_slots.1.slot_ref, bf16[1536,512]{1,0:T(8,128)(2,1)S(1)} %copy-done.1, f32[1,512]{1,0:T(1,128)S(1)} %bitcast.4, bf16[784,512]{1,0:T(8,128)(2,1)S(1)} %collective-permute-done.refs_2_, ...), custom_call_target="tpu_custom_call" | custom-call | flops 5100273664 | bytes 8388608 | tf_op jit(solution)/shard_map/edge_update_2/pallas_call | solution.py:351
  61.3 0.0 collective-permute-done.15.refs_1_.refs_3_
  61.3 0.8 %collect.2.refs_1_ = f32[512,512]{1,0:T(8,128)S(1)} custom-call(s32[1,1536]{1,0:T(1,128)S(1)} %mask_slots.1.slot_ref, bf16[256,512]{1,0:T(8,128)(2,1)S(1)} %get-tuple-element.43.refs_0_, bf16[256,512]{1,0:T(8,128)(2,1)S(1)} %get-tuple-element.46.refs_2_.refs_1_, bf16[512,512]{1,0:T(8,128)(2,1)S(1)} %edge_update_2.1.refs_4_.refs_2_, ...), custom_call_target="tpu_custom_call" | custom-call | tf_op jit(solution)/shard_map/collect/pallas_call | solution.py:399
  62.1 2.1 %collective-permute-done.16.refs_3_.refs_0_ = bf16[256,512]{1,0:T(8,128)(2,1)S(1)} collective-permute-done((bf16[256,512]{1,0:T(8,128)(2,1)S(1)}, bf16[256,512]{1,0:T(8,128)(2,1)S(1)}, u32[]{:S(2)}, u32[]{:S(2)}) %collective-permute-start.16) | collective-permute-done | bytes 262176 | tf_op jit(solution)/shard_map/ppermute | solution.py:35
  64.2 0.3 collect.3
  64.5 1.9 %collective-permute-start.18 = (bf16[64,512]{1,0:T(8,128)(2,1)S(1)}, bf16[64,512]{1,0:T(8,128)(2,1)S(1)}, u32[]{:S(2)}, u32[]{:S(2)}) collective-permute-start(bf16[64,512]{1,0:T(8,128)(2,1)S(1)} %get-tuple-element.52), channel_id=1, source_target_pairs={{0,4},{1,5},{4,8},{5,9},{8,12},{9,13},{12,0},{13,1},{2,6},{3,7},{6... | collective-permute-start | bytes 196616 | tf_op jit(solution)/shard_map/ppermute | solution.py:35
  66.4 3.5 %collective-permute-start.20 = (bf16[64,512]{1,0:T(8,128)(2,1)S(1)}, bf16[64,512]{1,0:T(8,128)(2,1)S(1)}, u32[]{:S(2)}, u32[]{:S(2)}) collective-permute-start(bf16[64,512]{1,0:T(8,128)(2,1)S(1)} %get-tuple-element.54), channel_id=1, source_target_pairs={{0,13},{1,0},{4,1},{5,4},{8,5},{9,8},{12,9},{13,12},{2,15},{3,2},{... | collective-permute-start | bytes 196616 | tf_op jit(solution)/shard_map/ppermute | solution.py:35
  70.0 0.3 collective-permute-start.21
  70.3 1.3 %write.1 = bf16[1536,512]{1,0:T(8,128)(2,1)} custom-call(bf16[256,512]{1,0:T(8,128)(2,1)S(1)} %get-tuple-element.43.refs_0_, bf16[256,512]{1,0:T(8,128)(2,1)S(1)} %collective-permute-done.15.refs_1_.refs_3_, bf16[256,512]{1,0:T(8,128)(2,1)S(1)} %get-tuple-element.46.refs_2_.refs_1_, bf16[256,512]{1,0:T(8,128)(2,1)S(1)} %collective-permute-done.16.refs_3_.refs_0_, ...), custom_call_target="tpu_custom_call" | custom-call | tf_op jit(solution)/shard_map/write/pallas_call | solution.py:418
  71.5 0.0 collective-permute-done.18.refs_0_
  71.5 0.6 collective-permute-done.19.refs_1_
  72.1 2.1 %collective-permute-done.21.refs_3_ = bf16[64,512]{1,0:T(8,128)(2,1)S(1)} collective-permute-done((bf16[64,512]{1,0:T(8,128)(2,1)S(1)}, bf16[64,512]{1,0:T(8,128)(2,1)S(1)}, u32[]{:S(2)}, u32[]{:S(2)}) %collective-permute-start.21) | collective-permute-done | bytes 65568 | tf_op jit(solution)/shard_map/ppermute | solution.py:35
  74.2 1.1 %finish.1 = f32[256,512]{1,0:T(8,128)} custom-call(s32[1,4,64]{2,1,0:T(4,128)S(1)} %copy-done.5, f32[256,512]{1,0:T(8,128)S(1)} %get-tuple-element.51.own, bf16[64,512]{1,0:T(8,128)(2,1)S(1)} %collective-permute-done.18.refs_0_, bf16[64,512]{1,0:T(8,128)(2,1)S(1)} %collective-permute-done.19.refs_1_, bf16[64,512]{1,0:T(8,128)(2,1)S(1)} %collective-permute-done.20.refs_2_, ...), custom_call_target="tpu_custom_call" | custom-call | tf_op jit(solution)/shard_map/finish/pallas_call | solution.py:437
  (16 shorter events, 0.1 us)
Async XLA Ops:
  0.6 10.4 %collective-permute-start.1 = (bf16[256,512]{1,0:T(8,128)(2,1)}, bf16[256,512]{1,0:T(8,128)(2,1)S(1)}, u32[]{:S(2)}, u32[]{:S(2)}) collective-permute-start(bf16[256,512]{1,0:T(8,128)(2,1)} %refs_4_.1), channel_id=1, source_target_pairs={{0,2},{2,0},{1,3},{3,1},{4,6},{6,4},{5,7},{7,5},{8,10},{10,8},{9,1... | collective-permute-start | bytes 786440 | tf_op jit(solution)/shard_map/ppermute | solution.py:35
  5.3 5.7 %copy-start.3 = (bf16[256,512]{1,0:T(8,128)(2,1)S(1)}, bf16[256,512]{1,0:T(8,128)(2,1)}, u32[]{:S(2)}) copy-start(bf16[256,512]{1,0:T(8,128)(2,1)} %refs_4_.1) | copy-start | bytes 786436
  5.3 5.6 %copy-start.5 = (s32[1,4,64]{2,1,0:T(4,128)S(1)}, s32[1,4,64]{2,1,0:T(4,128)}, u32[]{:S(2)}) copy-start(s32[1,4,64]{2,1,0:T(4,128)} %rows_ref.3) | copy-start | bytes 3076
  5.3 11.7 %collective-permute-start.6 = (bf16[2,64,1024]{2,1,0:T(8,128)(2,1)}, bf16[2,64,1024]{2,1,0:T(8,128)(2,1)S(1)}, u32[]{:S(2)}, u32[]{:S(2)}) collective-permute-start(bf16[2,64,1024]{2,1,0:T(8,128)(2,1)} %prepare_first.1), channel_id=1, source_target_pairs={{0,2},{2,0},{1,3},{3,1},{4,6},{6,4},{5,7},{7,5},{8,10},{10,8},{9,1... | collective-permute-start | bytes 786440 | tf_op jit(solution)/shard_map/ppermute | solution.py:35
  7.3 8.9 %copy-start.7 = (s32[1536]{0:T(1024)S(1)}, s32[1536]{0:T(1024)}, u32[]{:S(2)}) copy-start(s32[1536]{0:T(1024)} %param.11) | copy-start | bytes 18436
  7.3 8.9 %copy-start.8 = (s32[1536]{0:T(1024)S(1)}, s32[1536]{0:T(1024)}, u32[]{:S(2)}) copy-start(s32[1536]{0:T(1024)} %param.12) | copy-start | bytes 18436
  7.3 8.9 %copy-start.6 = (s32[8]{0:T(128)S(1)}, s32[8]{0:T(128)}, u32[]{:S(2)}) copy-start(s32[8]{0:T(128)} %counts.1) | copy-start | bytes 100
  7.4 9.5 %copy-start.1 = (bf16[1536,512]{1,0:T(8,128)(2,1)S(1)}, bf16[1536,512]{1,0:T(8,128)(2,1)}, u32[]{:S(2)}) copy-start(bf16[1536,512]{1,0:T(8,128)(2,1)} %refs_0_.5) | copy-start | bytes 4718596
  7.4 9.5 %copy-start.4 = (f32[512]{0:T(512)S(1)}, f32[512]{0:T(512)}, u32[]{:S(2)}) copy-start(f32[512]{0:T(512)} %param.17) | copy-start | bytes 6148
  7.4 22.9 %collective-permute-start.11 = (bf16[2,128,1024]{2,1,0:T(8,128)(2,1)}, bf16[2,128,1024]{2,1,0:T(8,128)(2,1)S(1)}, u32[]{:S(2)}, u32[]{:S(2)}) collective-permute-start(bf16[2,128,1024]{2,1,0:T(8,128)(2,1)} %prepare_second.1), channel_id=1, source_target_pairs={{0,2},{2,0},{1,3},{3,1},{4,6},{6,4},{5,7},{7,5},{8,10},{10,8},{9,1... | collective-permute-start | bytes 1572872 | tf_op jit(solution)/shard_map/ppermute | solution.py:35
  11.0 19.8 %copy-start = (bf16[3,512,1024]{2,1,0:T(8,128)(2,1)S(1)}, bf16[3,512,1024]{2,1,0:T(8,128)(2,1)}, u32[]{:S(2)}) copy-start(bf16[3,512,1024]{2,1,0:T(8,128)(2,1)} %w_in.4) | copy-start | bytes 9437188
  11.5 19.2 %copy-start.2 = (bf16[1024,512]{1,0:T(8,128)(2,1)S(1)}, bf16[1024,512]{1,0:T(8,128)(2,1)}, u32[]{:S(2)}) copy-start(bf16[1024,512]{1,0:T(8,128)(2,1)} %w_out.3) | copy-start | bytes 3145732
  11.5 7.9 %collective-permute-start.2 = (bf16[64,1024]{1,0:T(8,128)(2,1)S(1)}, bf16[64,1024]{1,0:T(8,128)(2,1)S(1)}, u32[]{:S(2)}, u32[]{:S(2)}) collective-permute-start(bf16[64,1024]{1,0:T(8,128)(2,1)S(1)} %get-tuple-element.31), channel_id=1, source_target_pairs={{0,12},{1,13},{4,0},{5,1},{8,4},{9,5},{12,8},{13,9},{2,14},{3,15},... | collective-permute-start | bytes 393224 | tf_op jit(solution)/shard_map/ppermute | solution.py:35
  15.7 5.1 %collective-permute-start.3 = (bf16[64,1024]{1,0:T(8,128)(2,1)S(1)}, bf16[64,1024]{1,0:T(8,128)(2,1)S(1)}, u32[]{:S(2)}, u32[]{:S(2)}) collective-permute-start(bf16[64,1024]{1,0:T(8,128)(2,1)S(1)} %get-tuple-element.32), channel_id=1, source_target_pairs={{0,13},{1,0},{4,1},{5,4},{8,5},{9,8},{12,9},{13,12},{2,15},{3,2},{... | collective-permute-start | bytes 393224 | tf_op jit(solution)/shard_map/ppermute | solution.py:35
  15.7 6.2 %collective-permute-start.4 = (bf16[64,1024]{1,0:T(8,128)(2,1)S(1)}, bf16[64,1024]{1,0:T(8,128)(2,1)S(1)}, u32[]{:S(2)}, u32[]{:S(2)}) collective-permute-start(bf16[64,1024]{1,0:T(8,128)(2,1)S(1)} %get-tuple-element.33), channel_id=1, source_target_pairs={{0,1},{1,4},{4,5},{5,8},{8,9},{9,12},{12,13},{13,0},{2,3},{3,6},{6... | collective-permute-start | bytes 393224 | tf_op jit(solution)/shard_map/ppermute | solution.py:35
  17.1 27.2 %collective-permute-start = (bf16[784,512]{1,0:T(8,128)(2,1)S(1)}, bf16[784,512]{1,0:T(8,128)(2,1)S(1)}, u32[]{:S(2)}, u32[]{:S(2)}) collective-permute-start(bf16[784,512]{1,0:T(8,128)(2,1)S(1)} %get-tuple-element.30), channel_id=1, source_target_pairs={{0,2},{2,0},{1,3},{3,1},{4,6},{6,4},{5,7},{7,5},{8,10},{10,8},{9,1... | collective-permute-start | bytes 2408456 | tf_op jit(solution)/shard_map/ppermute | solution.py:35
  21.9 6.4 %collective-permute-start.7 = (bf16[2,64,1024]{2,1,0:T(8,128)(2,1)S(1)}, bf16[2,64,1024]{2,1,0:T(8,128)(2,1)S(1)}, u32[]{:S(2)}, u32[]{:S(2)}) collective-permute-start(bf16[2,64,1024]{2,1,0:T(8,128)(2,1)S(1)} %collective-permute-done.6.first), channel_id=1, source_target_pairs={{0,16},{16,0},{1,17},{17,1},{2,18},{18,2},{3,19},{19,3},{4,20},{20... | collective-permute-start | bytes 786440 | tf_op jit(solution)/shard_map/ppermute | solution.py:40
  23.5 6.8 %collective-permute-start.5 = (bf16[64,1024]{1,0:T(8,128)(2,1)S(1)}, bf16[64,1024]{1,0:T(8,128)(2,1)S(1)}, u32[]{:S(2)}, u32[]{:S(2)}) collective-permute-start(bf16[64,1024]{1,0:T(8,128)(2,1)S(1)} %get-tuple-element.34), channel_id=1, source_target_pairs={{0,4},{1,5},{4,8},{5,9},{8,12},{9,13},{12,0},{13,1},{2,6},{3,7},{6... | collective-permute-start | bytes 393224 | tf_op jit(solution)/shard_map/ppermute | solution.py:35
  30.2 14.0 %collective-permute-start.8 = (bf16[2,128,1024]{2,1,0:T(8,128)(2,1)S(1)}, bf16[2,128,1024]{2,1,0:T(8,128)(2,1)S(1)}, u32[]{:S(2)}, u32[]{:S(2)}) collective-permute-start(bf16[2,128,1024]{2,1,0:T(8,128)(2,1)S(1)} %join.1.refs_0_), channel_id=1, source_target_pairs={{0,4},{4,0},{8,12},{12,8},{1,5},{5,1},{9,13},{13,9},{2,6},{6,2},{1... | collective-permute-start | bytes 1572872 | tf_op jit(solution)/shard_map/ppermute | solution.py:40
  30.2 14.0 %collective-permute-start.12 = (bf16[2,128,1024]{2,1,0:T(8,128)(2,1)S(1)}, bf16[2,128,1024]{2,1,0:T(8,128)(2,1)S(1)}, u32[]{:S(2)}, u32[]{:S(2)}) collective-permute-start(bf16[2,128,1024]{2,1,0:T(8,128)(2,1)S(1)} %collective-permute-done.11.refs_0_), channel_id=1, source_target_pairs={{0,16},{16,0},{1,17},{17,1},{2,18},{18,2},{3,19},{19,3},{4,20},{20... | collective-permute-start | bytes 1572872 | tf_op jit(solution)/shard_map/ppermute | solution.py:40
  31.1 15.4 %collective-permute-start.9 = (bf16[2,128,1024]{2,1,0:T(8,128)(2,1)S(1)}, bf16[2,128,1024]{2,1,0:T(8,128)(2,1)S(1)}, u32[]{:S(2)}, u32[]{:S(2)}) collective-permute-start(bf16[2,128,1024]{2,1,0:T(8,128)(2,1)S(1)} %join.1.refs_0_), channel_id=1, source_target_pairs={{0,1},{1,0},{2,3},{3,2},{4,5},{5,4},{6,7},{7,6},{8,9},{9,8},{10,11... | collective-permute-start | bytes 1572872 | tf_op jit(solution)/shard_map/ppermute | solution.py:40
  31.1 15.5 %collective-permute-start.13 = (bf16[2,128,1024]{2,1,0:T(8,128)(2,1)S(1)}, bf16[2,128,1024]{2,1,0:T(8,128)(2,1)S(1)}, u32[]{:S(2)}, u32[]{:S(2)}) collective-permute-start(bf16[2,128,1024]{2,1,0:T(8,128)(2,1)S(1)} %collective-permute-done.11.refs_0_), channel_id=1, source_target_pairs={{0,1},{1,0},{2,3},{3,2},{4,5},{5,4},{6,7},{7,6},{8,9},{9,8},{10,11... | collective-permute-start | bytes 1572872 | tf_op jit(solution)/shard_map/ppermute | solution.py:40
  44.2 2.3 %collective-permute-start.10 = (bf16[2,128,1024]{2,1,0:T(8,128)(2,1)S(1)}, bf16[2,128,1024]{2,1,0:T(8,128)(2,1)S(1)}, u32[]{:S(2)}, u32[]{:S(2)}) collective-permute-start(bf16[2,128,1024]{2,1,0:T(8,128)(2,1)S(1)} %collective-permute-done.8.refs_1_), channel_id=1, source_target_pairs={{0,1},{1,0},{2,3},{3,2},{4,5},{5,4},{6,7},{7,6},{8,9},{9,8},{10,11... | collective-permute-start | bytes 1572872 | tf_op jit(solution)/shard_map/ppermute | solution.py:40
  44.2 2.7 %collective-permute-start.14 = (bf16[2,128,1024]{2,1,0:T(8,128)(2,1)S(1)}, bf16[2,128,1024]{2,1,0:T(8,128)(2,1)S(1)}, u32[]{:S(2)}, u32[]{:S(2)}) collective-permute-start(bf16[2,128,1024]{2,1,0:T(8,128)(2,1)S(1)} %collective-permute-done.12.refs_1_), channel_id=1, source_target_pairs={{0,1},{1,0},{2,3},{3,2},{4,5},{5,4},{6,7},{7,6},{8,9},{9,8},{10,11... | collective-permute-start | bytes 1572872 | tf_op jit(solution)/shard_map/ppermute | solution.py:40
  44.7 10.8 %collective-permute-start.17 = (bf16[256,512]{1,0:T(8,128)(2,1)S(1)}, bf16[256,512]{1,0:T(8,128)(2,1)S(1)}, u32[]{:S(2)}, u32[]{:S(2)}) collective-permute-start(bf16[256,512]{1,0:T(8,128)(2,1)S(1)} %get-tuple-element.50), channel_id=1, source_target_pairs={{0,2},{2,0},{1,3},{3,1},{4,6},{6,4},{5,7},{7,5},{8,10},{10,8},{9,1... | collective-permute-start | bytes 786440 | tf_op jit(solution)/shard_map/ppermute | solution.py:35
  50.2 11.1 %collective-permute-start.15 = (bf16[256,512]{1,0:T(8,128)(2,1)S(1)}, bf16[256,512]{1,0:T(8,128)(2,1)S(1)}, u32[]{:S(2)}, u32[]{:S(2)}) collective-permute-start(bf16[256,512]{1,0:T(8,128)(2,1)S(1)} %get-tuple-element.44), channel_id=1, source_target_pairs={{0,2},{2,0},{1,3},{3,1},{4,6},{6,4},{5,7},{7,5},{8,10},{10,8},{9,1... | collective-permute-start | bytes 786440 | tf_op jit(solution)/shard_map/ppermute | solution.py:35
  55.2 9.1 %collective-permute-start.16 = (bf16[256,512]{1,0:T(8,128)(2,1)S(1)}, bf16[256,512]{1,0:T(8,128)(2,1)S(1)}, u32[]{:S(2)}, u32[]{:S(2)}) collective-permute-start(bf16[256,512]{1,0:T(8,128)(2,1)S(1)} %get-tuple-element.47), channel_id=1, source_target_pairs={{0,2},{2,0},{1,3},{3,1},{4,6},{6,4},{5,7},{7,5},{8,10},{10,8},{9,1... | collective-permute-start | bytes 786440 | tf_op jit(solution)/shard_map/ppermute | solution.py:35
  64.5 7.0 %collective-permute-start.18 = (bf16[64,512]{1,0:T(8,128)(2,1)S(1)}, bf16[64,512]{1,0:T(8,128)(2,1)S(1)}, u32[]{:S(2)}, u32[]{:S(2)}) collective-permute-start(bf16[64,512]{1,0:T(8,128)(2,1)S(1)} %get-tuple-element.52), channel_id=1, source_target_pairs={{0,4},{1,5},{4,8},{5,9},{8,12},{9,13},{12,0},{13,1},{2,6},{3,7},{6... | collective-permute-start | bytes 196616 | tf_op jit(solution)/shard_map/ppermute | solution.py:35
  66.4 5.7 %collective-permute-start.19 = (bf16[64,512]{1,0:T(8,128)(2,1)S(1)}, bf16[64,512]{1,0:T(8,128)(2,1)S(1)}, u32[]{:S(2)}, u32[]{:S(2)}) collective-permute-start(bf16[64,512]{1,0:T(8,128)(2,1)S(1)} %get-tuple-element.53), channel_id=1, source_target_pairs={{0,1},{1,4},{4,5},{5,8},{8,9},{9,12},{12,13},{13,0},{2,3},{3,6},{6... | collective-permute-start | bytes 196616 | tf_op jit(solution)/shard_map/ppermute | solution.py:35
  66.4 5.7 %collective-permute-start.20 = (bf16[64,512]{1,0:T(8,128)(2,1)S(1)}, bf16[64,512]{1,0:T(8,128)(2,1)S(1)}, u32[]{:S(2)}, u32[]{:S(2)}) collective-permute-start(bf16[64,512]{1,0:T(8,128)(2,1)S(1)} %get-tuple-element.54), channel_id=1, source_target_pairs={{0,13},{1,0},{4,1},{5,4},{8,5},{9,8},{12,9},{13,12},{2,15},{3,2},{... | collective-permute-start | bytes 196616 | tf_op jit(solution)/shard_map/ppermute | solution.py:35
  70.0 4.3 %collective-permute-start.21 = (bf16[64,512]{1,0:T(8,128)(2,1)S(1)}, bf16[64,512]{1,0:T(8,128)(2,1)S(1)}, u32[]{:S(2)}, u32[]{:S(2)}) collective-permute-start(bf16[64,512]{1,0:T(8,128)(2,1)S(1)} %get-tuple-element.55), channel_id=1, source_target_pairs={{0,12},{1,13},{4,0},{5,1},{8,4},{9,5},{12,8},{13,9},{2,14},{3,15},... | collective-permute-start | bytes 196616 | tf_op jit(solution)/shard_map/ppermute | solution.py:35

commit v6 on v5

--- a/solution.py
+++ b/solution.py
@@ -231,8 +231,7 @@
     return pieces
 
 
-def assemble_kernel(axes, *refs):
-    pieces, out = refs[:-1], refs[-1]
+def assemble_part(axes, pieces, out):
     share = share_index(axes)
     each = (1 << len(axes)) // len(pieces)
     rows = pieces[0].shape[1] // each
@@ -243,14 +242,21 @@
             out[part, pl.ds(start, rows), :] = pieces[m // each][part, place : place + rows, :]
 
 
-def assemble(pieces, axes):
-    parts, rows, channels = pieces[0].shape
-    return pl.pallas_call(
-        functools.partial(assemble_kernel, axes),
-        out_shape=shape(parts, rows * len(pieces), channels),
+def assemble_kernel(groups, *refs):
+    sources, outs = refs[: -len(groups)], refs[-len(groups) :]
+    for (axes, count), out in zip(groups, outs):
+        assemble_part(axes, sources[:count], out)
+        sources = sources[count:]
+
+
+def assemble(groups):
+    parts, rows, channels = groups[0][0][0].shape
+    return pl.pallas_call(
+        functools.partial(assemble_kernel, [(axes, len(pieces)) for pieces, axes in groups]),
+        out_shape=[shape(pieces[0].shape[0], pieces[0].shape[1] * len(pieces), channels) for pieces, _ in groups],
         compiler_params=params(),
         name="assemble",
-    )(*pieces)
+    )(*[piece for pieces, _ in groups for piece in pieces])
 
 
 def stage_kernel(w_in, w_out, inner, outer, sems):
@@ -480,9 +486,11 @@
     pieces = [join(piece, swapped(piece, axes_a[0])) for piece in pieces]
     pieces = [tie(piece, *halos[3:]) for piece in pieces]
     crossed_b = [tie(piece, *pieces) for piece in crossed_b]
-    others_a = [assemble(gather_shares(piece, axes_a[1:], edges), axes_a) for piece in pieces]
+    groups_a = [(gather_shares(piece, axes_a[1:], []), axes_a) for piece in pieces]
     inner, outer = stage(tie(weight_in, *outgoing), weight_out)
-    others_b = [assemble(gather_shares(piece, axes_b, [inner, outer]), axes_b) for piece in crossed_b]
+    groups_b = [(gather_shares(piece, axes_b, [inner, outer, *edges]), axes_b) for piece in crossed_b]
+    others = assemble(groups_a + groups_b)
+    others_a, others_b = others[: len(groups_a)], others[len(groups_a) :]
 
     def collected(places, parts, sums, last=False):
         return collect(places, parts, sums, slot_row, ways, local_nodes, halo_size, last)
@@ -492,9 +500,9 @@
         jobs.append((0, ways * split, split, early + late, 1))
     parts, places, order = [], [], edge_feats
     for k, (stride, base, start, mine, results) in enumerate(jobs):
-        others = late_edges if k == len(alone) else []
+        late_rows = late_edges if k == len(alone) else []
         outs = edge_update(
-            k, (stride, base, start), mine, results, sender_row, slot_row, order, gain, edges, others,
+            k, (stride, base, start), mine, results, sender_row, slot_row, order, gain, edges, late_rows,
             nodes, halos, inner, outer, others_a, others_b,
         )
         order = tie(order, *outs)

time: 75.5 us -> 75.4 us (level)
    ppermute x7, waiting for transfers between devices: 5.08 us -> 15.7 us  [swapped(): return lax.ppermute(block, axis, [(i, i ^ 1) for i in range(size)])]
    ppermute x15, waiting for transfers between devices: 24.1 us -> 13.9 us  [shifted(): lax.ppermute(block, axis, [(i, (i + distance) % size) for i in range(size)])]
  transfers between devices with their start and end apart: 22 -> 22, of which waited for: 11 -> 12; matrix products, arithmetic and copies ran while one was open for 0% -> 0% of each run, Pallas kernels for 26% -> 26%
where the time goes in v6:
time: 75.4 us; the launch traced here: 75.2 us
  waiting for transfers between devices  29.6 us (39%)
  starting transfers between devices  23.7 us (31%)
  Pallas kernels  20.9 us (28%)
  between operations  0.87 us (1%)
    ppermute x15, starting transfers between devices, shifted(): lax.ppermute(block, axis, [(i, (i + distance) % size) for i in range(size)])  21.1 us
    ppermute x7, waiting for transfers between devices, swapped(): return lax.ppermute(block, axis, [(i, i ^ 1) for i in range(size)])  15.7 us
    ppermute x15, waiting for transfers between devices, shifted(): lax.ppermute(block, axis, [(i, (i + distance) % size) for i in range(size)])  13.9 us
    pallas_call x3, Pallas kernels, edge_update(): pl.pallas_call(functools.partial(edge_kernel, ways, place, mine, bool(oth...  12.1 us
    ppermute x7, starting transfers between devices, swapped(): return lax.ppermute(block, axis, [(i, i ^ 1) for i in range(size)])  2.6 us
    pallas_call x1, Pallas kernels, prepare_second(): pl.pallas_call(functools.partial(second_kernel, ways, axes), out_shape=sh...  1.86 us
    pallas_call x1, Pallas kernels, prepare_first(): pl.pallas_call(functools.partial(first_kernel, axes), out_shape=shape(2,...  1.68 us
  transfers between devices with their start and end apart: 22, of which 12 were waited for; matrix products, arithmetic and copies ran while one was open for 0% of the time, Pallas kernels for 26%

profile of v6, /device:TPU:0, one launch (start us, length us, event | category | flops | bytes accessed | tf_op | source)
XLA Modules:
  0.0 75.2 jit_solution(7483725875784604425)
XLA Ops:
  0.6 3.0 %collective-permute-start.1 = (bf16[256,512]{1,0:T(8,128)(2,1)}, bf16[256,512]{1,0:T(8,128)(2,1)S(1)}, u32[]{:S(2)}, u32[]{:S(2)}) collective-permute-start(bf16[256,512]{1,0:T(8,128)(2,1)} %refs_4_.1), channel_id=1, source_target_pairs={{0,2},{2,0},{1,3},{3,1},{4,6},{6,4},{5,7},{7,5},{8,10},{10,8},{9,1... | collective-permute-start | bytes 786440 | tf_op jit(solution)/shard_map/ppermute | solution.py:35
  3.6 1.7 %prepare_first.1 = bf16[2,64,1024]{2,1,0:T(8,128)(2,1)} custom-call(bf16[3,512,1024]{2,1,0:T(8,128)(2,1)} %w_in.4), custom_call_target="tpu_custom_call" | custom-call | tf_op jit(solution)/shard_map/prepare_first/pallas_call | solution.py:94
  5.3 0.0 copy-start.3
  5.3 0.0 copy-start.5
  5.3 0.1 collective-permute-start.6
  5.5 1.9 %prepare_second.1 = bf16[2,128,1024]{2,1,0:T(8,128)(2,1)} custom-call(bf16[3,512,1024]{2,1,0:T(8,128)(2,1)} %w_in.4, bf16[1024,512]{1,0:T(8,128)(2,1)} %w_out.3), custom_call_target="tpu_custom_call" | custom-call | tf_op jit(solution)/shard_map/prepare_second/pallas_call | solution.py:118
  7.3 0.0 copy-start.7
  7.3 0.0 copy-start.8
  7.3 0.0 copy-start.6
  7.4 0.0 copy-start.1
  7.4 0.0 copy-start.4
  7.4 2.1 %collective-permute-start.11 = (bf16[2,128,1024]{2,1,0:T(8,128)(2,1)}, bf16[2,128,1024]{2,1,0:T(8,128)(2,1)S(1)}, u32[]{:S(2)}, u32[]{:S(2)}) collective-permute-start(bf16[2,128,1024]{2,1,0:T(8,128)(2,1)} %prepare_second.1), channel_id=1, source_target_pairs={{0,2},{2,0},{1,3},{3,1},{4,6},{6,4},{5,7},{7,5},{8,10},{10,8},{9,1... | collective-permute-start | bytes 1572872 | tf_op jit(solution)/shard_map/ppermute | solution.py:35
  9.4 1.5 %collective-permute-done.1.refs_1_.refs_4_.refs_5_ = bf16[256,512]{1,0:T(8,128)(2,1)S(1)} collective-permute-done((bf16[256,512]{1,0:T(8,128)(2,1)}, bf16[256,512]{1,0:T(8,128)(2,1)S(1)}, u32[]{:S(2)}, u32[]{:S(2)}) %collective-permute-start.1) | collective-permute-done | bytes 262176 | tf_op jit(solution)/shard_map/ppermute | solution.py:35
  11.0 0.5 halo_gather.1
  11.5 0.0 copy-start.2
  11.5 4.2 %collective-permute-start.2 = (bf16[64,1024]{1,0:T(8,128)(2,1)S(1)}, bf16[64,1024]{1,0:T(8,128)(2,1)S(1)}, u32[]{:S(2)}, u32[]{:S(2)}) collective-permute-start(bf16[64,1024]{1,0:T(8,128)(2,1)S(1)} %get-tuple-element.32), channel_id=1, source_target_pairs={{0,12},{1,13},{4,0},{5,1},{8,4},{9,5},{12,8},{13,9},{2,14},{3,15},... | collective-permute-start | bytes 393224 | tf_op jit(solution)/shard_map/ppermute | solution.py:35
  15.7 0.0 collective-permute-start.3
  15.7 0.5 collective-permute-start.4
  16.3 0.6 mask_slots.1.slot_ref
  16.9 0.1 prepare_blocks.1
  17.0 0.0 collective-permute-done.6.first
  17.1 1.6 %collective-permute-start = (bf16[784,512]{1,0:T(8,128)(2,1)S(1)}, bf16[784,512]{1,0:T(8,128)(2,1)S(1)}, u32[]{:S(2)}, u32[]{:S(2)}) collective-permute-start(bf16[784,512]{1,0:T(8,128)(2,1)S(1)} %get-tuple-element.31), channel_id=1, source_target_pairs={{0,2},{2,0},{1,3},{3,1},{4,6},{6,4},{5,7},{7,5},{8,10},{10,8},{9,1... | collective-permute-start | bytes 2408456 | tf_op jit(solution)/shard_map/ppermute | solution.py:35
  18.7 0.8 %collective-permute-done.2.refs_5_.refs_6_ = bf16[64,1024]{1,0:T(8,128)(2,1)S(1)} collective-permute-done((bf16[64,1024]{1,0:T(8,128)(2,1)S(1)}, bf16[64,1024]{1,0:T(8,128)(2,1)S(1)}, u32[]{:S(2)}, u32[]{:S(2)}) %collective-permute-start.2) | collective-permute-done | bytes 131104 | tf_op jit(solution)/shard_map/ppermute | solution.py:35
  19.5 1.4 %collective-permute-done.3.refs_6_.refs_7_ = bf16[64,1024]{1,0:T(8,128)(2,1)S(1)} collective-permute-done((bf16[64,1024]{1,0:T(8,128)(2,1)S(1)}, bf16[64,1024]{1,0:T(8,128)(2,1)S(1)}, u32[]{:S(2)}, u32[]{:S(2)}) %collective-permute-start.3) | collective-permute-done | bytes 131104 | tf_op jit(solution)/shard_map/ppermute | solution.py:35
  20.9 1.1 %collective-permute-done.4.refs_7_.refs_8_ = bf16[64,1024]{1,0:T(8,128)(2,1)S(1)} collective-permute-done((bf16[64,1024]{1,0:T(8,128)(2,1)S(1)}, bf16[64,1024]{1,0:T(8,128)(2,1)S(1)}, u32[]{:S(2)}, u32[]{:S(2)}) %collective-permute-start.4) | collective-permute-done | bytes 131104 | tf_op jit(solution)/shard_map/ppermute | solution.py:35
  21.9 1.5 %collective-permute-start.7 = (bf16[2,64,1024]{2,1,0:T(8,128)(2,1)S(1)}, bf16[2,64,1024]{2,1,0:T(8,128)(2,1)S(1)}, u32[]{:S(2)}, u32[]{:S(2)}) collective-permute-start(bf16[2,64,1024]{2,1,0:T(8,128)(2,1)S(1)} %collective-permute-done.6.first), channel_id=1, source_target_pairs={{0,16},{16,0},{1,17},{17,1},{2,18},{18,2},{3,19},{19,3},{4,20},{20... | collective-permute-start | bytes 786440 | tf_op jit(solution)/shard_map/ppermute | solution.py:40
  23.5 0.0 collective-permute-start.5
  23.5 4.8 %collective-permute-done.7.second = bf16[2,64,1024]{2,1,0:T(8,128)(2,1)S(1)} collective-permute-done((bf16[2,64,1024]{2,1,0:T(8,128)(2,1)S(1)}, bf16[2,64,1024]{2,1,0:T(8,128)(2,1)S(1)}, u32[]{:S(2)}, u32[]{:S(2)}) %collective-permute-start.7) | collective-permute-done | bytes 262176 | tf_op jit(solution)/shard_map/ppermute | solution.py:40
  28.4 1.9 %collective-permute-done.5.refs_8_.refs_9_ = bf16[64,1024]{1,0:T(8,128)(2,1)S(1)} collective-permute-done((bf16[64,1024]{1,0:T(8,128)(2,1)S(1)}, bf16[64,1024]{1,0:T(8,128)(2,1)S(1)}, u32[]{:S(2)}, u32[]{:S(2)}) %collective-permute-start.5) | collective-permute-done | bytes 131104 | tf_op jit(solution)/shard_map/ppermute | solution.py:35
  30.2 0.0 collective-permute-start.8
  30.2 0.0 collective-permute-done.11.refs_4_
  30.2 0.5 collective-permute-start.12
  30.8 0.3 stage.1
  31.1 0.1 collective-permute-start.9
  31.1 0.5 collective-permute-start.13
  31.6 10.7 %collective-permute-done.8.refs_1_ = bf16[2,128,1024]{2,1,0:T(8,128)(2,1)S(1)} collective-permute-done((bf16[2,128,1024]{2,1,0:T(8,128)(2,1)S(1)}, bf16[2,128,1024]{2,1,0:T(8,128)(2,1)S(1)}, u32[]{:S(2)}, u32[]{:S(2)}) %collective-permute-start.8) | collective-permute-done | bytes 524320 | tf_op jit(solution)/shard_map/ppermute | solution.py:40
  42.4 0.0 collective-permute-start.10
  42.4 1.9 %collective-permute-done.refs_2_ = bf16[784,512]{1,0:T(8,128)(2,1)S(1)} collective-permute-done((bf16[784,512]{1,0:T(8,128)(2,1)S(1)}, bf16[784,512]{1,0:T(8,128)(2,1)S(1)}, u32[]{:S(2)}, u32[]{:S(2)}) %collective-permute-start) | collective-permute-done | bytes 802848 | tf_op jit(solution)/shard_map/ppermute | solution.py:35
  44.2 0.0 collective-permute-done.12.refs_5_
  44.2 0.0 collective-permute-start.14
  44.2 1.7 %collective-permute-start.17 = (bf16[256,512]{1,0:T(8,128)(2,1)S(1)}, bf16[256,512]{1,0:T(8,128)(2,1)S(1)}, u32[]{:S(2)}, u32[]{:S(2)}) collective-permute-start(bf16[256,512]{1,0:T(8,128)(2,1)S(1)} %get-tuple-element.52), channel_id=1, source_target_pairs={{0,2},{2,0},{1,3},{3,1},{4,6},{6,4},{5,7},{7,5},{8,10},{10,8},{9,1... | collective-permute-start | bytes 786440 | tf_op jit(solution)/shard_map/ppermute | solution.py:35
  46.0 0.0 collective-permute-done.9.refs_2_
  46.0 0.0 collective-permute-done.13.refs_6_
  46.0 0.0 collective-permute-done.10.refs_3_
  46.0 0.2 collective-permute-done.14.refs_7_
  46.1 0.3 assemble.1
  46.4 3.2 %edge_update_0.1 = (bf16[256,512]{1,0:T(8,128)(2,1)S(1)}, bf16[256,512]{1,0:T(8,128)(2,1)S(1)}) custom-call(s32[1,1536]{1,0:T(1,128)S(1)} %reshape.13.sender_ref, s32[1,1536]{1,0:T(1,128)S(1)} %mask_slots.1.slot_ref, bf16[1536,512]{1,0:T(8,128)(2,1)S(1)} %copy-done.1, f32[1,512]{1,0:T(1,128)S(1)} %bitcast.2, ...), custom_call_target="tpu_custom_call" | custom-call | flops 2550136832 | bytes 8388608 | tf_op jit(solution)/shard_map/edge_update_0/pallas_call | solution.py:357
  49.6 1.8 %collective-permute-start.15 = (bf16[256,512]{1,0:T(8,128)(2,1)S(1)}, bf16[256,512]{1,0:T(8,128)(2,1)S(1)}, u32[]{:S(2)}, u32[]{:S(2)}) collective-permute-start(bf16[256,512]{1,0:T(8,128)(2,1)S(1)} %get-tuple-element.46), channel_id=1, source_target_pairs={{0,2},{2,0},{1,3},{3,1},{4,6},{6,4},{5,7},{7,5},{8,10},{10,8},{9,1... | collective-permute-start | bytes 786440 | tf_op jit(solution)/shard_map/ppermute | solution.py:35
  51.4 3.1 %edge_update_1.1 = (bf16[256,512]{1,0:T(8,128)(2,1)S(1)}, bf16[256,512]{1,0:T(8,128)(2,1)S(1)}) custom-call(s32[1,1536]{1,0:T(1,128)S(1)} %reshape.13.sender_ref, s32[1,1536]{1,0:T(1,128)S(1)} %mask_slots.1.slot_ref, bf16[1536,512]{1,0:T(8,128)(2,1)S(1)} %copy-done.1, f32[1,512]{1,0:T(1,128)S(1)} %bitcast.3, ...), custom_call_target="tpu_custom_call" | custom-call | flops 2550136832 | bytes 8388608 | tf_op jit(solution)/shard_map/edge_update_1/pallas_call | solution.py:357
  54.6 0.3 collective-permute-start.16
  54.9 0.0 collective-permute-done.17.refs_3_
  54.9 5.8 %edge_update_2.1.refs_4_.refs_2_ = bf16[512,512]{1,0:T(8,128)(2,1)S(1)} custom-call(s32[1,1536]{1,0:T(1,128)S(1)} %reshape.13.sender_ref, s32[1,1536]{1,0:T(1,128)S(1)} %mask_slots.1.slot_ref, bf16[1536,512]{1,0:T(8,128)(2,1)S(1)} %copy-done.1, f32[1,512]{1,0:T(1,128)S(1)} %bitcast.4, bf16[784,512]{1,0:T(8,128)(2,1)S(1)} %collective-permute-done.refs_2_, ...), custom_call_target="tpu_custom_call" | custom-call | flops 5100273664 | bytes 8388608 | tf_op jit(solution)/shard_map/edge_update_2/pallas_call | solution.py:357
  60.7 0.0 collective-permute-done.15.refs_1_.refs_3_
  60.7 0.8 %collect.2.refs_1_ = f32[512,512]{1,0:T(8,128)S(1)} custom-call(s32[1,1536]{1,0:T(1,128)S(1)} %mask_slots.1.slot_ref, bf16[256,512]{1,0:T(8,128)(2,1)S(1)} %get-tuple-element.45.refs_0_, bf16[256,512]{1,0:T(8,128)(2,1)S(1)} %get-tuple-element.48.refs_2_.refs_1_, bf16[512,512]{1,0:T(8,128)(2,1)S(1)} %edge_update_2.1.refs_4_.refs_2_, ...), custom_call_target="tpu_custom_call" | custom-call | tf_op jit(solution)/shard_map/collect/pallas_call | solution.py:405
  61.5 2.6 %collective-permute-done.16.refs_3_.refs_0_ = bf16[256,512]{1,0:T(8,128)(2,1)S(1)} collective-permute-done((bf16[256,512]{1,0:T(8,128)(2,1)S(1)}, bf16[256,512]{1,0:T(8,128)(2,1)S(1)}, u32[]{:S(2)}, u32[]{:S(2)}) %collective-permute-start.16) | collective-permute-done | bytes 262176 | tf_op jit(solution)/shard_map/ppermute | solution.py:35
  64.2 0.3 collect.3
  64.5 1.9 %collective-permute-start.18 = (bf16[64,512]{1,0:T(8,128)(2,1)S(1)}, bf16[64,512]{1,0:T(8,128)(2,1)S(1)}, u32[]{:S(2)}, u32[]{:S(2)}) collective-permute-start(bf16[64,512]{1,0:T(8,128)(2,1)S(1)} %get-tuple-element.54), channel_id=1, source_target_pairs={{0,4},{1,5},{4,8},{5,9},{8,12},{9,13},{12,0},{13,1},{2,6},{3,7},{6... | collective-permute-start | bytes 196616 | tf_op jit(solution)/shard_map/ppermute | solution.py:35
  66.4 3.5 %collective-permute-start.20 = (bf16[64,512]{1,0:T(8,128)(2,1)S(1)}, bf16[64,512]{1,0:T(8,128)(2,1)S(1)}, u32[]{:S(2)}, u32[]{:S(2)}) collective-permute-start(bf16[64,512]{1,0:T(8,128)(2,1)S(1)} %get-tuple-element.56), channel_id=1, source_target_pairs={{0,13},{1,0},{4,1},{5,4},{8,5},{9,8},{12,9},{13,12},{2,15},{3,2},{... | collective-permute-start | bytes 196616 | tf_op jit(solution)/shard_map/ppermute | solution.py:35
  69.9 0.3 collective-permute-start.21
  70.2 1.3 %write.1 = bf16[1536,512]{1,0:T(8,128)(2,1)} custom-call(bf16[256,512]{1,0:T(8,128)(2,1)S(1)} %get-tuple-element.45.refs_0_, bf16[256,512]{1,0:T(8,128)(2,1)S(1)} %collective-permute-done.15.refs_1_.refs_3_, bf16[256,512]{1,0:T(8,128)(2,1)S(1)} %get-tuple-element.48.refs_2_.refs_1_, bf16[256,512]{1,0:T(8,128)(2,1)S(1)} %collective-permute-done.16.refs_3_.refs_0_, ...), custom_call_target="tpu_custom_call" | custom-call | tf_op jit(solution)/shard_map/write/pallas_call | solution.py:424
  71.5 0.0 collective-permute-done.18.refs_0_
  71.5 0.5 collective-permute-done.19.refs_1_
  72.0 2.2 %collective-permute-done.21.refs_3_ = bf16[64,512]{1,0:T(8,128)(2,1)S(1)} collective-permute-done((bf16[64,512]{1,0:T(8,128)(2,1)S(1)}, bf16[64,512]{1,0:T(8,128)(2,1)S(1)}, u32[]{:S(2)}, u32[]{:S(2)}) %collective-permute-start.21) | collective-permute-done | bytes 65568 | tf_op jit(solution)/shard_map/ppermute | solution.py:35
  74.2 1.1 %finish.1 = f32[256,512]{1,0:T(8,128)} custom-call(s32[1,4,64]{2,1,0:T(4,128)S(1)} %copy-done.5, f32[256,512]{1,0:T(8,128)S(1)} %get-tuple-element.53.own, bf16[64,512]{1,0:T(8,128)(2,1)S(1)} %collective-permute-done.18.refs_0_, bf16[64,512]{1,0:T(8,128)(2,1)S(1)} %collective-permute-done.19.refs_1_, bf16[64,512]{1,0:T(8,128)(2,1)S(1)} %collective-permute-done.20.refs_2_, ...), custom_call_target="tpu_custom_call" | custom-call | tf_op jit(solution)/shard_map/finish/pallas_call | solution.py:443
  (15 shorter events, 0.1 us)
Async XLA Ops:
  0.6 10.4 %collective-permute-start.1 = (bf16[256,512]{1,0:T(8,128)(2,1)}, bf16[256,512]{1,0:T(8,128)(2,1)S(1)}, u32[]{:S(2)}, u32[]{:S(2)}) collective-permute-start(bf16[256,512]{1,0:T(8,128)(2,1)} %refs_4_.1), channel_id=1, source_target_pairs={{0,2},{2,0},{1,3},{3,1},{4,6},{6,4},{5,7},{7,5},{8,10},{10,8},{9,1... | collective-permute-start | bytes 786440 | tf_op jit(solution)/shard_map/ppermute | solution.py:35
  5.3 5.7 %copy-start.3 = (bf16[256,512]{1,0:T(8,128)(2,1)S(1)}, bf16[256,512]{1,0:T(8,128)(2,1)}, u32[]{:S(2)}) copy-start(bf16[256,512]{1,0:T(8,128)(2,1)} %refs_4_.1) | copy-start | bytes 786436
  5.3 5.6 %copy-start.5 = (s32[1,4,64]{2,1,0:T(4,128)S(1)}, s32[1,4,64]{2,1,0:T(4,128)}, u32[]{:S(2)}) copy-start(s32[1,4,64]{2,1,0:T(4,128)} %rows_ref.3) | copy-start | bytes 3076
  5.3 11.7 %collective-permute-start.6 = (bf16[2,64,1024]{2,1,0:T(8,128)(2,1)}, bf16[2,64,1024]{2,1,0:T(8,128)(2,1)S(1)}, u32[]{:S(2)}, u32[]{:S(2)}) collective-permute-start(bf16[2,64,1024]{2,1,0:T(8,128)(2,1)} %prepare_first.1), channel_id=1, source_target_pairs={{0,2},{2,0},{1,3},{3,1},{4,6},{6,4},{5,7},{7,5},{8,10},{10,8},{9,1... | collective-permute-start | bytes 786440 | tf_op jit(solution)/shard_map/ppermute | solution.py:35
  7.3 8.9 %copy-start.7 = (s32[1536]{0:T(1024)S(1)}, s32[1536]{0:T(1024)}, u32[]{:S(2)}) copy-start(s32[1536]{0:T(1024)} %param.11) | copy-start | bytes 18436
  7.3 8.9 %copy-start.8 = (s32[1536]{0:T(1024)S(1)}, s32[1536]{0:T(1024)}, u32[]{:S(2)}) copy-start(s32[1536]{0:T(1024)} %param.12) | copy-start | bytes 18436
  7.3 8.9 %copy-start.6 = (s32[8]{0:T(128)S(1)}, s32[8]{0:T(128)}, u32[]{:S(2)}) copy-start(s32[8]{0:T(128)} %counts.1) | copy-start | bytes 100
  7.4 9.5 %copy-start.1 = (bf16[1536,512]{1,0:T(8,128)(2,1)S(1)}, bf16[1536,512]{1,0:T(8,128)(2,1)}, u32[]{:S(2)}) copy-start(bf16[1536,512]{1,0:T(8,128)(2,1)} %refs_0_.5) | copy-start | bytes 4718596
  7.4 9.5 %copy-start.4 = (f32[512]{0:T(512)S(1)}, f32[512]{0:T(512)}, u32[]{:S(2)}) copy-start(f32[512]{0:T(512)} %param.17) | copy-start | bytes 6148
  7.4 22.9 %collective-permute-start.11 = (bf16[2,128,1024]{2,1,0:T(8,128)(2,1)}, bf16[2,128,1024]{2,1,0:T(8,128)(2,1)S(1)}, u32[]{:S(2)}, u32[]{:S(2)}) collective-permute-start(bf16[2,128,1024]{2,1,0:T(8,128)(2,1)} %prepare_second.1), channel_id=1, source_target_pairs={{0,2},{2,0},{1,3},{3,1},{4,6},{6,4},{5,7},{7,5},{8,10},{10,8},{9,1... | collective-permute-start | bytes 1572872 | tf_op jit(solution)/shard_map/ppermute | solution.py:35
  11.0 19.8 %copy-start = (bf16[3,512,1024]{2,1,0:T(8,128)(2,1)S(1)}, bf16[3,512,1024]{2,1,0:T(8,128)(2,1)}, u32[]{:S(2)}) copy-start(bf16[3,512,1024]{2,1,0:T(8,128)(2,1)} %w_in.4) | copy-start | bytes 9437188
  11.5 19.2 %copy-start.2 = (bf16[1024,512]{1,0:T(8,128)(2,1)S(1)}, bf16[1024,512]{1,0:T(8,128)(2,1)}, u32[]{:S(2)}) copy-start(bf16[1024,512]{1,0:T(8,128)(2,1)} %w_out.3) | copy-start | bytes 3145732
  11.5 7.9 %collective-permute-start.2 = (bf16[64,1024]{1,0:T(8,128)(2,1)S(1)}, bf16[64,1024]{1,0:T(8,128)(2,1)S(1)}, u32[]{:S(2)}, u32[]{:S(2)}) collective-permute-start(bf16[64,1024]{1,0:T(8,128)(2,1)S(1)} %get-tuple-element.32), channel_id=1, source_target_pairs={{0,12},{1,13},{4,0},{5,1},{8,4},{9,5},{12,8},{13,9},{2,14},{3,15},... | collective-permute-start | bytes 393224 | tf_op jit(solution)/shard_map/ppermute | solution.py:35
  15.7 5.1 %collective-permute-start.3 = (bf16[64,1024]{1,0:T(8,128)(2,1)S(1)}, bf16[64,1024]{1,0:T(8,128)(2,1)S(1)}, u32[]{:S(2)}, u32[]{:S(2)}) collective-permute-start(bf16[64,1024]{1,0:T(8,128)(2,1)S(1)} %get-tuple-element.33), channel_id=1, source_target_pairs={{0,13},{1,0},{4,1},{5,4},{8,5},{9,8},{12,9},{13,12},{2,15},{3,2},{... | collective-permute-start | bytes 393224 | tf_op jit(solution)/shard_map/ppermute | solution.py:35
  15.7 6.2 %collective-permute-start.4 = (bf16[64,1024]{1,0:T(8,128)(2,1)S(1)}, bf16[64,1024]{1,0:T(8,128)(2,1)S(1)}, u32[]{:S(2)}, u32[]{:S(2)}) collective-permute-start(bf16[64,1024]{1,0:T(8,128)(2,1)S(1)} %get-tuple-element.34), channel_id=1, source_target_pairs={{0,1},{1,4},{4,5},{5,8},{8,9},{9,12},{12,13},{13,0},{2,3},{3,6},{6... | collective-permute-start | bytes 393224 | tf_op jit(solution)/shard_map/ppermute | solution.py:35
  17.1 27.2 %collective-permute-start = (bf16[784,512]{1,0:T(8,128)(2,1)S(1)}, bf16[784,512]{1,0:T(8,128)(2,1)S(1)}, u32[]{:S(2)}, u32[]{:S(2)}) collective-permute-start(bf16[784,512]{1,0:T(8,128)(2,1)S(1)} %get-tuple-element.31), channel_id=1, source_target_pairs={{0,2},{2,0},{1,3},{3,1},{4,6},{6,4},{5,7},{7,5},{8,10},{10,8},{9,1... | collective-permute-start | bytes 2408456 | tf_op jit(solution)/shard_map/ppermute | solution.py:35
  21.9 6.4 %collective-permute-start.7 = (bf16[2,64,1024]{2,1,0:T(8,128)(2,1)S(1)}, bf16[2,64,1024]{2,1,0:T(8,128)(2,1)S(1)}, u32[]{:S(2)}, u32[]{:S(2)}) collective-permute-start(bf16[2,64,1024]{2,1,0:T(8,128)(2,1)S(1)} %collective-permute-done.6.first), channel_id=1, source_target_pairs={{0,16},{16,0},{1,17},{17,1},{2,18},{18,2},{3,19},{19,3},{4,20},{20... | collective-permute-start | bytes 786440 | tf_op jit(solution)/shard_map/ppermute | solution.py:40
  23.5 6.8 %collective-permute-start.5 = (bf16[64,1024]{1,0:T(8,128)(2,1)S(1)}, bf16[64,1024]{1,0:T(8,128)(2,1)S(1)}, u32[]{:S(2)}, u32[]{:S(2)}) collective-permute-start(bf16[64,1024]{1,0:T(8,128)(2,1)S(1)} %get-tuple-element.35), channel_id=1, source_target_pairs={{0,4},{1,5},{4,8},{5,9},{8,12},{9,13},{12,0},{13,1},{2,6},{3,7},{6... | collective-permute-start | bytes 393224 | tf_op jit(solution)/shard_map/ppermute | solution.py:35
  30.2 12.1 %collective-permute-start.8 = (bf16[2,128,1024]{2,1,0:T(8,128)(2,1)S(1)}, bf16[2,128,1024]{2,1,0:T(8,128)(2,1)S(1)}, u32[]{:S(2)}, u32[]{:S(2)}) collective-permute-start(bf16[2,128,1024]{2,1,0:T(8,128)(2,1)S(1)} %join.1.refs_0_), channel_id=1, source_target_pairs={{0,4},{4,0},{8,12},{12,8},{1,5},{5,1},{9,13},{13,9},{2,6},{6,2},{1... | collective-permute-start | bytes 1572872 | tf_op jit(solution)/shard_map/ppermute | solution.py:40
  30.2 14.0 %collective-permute-start.12 = (bf16[2,128,1024]{2,1,0:T(8,128)(2,1)S(1)}, bf16[2,128,1024]{2,1,0:T(8,128)(2,1)S(1)}, u32[]{:S(2)}, u32[]{:S(2)}) collective-permute-start(bf16[2,128,1024]{2,1,0:T(8,128)(2,1)S(1)} %collective-permute-done.11.refs_4_), channel_id=1, source_target_pairs={{0,16},{16,0},{1,17},{17,1},{2,18},{18,2},{3,19},{19,3},{4,20},{20... | collective-permute-start | bytes 1572872 | tf_op jit(solution)/shard_map/ppermute | solution.py:40
  31.1 14.9 %collective-permute-start.9 = (bf16[2,128,1024]{2,1,0:T(8,128)(2,1)S(1)}, bf16[2,128,1024]{2,1,0:T(8,128)(2,1)S(1)}, u32[]{:S(2)}, u32[]{:S(2)}) collective-permute-start(bf16[2,128,1024]{2,1,0:T(8,128)(2,1)S(1)} %join.1.refs_0_), channel_id=1, source_target_pairs={{0,1},{1,0},{2,3},{3,2},{4,5},{5,4},{6,7},{7,6},{8,9},{9,8},{10,11... | collective-permute-start | bytes 1572872 | tf_op jit(solution)/shard_map/ppermute | solution.py:40
  31.1 14.8 %collective-permute-start.13 = (bf16[2,128,1024]{2,1,0:T(8,128)(2,1)S(1)}, bf16[2,128,1024]{2,1,0:T(8,128)(2,1)S(1)}, u32[]{:S(2)}, u32[]{:S(2)}) collective-permute-start(bf16[2,128,1024]{2,1,0:T(8,128)(2,1)S(1)} %collective-permute-done.11.refs_4_), channel_id=1, source_target_pairs={{0,1},{1,0},{2,3},{3,2},{4,5},{5,4},{6,7},{7,6},{8,9},{9,8},{10,11... | collective-permute-start | bytes 1572872 | tf_op jit(solution)/shard_map/ppermute | solution.py:40
  42.4 3.6 %collective-permute-start.10 = (bf16[2,128,1024]{2,1,0:T(8,128)(2,1)S(1)}, bf16[2,128,1024]{2,1,0:T(8,128)(2,1)S(1)}, u32[]{:S(2)}, u32[]{:S(2)}) collective-permute-start(bf16[2,128,1024]{2,1,0:T(8,128)(2,1)S(1)} %collective-permute-done.8.refs_1_), channel_id=1, source_target_pairs={{0,1},{1,0},{2,3},{3,2},{4,5},{5,4},{6,7},{7,6},{8,9},{9,8},{10,11... | collective-permute-start | bytes 1572872 | tf_op jit(solution)/shard_map/ppermute | solution.py:40
  44.2 1.9 %collective-permute-start.14 = (bf16[2,128,1024]{2,1,0:T(8,128)(2,1)S(1)}, bf16[2,128,1024]{2,1,0:T(8,128)(2,1)S(1)}, u32[]{:S(2)}, u32[]{:S(2)}) collective-permute-start(bf16[2,128,1024]{2,1,0:T(8,128)(2,1)S(1)} %collective-permute-done.12.refs_5_), channel_id=1, source_target_pairs={{0,1},{1,0},{2,3},{3,2},{4,5},{5,4},{6,7},{7,6},{8,9},{9,8},{10,11... | collective-permute-start | bytes 1572872 | tf_op jit(solution)/shard_map/ppermute | solution.py:40
  44.2 10.7 %collective-permute-start.17 = (bf16[256,512]{1,0:T(8,128)(2,1)S(1)}, bf16[256,512]{1,0:T(8,128)(2,1)S(1)}, u32[]{:S(2)}, u32[]{:S(2)}) collective-permute-start(bf16[256,512]{1,0:T(8,128)(2,1)S(1)} %get-tuple-element.52), channel_id=1, source_target_pairs={{0,2},{2,0},{1,3},{3,1},{4,6},{6,4},{5,7},{7,5},{8,10},{10,8},{9,1... | collective-permute-start | bytes 786440 | tf_op jit(solution)/shard_map/ppermute | solution.py:35
  49.6 11.1 %collective-permute-start.15 = (bf16[256,512]{1,0:T(8,128)(2,1)S(1)}, bf16[256,512]{1,0:T(8,128)(2,1)S(1)}, u32[]{:S(2)}, u32[]{:S(2)}) collective-permute-start(bf16[256,512]{1,0:T(8,128)(2,1)S(1)} %get-tuple-element.46), channel_id=1, source_target_pairs={{0,2},{2,0},{1,3},{3,1},{4,6},{6,4},{5,7},{7,5},{8,10},{10,8},{9,1... | collective-permute-start | bytes 786440 | tf_op jit(solution)/shard_map/ppermute | solution.py:35
  54.6 9.6 %collective-permute-start.16 = (bf16[256,512]{1,0:T(8,128)(2,1)S(1)}, bf16[256,512]{1,0:T(8,128)(2,1)S(1)}, u32[]{:S(2)}, u32[]{:S(2)}) collective-permute-start(bf16[256,512]{1,0:T(8,128)(2,1)S(1)} %get-tuple-element.49), channel_id=1, source_target_pairs={{0,2},{2,0},{1,3},{3,1},{4,6},{6,4},{5,7},{7,5},{8,10},{10,8},{9,1... | collective-permute-start | bytes 786440 | tf_op jit(solution)/shard_map/ppermute | solution.py:35
  64.5 7.0 %collective-permute-start.18 = (bf16[64,512]{1,0:T(8,128)(2,1)S(1)}, bf16[64,512]{1,0:T(8,128)(2,1)S(1)}, u32[]{:S(2)}, u32[]{:S(2)}) collective-permute-start(bf16[64,512]{1,0:T(8,128)(2,1)S(1)} %get-tuple-element.54), channel_id=1, source_target_pairs={{0,4},{1,5},{4,8},{5,9},{8,12},{9,13},{12,0},{13,1},{2,6},{3,7},{6... | collective-permute-start | bytes 196616 | tf_op jit(solution)/shard_map/ppermute | solution.py:35
  66.3 5.6 %collective-permute-start.19 = (bf16[64,512]{1,0:T(8,128)(2,1)S(1)}, bf16[64,512]{1,0:T(8,128)(2,1)S(1)}, u32[]{:S(2)}, u32[]{:S(2)}) collective-permute-start(bf16[64,512]{1,0:T(8,128)(2,1)S(1)} %get-tuple-element.55), channel_id=1, source_target_pairs={{0,1},{1,4},{4,5},{5,8},{8,9},{9,12},{12,13},{13,0},{2,3},{3,6},{6... | collective-permute-start | bytes 196616 | tf_op jit(solution)/shard_map/ppermute | solution.py:35
  66.4 5.6 %collective-permute-start.20 = (bf16[64,512]{1,0:T(8,128)(2,1)S(1)}, bf16[64,512]{1,0:T(8,128)(2,1)S(1)}, u32[]{:S(2)}, u32[]{:S(2)}) collective-permute-start(bf16[64,512]{1,0:T(8,128)(2,1)S(1)} %get-tuple-element.56), channel_id=1, source_target_pairs={{0,13},{1,0},{4,1},{5,4},{8,5},{9,8},{12,9},{13,12},{2,15},{3,2},{... | collective-permute-start | bytes 196616 | tf_op jit(solution)/shard_map/ppermute | solution.py:35
  69.9 4.3 %collective-permute-start.21 = (bf16[64,512]{1,0:T(8,128)(2,1)S(1)}, bf16[64,512]{1,0:T(8,128)(2,1)S(1)}, u32[]{:S(2)}, u32[]{:S(2)}) collective-permute-start(bf16[64,512]{1,0:T(8,128)(2,1)S(1)} %get-tuple-element.57), channel_id=1, source_target_pairs={{0,12},{1,13},{4,0},{5,1},{8,4},{9,5},{12,8},{13,9},{2,14},{3,15},... | collective-permute-start | bytes 196616 | tf_op jit(solution)/shard_map/ppermute | solution.py:35

commit v7 on v6

--- a/solution.py
+++ b/solution.py
@@ -490,6 +490,7 @@
     inner, outer = stage(tie(weight_in, *outgoing), weight_out)
     groups_b = [(gather_shares(piece, axes_b, [inner, outer, *edges]), axes_b) for piece in crossed_b]
     others = assemble(groups_a + groups_b)
+    edges = [tie(e, *others) for e in edges]
     others_a, others_b = others[: len(groups_a)], others[len(groups_a) :]
 
     def collected(places, parts, sums, last=False):

time: 75.4 us -> 75.4 us (level)
  no operation moved by 1% of the time
where the time goes in v7:
time: 75.4 us; the launch traced here: 75.2 us
  waiting for transfers between devices  29.6 us (39%)
  starting transfers between devices  23.7 us (31%)
  Pallas kernels  20.9 us (28%)
  between operations  0.87 us (1%)
    ppermute x15, starting transfers between devices, shifted(): lax.ppermute(block, axis, [(i, (i + distance) % size) for i in range(size)])  21.1 us
    ppermute x7, waiting for transfers between devices, swapped(): return lax.ppermute(block, axis, [(i, i ^ 1) for i in range(size)])  15.7 us
    ppermute x15, waiting for transfers between devices, shifted(): lax.ppermute(block, axis, [(i, (i + distance) % size) for i in range(size)])  13.9 us
    pallas_call x3, Pallas kernels, edge_update(): pl.pallas_call(functools.partial(edge_kernel, ways, place, mine, bool(oth...  12.1 us
    ppermute x7, starting transfers between devices, swapped(): return lax.ppermute(block, axis, [(i, i ^ 1) for i in range(size)])  2.6 us
    pallas_call x1, Pallas kernels, prepare_second(): pl.pallas_call(functools.partial(second_kernel, ways, axes), out_shape=sh...  1.86 us
    pallas_call x1, Pallas kernels, prepare_first(): pl.pallas_call(functools.partial(first_kernel, axes), out_shape=shape(2,...  1.68 us
  transfers between devices with their start and end apart: 22, of which 12 were waited for; matrix products, arithmetic and copies ran while one was open for 0% of the time, Pallas kernels for 26%

profile of v7, /device:TPU:0, one launch (start us, length us, event | category | flops | bytes accessed | tf_op | source)
XLA Modules:
  0.0 75.2 jit_solution(5355563831877536968)
XLA Ops:
  0.6 3.0 %collective-permute-start.2 = (bf16[256,512]{1,0:T(8,128)(2,1)}, bf16[256,512]{1,0:T(8,128)(2,1)S(1)}, u32[]{:S(2)}, u32[]{:S(2)}) collective-permute-start(bf16[256,512]{1,0:T(8,128)(2,1)} %refs_4_.1), channel_id=1, source_target_pairs={{0,2},{2,0},{1,3},{3,1},{4,6},{6,4},{5,7},{7,5},{8,10},{10,8},{9,1... | collective-permute-start | bytes 786440 | tf_op jit(solution)/shard_map/ppermute | solution.py:35
  3.6 1.7 %prepare_first.1 = bf16[2,64,1024]{2,1,0:T(8,128)(2,1)} custom-call(bf16[3,512,1024]{2,1,0:T(8,128)(2,1)} %w_in.4), custom_call_target="tpu_custom_call" | custom-call | tf_op jit(solution)/shard_map/prepare_first/pallas_call | solution.py:94
  5.3 0.0 copy-start.3
  5.3 0.0 copy-start.5
  5.3 0.1 collective-permute-start.1
  5.5 1.9 %prepare_second.1 = bf16[2,128,1024]{2,1,0:T(8,128)(2,1)} custom-call(bf16[3,512,1024]{2,1,0:T(8,128)(2,1)} %w_in.4, bf16[1024,512]{1,0:T(8,128)(2,1)} %w_out.3), custom_call_target="tpu_custom_call" | custom-call | tf_op jit(solution)/shard_map/prepare_second/pallas_call | solution.py:118
  7.3 0.0 copy-start.7
  7.3 0.0 copy-start.8
  7.3 0.0 copy-start.6
  7.4 0.0 copy-start.1
  7.4 0.0 copy-start.4
  7.4 2.1 %collective-permute-start.11 = (bf16[2,128,1024]{2,1,0:T(8,128)(2,1)}, bf16[2,128,1024]{2,1,0:T(8,128)(2,1)S(1)}, u32[]{:S(2)}, u32[]{:S(2)}) collective-permute-start(bf16[2,128,1024]{2,1,0:T(8,128)(2,1)} %prepare_second.1), channel_id=1, source_target_pairs={{0,2},{2,0},{1,3},{3,1},{4,6},{6,4},{5,7},{7,5},{8,10},{10,8},{9,1... | collective-permute-start | bytes 1572872 | tf_op jit(solution)/shard_map/ppermute | solution.py:35
  9.4 1.5 %collective-permute-done.2.refs_1_.refs_4_.refs_5_ = bf16[256,512]{1,0:T(8,128)(2,1)S(1)} collective-permute-done((bf16[256,512]{1,0:T(8,128)(2,1)}, bf16[256,512]{1,0:T(8,128)(2,1)S(1)}, u32[]{:S(2)}, u32[]{:S(2)}) %collective-permute-start.2) | collective-permute-done | bytes 262176 | tf_op jit(solution)/shard_map/ppermute | solution.py:35
  11.0 0.5 halo_gather.1
  11.5 0.0 copy-start.2
  11.5 4.2 %collective-permute-start.3 = (bf16[64,1024]{1,0:T(8,128)(2,1)S(1)}, bf16[64,1024]{1,0:T(8,128)(2,1)S(1)}, u32[]{:S(2)}, u32[]{:S(2)}) collective-permute-start(bf16[64,1024]{1,0:T(8,128)(2,1)S(1)} %get-tuple-element.33), channel_id=1, source_target_pairs={{0,12},{1,13},{4,0},{5,1},{8,4},{9,5},{12,8},{13,9},{2,14},{3,15},... | collective-permute-start | bytes 393224 | tf_op jit(solution)/shard_map/ppermute | solution.py:35
  15.7 0.0 collective-permute-start.4
  15.7 0.5 collective-permute-start.5
  16.3 0.6 mask_slots.1.slot_ref
  16.9 0.1 prepare_blocks.1
  17.0 0.0 collective-permute-done.1.first
  17.1 1.6 %collective-permute-start = (bf16[784,512]{1,0:T(8,128)(2,1)S(1)}, bf16[784,512]{1,0:T(8,128)(2,1)S(1)}, u32[]{:S(2)}, u32[]{:S(2)}) collective-permute-start(bf16[784,512]{1,0:T(8,128)(2,1)S(1)} %get-tuple-element.32), channel_id=1, source_target_pairs={{0,2},{2,0},{1,3},{3,1},{4,6},{6,4},{5,7},{7,5},{8,10},{10,8},{9,1... | collective-permute-start | bytes 2408456 | tf_op jit(solution)/shard_map/ppermute | solution.py:35
  18.7 0.8 %collective-permute-done.3.refs_5_.refs_6_ = bf16[64,1024]{1,0:T(8,128)(2,1)S(1)} collective-permute-done((bf16[64,1024]{1,0:T(8,128)(2,1)S(1)}, bf16[64,1024]{1,0:T(8,128)(2,1)S(1)}, u32[]{:S(2)}, u32[]{:S(2)}) %collective-permute-start.3) | collective-permute-done | bytes 131104 | tf_op jit(solution)/shard_map/ppermute | solution.py:35
  19.5 1.4 %collective-permute-done.4.refs_6_.refs_7_ = bf16[64,1024]{1,0:T(8,128)(2,1)S(1)} collective-permute-done((bf16[64,1024]{1,0:T(8,128)(2,1)S(1)}, bf16[64,1024]{1,0:T(8,128)(2,1)S(1)}, u32[]{:S(2)}, u32[]{:S(2)}) %collective-permute-start.4) | collective-permute-done | bytes 131104 | tf_op jit(solution)/shard_map/ppermute | solution.py:35
  20.9 1.1 %collective-permute-done.5.refs_7_.refs_8_ = bf16[64,1024]{1,0:T(8,128)(2,1)S(1)} collective-permute-done((bf16[64,1024]{1,0:T(8,128)(2,1)S(1)}, bf16[64,1024]{1,0:T(8,128)(2,1)S(1)}, u32[]{:S(2)}, u32[]{:S(2)}) %collective-permute-start.5) | collective-permute-done | bytes 131104 | tf_op jit(solution)/shard_map/ppermute | solution.py:35
  21.9 1.5 %collective-permute-start.6 = (bf16[2,64,1024]{2,1,0:T(8,128)(2,1)S(1)}, bf16[2,64,1024]{2,1,0:T(8,128)(2,1)S(1)}, u32[]{:S(2)}, u32[]{:S(2)}) collective-permute-start(bf16[2,64,1024]{2,1,0:T(8,128)(2,1)S(1)} %collective-permute-done.1.first), channel_id=1, source_target_pairs={{0,16},{16,0},{1,17},{17,1},{2,18},{18,2},{3,19},{19,3},{4,20},{20... | collective-permute-start | bytes 786440 | tf_op jit(solution)/shard_map/ppermute | solution.py:40
  23.5 0.0 collective-permute-start.7
  23.5 4.8 %collective-permute-done.6.second = bf16[2,64,1024]{2,1,0:T(8,128)(2,1)S(1)} collective-permute-done((bf16[2,64,1024]{2,1,0:T(8,128)(2,1)S(1)}, bf16[2,64,1024]{2,1,0:T(8,128)(2,1)S(1)}, u32[]{:S(2)}, u32[]{:S(2)}) %collective-permute-start.6) | collective-permute-done | bytes 262176 | tf_op jit(solution)/shard_map/ppermute | solution.py:40
  28.4 1.9 %collective-permute-done.7.refs_8_.refs_9_ = bf16[64,1024]{1,0:T(8,128)(2,1)S(1)} collective-permute-done((bf16[64,1024]{1,0:T(8,128)(2,1)S(1)}, bf16[64,1024]{1,0:T(8,128)(2,1)S(1)}, u32[]{:S(2)}, u32[]{:S(2)}) %collective-permute-start.7) | collective-permute-done | bytes 131104 | tf_op jit(solution)/shard_map/ppermute | solution.py:35
  30.2 0.0 collective-permute-start.8
  30.2 0.0 collective-permute-done.11.refs_4_
  30.2 0.5 collective-permute-start.12
  30.8 0.3 stage.1
  31.1 0.1 collective-permute-start.9
  31.1 0.5 collective-permute-start.13
  31.6 10.7 %collective-permute-done.8.refs_1_ = bf16[2,128,1024]{2,1,0:T(8,128)(2,1)S(1)} collective-permute-done((bf16[2,128,1024]{2,1,0:T(8,128)(2,1)S(1)}, bf16[2,128,1024]{2,1,0:T(8,128)(2,1)S(1)}, u32[]{:S(2)}, u32[]{:S(2)}) %collective-permute-start.8) | collective-permute-done | bytes 524320 | tf_op jit(solution)/shard_map/ppermute | solution.py:40
  42.4 0.0 collective-permute-start.10
  42.4 1.9 %collective-permute-done.refs_2_ = bf16[784,512]{1,0:T(8,128)(2,1)S(1)} collective-permute-done((bf16[784,512]{1,0:T(8,128)(2,1)S(1)}, bf16[784,512]{1,0:T(8,128)(2,1)S(1)}, u32[]{:S(2)}, u32[]{:S(2)}) %collective-permute-start) | collective-permute-done | bytes 802848 | tf_op jit(solution)/shard_map/ppermute | solution.py:35
  44.2 0.0 collective-permute-done.12.refs_5_
  44.2 0.0 collective-permute-start.14
  44.2 1.7 %collective-permute-start.17 = (bf16[256,512]{1,0:T(8,128)(2,1)S(1)}, bf16[256,512]{1,0:T(8,128)(2,1)S(1)}, u32[]{:S(2)}, u32[]{:S(2)}) collective-permute-start(bf16[256,512]{1,0:T(8,128)(2,1)S(1)} %get-tuple-element.54), channel_id=1, source_target_pairs={{0,2},{2,0},{1,3},{3,1},{4,6},{6,4},{5,7},{7,5},{8,10},{10,8},{9,1... | collective-permute-start | bytes 786440 | tf_op jit(solution)/shard_map/ppermute | solution.py:35
  46.0 0.0 collective-permute-done.9.refs_2_
  46.0 0.0 collective-permute-done.13.refs_6_
  46.0 0.0 collective-permute-done.10.refs_3_
  46.0 0.2 collective-permute-done.14.refs_7_
  46.1 0.3 assemble.1
  46.4 3.2 %edge_update_0.1 = (bf16[256,512]{1,0:T(8,128)(2,1)S(1)}, bf16[256,512]{1,0:T(8,128)(2,1)S(1)}) custom-call(s32[1,1536]{1,0:T(1,128)S(1)} %reshape.13.sender_ref, s32[1,1536]{1,0:T(1,128)S(1)} %mask_slots.1.slot_ref, bf16[1536,512]{1,0:T(8,128)(2,1)S(1)} %copy-done.1, f32[1,512]{1,0:T(1,128)S(1)} %bitcast.2, ...), custom_call_target="tpu_custom_call" | custom-call | flops 2550136832 | bytes 8388608 | tf_op jit(solution)/shard_map/edge_update_0/pallas_call | solution.py:357
  49.6 1.8 %collective-permute-start.15 = (bf16[256,512]{1,0:T(8,128)(2,1)S(1)}, bf16[256,512]{1,0:T(8,128)(2,1)S(1)}, u32[]{:S(2)}, u32[]{:S(2)}) collective-permute-start(bf16[256,512]{1,0:T(8,128)(2,1)S(1)} %get-tuple-element.48), channel_id=1, source_target_pairs={{0,2},{2,0},{1,3},{3,1},{4,6},{6,4},{5,7},{7,5},{8,10},{10,8},{9,1... | collective-permute-start | bytes 786440 | tf_op jit(solution)/shard_map/ppermute | solution.py:35
  51.4 3.1 %edge_update_1.1 = (bf16[256,512]{1,0:T(8,128)(2,1)S(1)}, bf16[256,512]{1,0:T(8,128)(2,1)S(1)}) custom-call(s32[1,1536]{1,0:T(1,128)S(1)} %reshape.13.sender_ref, s32[1,1536]{1,0:T(1,128)S(1)} %mask_slots.1.slot_ref, bf16[1536,512]{1,0:T(8,128)(2,1)S(1)} %copy-done.1, f32[1,512]{1,0:T(1,128)S(1)} %bitcast.3, ...), custom_call_target="tpu_custom_call" | custom-call | flops 2550136832 | bytes 8388608 | tf_op jit(solution)/shard_map/edge_update_1/pallas_call | solution.py:357
  54.6 0.3 collective-permute-start.16
  54.9 0.0 collective-permute-done.17.refs_3_
  54.9 5.8 %edge_update_2.1.refs_4_.refs_2_ = bf16[512,512]{1,0:T(8,128)(2,1)S(1)} custom-call(s32[1,1536]{1,0:T(1,128)S(1)} %reshape.13.sender_ref, s32[1,1536]{1,0:T(1,128)S(1)} %mask_slots.1.slot_ref, bf16[1536,512]{1,0:T(8,128)(2,1)S(1)} %copy-done.1, f32[1,512]{1,0:T(1,128)S(1)} %bitcast.4, bf16[784,512]{1,0:T(8,128)(2,1)S(1)} %collective-permute-done.refs_2_, ...), custom_call_target="tpu_custom_call" | custom-call | flops 5100273664 | bytes 8388608 | tf_op jit(solution)/shard_map/edge_update_2/pallas_call | solution.py:357
  60.7 0.0 collective-permute-done.15.refs_1_.refs_3_
  60.7 0.8 %collect.2.refs_1_ = f32[512,512]{1,0:T(8,128)S(1)} custom-call(s32[1,1536]{1,0:T(1,128)S(1)} %mask_slots.1.slot_ref, bf16[256,512]{1,0:T(8,128)(2,1)S(1)} %get-tuple-element.47.refs_0_, bf16[256,512]{1,0:T(8,128)(2,1)S(1)} %get-tuple-element.50.refs_2_.refs_1_, bf16[512,512]{1,0:T(8,128)(2,1)S(1)} %edge_update_2.1.refs_4_.refs_2_, ...), custom_call_target="tpu_custom_call" | custom-call | tf_op jit(solution)/shard_map/collect/pallas_call | solution.py:405
  61.5 2.6 %collective-permute-done.16.refs_3_.refs_0_ = bf16[256,512]{1,0:T(8,128)(2,1)S(1)} collective-permute-done((bf16[256,512]{1,0:T(8,128)(2,1)S(1)}, bf16[256,512]{1,0:T(8,128)(2,1)S(1)}, u32[]{:S(2)}, u32[]{:S(2)}) %collective-permute-start.16) | collective-permute-done | bytes 262176 | tf_op jit(solution)/shard_map/ppermute | solution.py:35
  64.2 0.3 collect.3
  64.5 1.9 %collective-permute-start.18 = (bf16[64,512]{1,0:T(8,128)(2,1)S(1)}, bf16[64,512]{1,0:T(8,128)(2,1)S(1)}, u32[]{:S(2)}, u32[]{:S(2)}) collective-permute-start(bf16[64,512]{1,0:T(8,128)(2,1)S(1)} %get-tuple-element.56), channel_id=1, source_target_pairs={{0,4},{1,5},{4,8},{5,9},{8,12},{9,13},{12,0},{13,1},{2,6},{3,7},{6... | collective-permute-start | bytes 196616 | tf_op jit(solution)/shard_map/ppermute | solution.py:35
  66.4 3.5 %collective-permute-start.20 = (bf16[64,512]{1,0:T(8,128)(2,1)S(1)}, bf16[64,512]{1,0:T(8,128)(2,1)S(1)}, u32[]{:S(2)}, u32[]{:S(2)}) collective-permute-start(bf16[64,512]{1,0:T(8,128)(2,1)S(1)} %get-tuple-element.58), channel_id=1, source_target_pairs={{0,13},{1,0},{4,1},{5,4},{8,5},{9,8},{12,9},{13,12},{2,15},{3,2},{... | collective-permute-start | bytes 196616 | tf_op jit(solution)/shard_map/ppermute | solution.py:35
  69.9 0.3 collective-permute-start.21
  70.2 1.3 %write.1 = bf16[1536,512]{1,0:T(8,128)(2,1)} custom-call(bf16[256,512]{1,0:T(8,128)(2,1)S(1)} %get-tuple-element.47.refs_0_, bf16[256,512]{1,0:T(8,128)(2,1)S(1)} %collective-permute-done.15.refs_1_.refs_3_, bf16[256,512]{1,0:T(8,128)(2,1)S(1)} %get-tuple-element.50.refs_2_.refs_1_, bf16[256,512]{1,0:T(8,128)(2,1)S(1)} %collective-permute-done.16.refs_3_.refs_0_, ...), custom_call_target="tpu_custom_call" | custom-call | tf_op jit(solution)/shard_map/write/pallas_call | solution.py:424
  71.5 0.0 collective-permute-done.18.refs_0_
  71.5 0.5 collective-permute-done.19.refs_1_
  72.0 2.2 %collective-permute-done.21.refs_3_ = bf16[64,512]{1,0:T(8,128)(2,1)S(1)} collective-permute-done((bf16[64,512]{1,0:T(8,128)(2,1)S(1)}, bf16[64,512]{1,0:T(8,128)(2,1)S(1)}, u32[]{:S(2)}, u32[]{:S(2)}) %collective-permute-start.21) | collective-permute-done | bytes 65568 | tf_op jit(solution)/shard_map/ppermute | solution.py:35
  74.2 1.1 %finish.1 = f32[256,512]{1,0:T(8,128)} custom-call(s32[1,4,64]{2,1,0:T(4,128)S(1)} %copy-done.5, f32[256,512]{1,0:T(8,128)S(1)} %get-tuple-element.55.own, bf16[64,512]{1,0:T(8,128)(2,1)S(1)} %collective-permute-done.18.refs_0_, bf16[64,512]{1,0:T(8,128)(2,1)S(1)} %collective-permute-done.19.refs_1_, bf16[64,512]{1,0:T(8,128)(2,1)S(1)} %collective-permute-done.20.refs_2_, ...), custom_call_target="tpu_custom_call" | custom-call | tf_op jit(solution)/shard_map/finish/pallas_call | solution.py:443
  (15 shorter events, 0.1 us)
Async XLA Ops:
  0.6 10.4 %collective-permute-start.2 = (bf16[256,512]{1,0:T(8,128)(2,1)}, bf16[256,512]{1,0:T(8,128)(2,1)S(1)}, u32[]{:S(2)}, u32[]{:S(2)}) collective-permute-start(bf16[256,512]{1,0:T(8,128)(2,1)} %refs_4_.1), channel_id=1, source_target_pairs={{0,2},{2,0},{1,3},{3,1},{4,6},{6,4},{5,7},{7,5},{8,10},{10,8},{9,1... | collective-permute-start | bytes 786440 | tf_op jit(solution)/shard_map/ppermute | solution.py:35
  5.3 5.7 %copy-start.3 = (bf16[256,512]{1,0:T(8,128)(2,1)S(1)}, bf16[256,512]{1,0:T(8,128)(2,1)}, u32[]{:S(2)}) copy-start(bf16[256,512]{1,0:T(8,128)(2,1)} %refs_4_.1) | copy-start | bytes 786436
  5.3 5.6 %copy-start.5 = (s32[1,4,64]{2,1,0:T(4,128)S(1)}, s32[1,4,64]{2,1,0:T(4,128)}, u32[]{:S(2)}) copy-start(s32[1,4,64]{2,1,0:T(4,128)} %rows_ref.3) | copy-start | bytes 3076
  5.3 11.7 %collective-permute-start.1 = (bf16[2,64,1024]{2,1,0:T(8,128)(2,1)}, bf16[2,64,1024]{2,1,0:T(8,128)(2,1)S(1)}, u32[]{:S(2)}, u32[]{:S(2)}) collective-permute-start(bf16[2,64,1024]{2,1,0:T(8,128)(2,1)} %prepare_first.1), channel_id=1, source_target_pairs={{0,2},{2,0},{1,3},{3,1},{4,6},{6,4},{5,7},{7,5},{8,10},{10,8},{9,1... | collective-permute-start | bytes 786440 | tf_op jit(solution)/shard_map/ppermute | solution.py:35
  7.3 8.9 %copy-start.7 = (s32[1536]{0:T(1024)S(1)}, s32[1536]{0:T(1024)}, u32[]{:S(2)}) copy-start(s32[1536]{0:T(1024)} %param.11) | copy-start | bytes 18436
  7.3 8.9 %copy-start.8 = (s32[1536]{0:T(1024)S(1)}, s32[1536]{0:T(1024)}, u32[]{:S(2)}) copy-start(s32[1536]{0:T(1024)} %param.12) | copy-start | bytes 18436
  7.3 8.9 %copy-start.6 = (s32[8]{0:T(128)S(1)}, s32[8]{0:T(128)}, u32[]{:S(2)}) copy-start(s32[8]{0:T(128)} %counts.1) | copy-start | bytes 100
  7.4 9.5 %copy-start.1 = (bf16[1536,512]{1,0:T(8,128)(2,1)S(1)}, bf16[1536,512]{1,0:T(8,128)(2,1)}, u32[]{:S(2)}) copy-start(bf16[1536,512]{1,0:T(8,128)(2,1)} %refs_0_.5) | copy-start | bytes 4718596
  7.4 9.5 %copy-start.4 = (f32[512]{0:T(512)S(1)}, f32[512]{0:T(512)}, u32[]{:S(2)}) copy-start(f32[512]{0:T(512)} %param.17) | copy-start | bytes 6148
  7.4 22.9 %collective-permute-start.11 = (bf16[2,128,1024]{2,1,0:T(8,128)(2,1)}, bf16[2,128,1024]{2,1,0:T(8,128)(2,1)S(1)}, u32[]{:S(2)}, u32[]{:S(2)}) collective-permute-start(bf16[2,128,1024]{2,1,0:T(8,128)(2,1)} %prepare_second.1), channel_id=1, source_target_pairs={{0,2},{2,0},{1,3},{3,1},{4,6},{6,4},{5,7},{7,5},{8,10},{10,8},{9,1... | collective-permute-start | bytes 1572872 | tf_op jit(solution)/shard_map/ppermute | solution.py:35
  11.0 19.8 %copy-start = (bf16[3,512,1024]{2,1,0:T(8,128)(2,1)S(1)}, bf16[3,512,1024]{2,1,0:T(8,128)(2,1)}, u32[]{:S(2)}) copy-start(bf16[3,512,1024]{2,1,0:T(8,128)(2,1)} %w_in.4) | copy-start | bytes 9437188
  11.5 19.2 %copy-start.2 = (bf16[1024,512]{1,0:T(8,128)(2,1)S(1)}, bf16[1024,512]{1,0:T(8,128)(2,1)}, u32[]{:S(2)}) copy-start(bf16[1024,512]{1,0:T(8,128)(2,1)} %w_out.3) | copy-start | bytes 3145732
  11.5 7.9 %collective-permute-start.3 = (bf16[64,1024]{1,0:T(8,128)(2,1)S(1)}, bf16[64,1024]{1,0:T(8,128)(2,1)S(1)}, u32[]{:S(2)}, u32[]{:S(2)}) collective-permute-start(bf16[64,1024]{1,0:T(8,128)(2,1)S(1)} %get-tuple-element.33), channel_id=1, source_target_pairs={{0,12},{1,13},{4,0},{5,1},{8,4},{9,5},{12,8},{13,9},{2,14},{3,15},... | collective-permute-start | bytes 393224 | tf_op jit(solution)/shard_map/ppermute | solution.py:35
  15.7 5.1 %collective-permute-start.4 = (bf16[64,1024]{1,0:T(8,128)(2,1)S(1)}, bf16[64,1024]{1,0:T(8,128)(2,1)S(1)}, u32[]{:S(2)}, u32[]{:S(2)}) collective-permute-start(bf16[64,1024]{1,0:T(8,128)(2,1)S(1)} %get-tuple-element.34), channel_id=1, source_target_pairs={{0,13},{1,0},{4,1},{5,4},{8,5},{9,8},{12,9},{13,12},{2,15},{3,2},{... | collective-permute-start | bytes 393224 | tf_op jit(solution)/shard_map/ppermute | solution.py:35
  15.7 6.2 %collective-permute-start.5 = (bf16[64,1024]{1,0:T(8,128)(2,1)S(1)}, bf16[64,1024]{1,0:T(8,128)(2,1)S(1)}, u32[]{:S(2)}, u32[]{:S(2)}) collective-permute-start(bf16[64,1024]{1,0:T(8,128)(2,1)S(1)} %get-tuple-element.35), channel_id=1, source_target_pairs={{0,1},{1,4},{4,5},{5,8},{8,9},{9,12},{12,13},{13,0},{2,3},{3,6},{6... | collective-permute-start | bytes 393224 | tf_op jit(solution)/shard_map/ppermute | solution.py:35
  17.1 27.2 %collective-permute-start = (bf16[784,512]{1,0:T(8,128)(2,1)S(1)}, bf16[784,512]{1,0:T(8,128)(2,1)S(1)}, u32[]{:S(2)}, u32[]{:S(2)}) collective-permute-start(bf16[784,512]{1,0:T(8,128)(2,1)S(1)} %get-tuple-element.32), channel_id=1, source_target_pairs={{0,2},{2,0},{1,3},{3,1},{4,6},{6,4},{5,7},{7,5},{8,10},{10,8},{9,1... | collective-permute-start | bytes 2408456 | tf_op jit(solution)/shard_map/ppermute | solution.py:35
  21.9 6.4 %collective-permute-start.6 = (bf16[2,64,1024]{2,1,0:T(8,128)(2,1)S(1)}, bf16[2,64,1024]{2,1,0:T(8,128)(2,1)S(1)}, u32[]{:S(2)}, u32[]{:S(2)}) collective-permute-start(bf16[2,64,1024]{2,1,0:T(8,128)(2,1)S(1)} %collective-permute-done.1.first), channel_id=1, source_target_pairs={{0,16},{16,0},{1,17},{17,1},{2,18},{18,2},{3,19},{19,3},{4,20},{20... | collective-permute-start | bytes 786440 | tf_op jit(solution)/shard_map/ppermute | solution.py:40
  23.5 6.8 %collective-permute-start.7 = (bf16[64,1024]{1,0:T(8,128)(2,1)S(1)}, bf16[64,1024]{1,0:T(8,128)(2,1)S(1)}, u32[]{:S(2)}, u32[]{:S(2)}) collective-permute-start(bf16[64,1024]{1,0:T(8,128)(2,1)S(1)} %get-tuple-element.37), channel_id=1, source_target_pairs={{0,4},{1,5},{4,8},{5,9},{8,12},{9,13},{12,0},{13,1},{2,6},{3,7},{6... | collective-permute-start | bytes 393224 | tf_op jit(solution)/shard_map/ppermute | solution.py:35
  30.2 12.1 %collective-permute-start.8 = (bf16[2,128,1024]{2,1,0:T(8,128)(2,1)S(1)}, bf16[2,128,1024]{2,1,0:T(8,128)(2,1)S(1)}, u32[]{:S(2)}, u32[]{:S(2)}) collective-permute-start(bf16[2,128,1024]{2,1,0:T(8,128)(2,1)S(1)} %join.1.refs_0_), channel_id=1, source_target_pairs={{0,4},{4,0},{8,12},{12,8},{1,5},{5,1},{9,13},{13,9},{2,6},{6,2},{1... | collective-permute-start | bytes 1572872 | tf_op jit(solution)/shard_map/ppermute | solution.py:40
  30.2 14.0 %collective-permute-start.12 = (bf16[2,128,1024]{2,1,0:T(8,128)(2,1)S(1)}, bf16[2,128,1024]{2,1,0:T(8,128)(2,1)S(1)}, u32[]{:S(2)}, u32[]{:S(2)}) collective-permute-start(bf16[2,128,1024]{2,1,0:T(8,128)(2,1)S(1)} %collective-permute-done.11.refs_4_), channel_id=1, source_target_pairs={{0,16},{16,0},{1,17},{17,1},{2,18},{18,2},{3,19},{19,3},{4,20},{20... | collective-permute-start | bytes 1572872 | tf_op jit(solution)/shard_map/ppermute | solution.py:40
  31.1 14.9 %collective-permute-start.9 = (bf16[2,128,1024]{2,1,0:T(8,128)(2,1)S(1)}, bf16[2,128,1024]{2,1,0:T(8,128)(2,1)S(1)}, u32[]{:S(2)}, u32[]{:S(2)}) collective-permute-start(bf16[2,128,1024]{2,1,0:T(8,128)(2,1)S(1)} %join.1.refs_0_), channel_id=1, source_target_pairs={{0,1},{1,0},{2,3},{3,2},{4,5},{5,4},{6,7},{7,6},{8,9},{9,8},{10,11... | collective-permute-start | bytes 1572872 | tf_op jit(solution)/shard_map/ppermute | solution.py:40
  31.1 14.8 %collective-permute-start.13 = (bf16[2,128,1024]{2,1,0:T(8,128)(2,1)S(1)}, bf16[2,128,1024]{2,1,0:T(8,128)(2,1)S(1)}, u32[]{:S(2)}, u32[]{:S(2)}) collective-permute-start(bf16[2,128,1024]{2,1,0:T(8,128)(2,1)S(1)} %collective-permute-done.11.refs_4_), channel_id=1, source_target_pairs={{0,1},{1,0},{2,3},{3,2},{4,5},{5,4},{6,7},{7,6},{8,9},{9,8},{10,11... | collective-permute-start | bytes 1572872 | tf_op jit(solution)/shard_map/ppermute | solution.py:40
  42.4 3.6 %collective-permute-start.10 = (bf16[2,128,1024]{2,1,0:T(8,128)(2,1)S(1)}, bf16[2,128,1024]{2,1,0:T(8,128)(2,1)S(1)}, u32[]{:S(2)}, u32[]{:S(2)}) collective-permute-start(bf16[2,128,1024]{2,1,0:T(8,128)(2,1)S(1)} %collective-permute-done.8.refs_1_), channel_id=1, source_target_pairs={{0,1},{1,0},{2,3},{3,2},{4,5},{5,4},{6,7},{7,6},{8,9},{9,8},{10,11... | collective-permute-start | bytes 1572872 | tf_op jit(solution)/shard_map/ppermute | solution.py:40
  44.2 1.9 %collective-permute-start.14 = (bf16[2,128,1024]{2,1,0:T(8,128)(2,1)S(1)}, bf16[2,128,1024]{2,1,0:T(8,128)(2,1)S(1)}, u32[]{:S(2)}, u32[]{:S(2)}) collective-permute-start(bf16[2,128,1024]{2,1,0:T(8,128)(2,1)S(1)} %collective-permute-done.12.refs_5_), channel_id=1, source_target_pairs={{0,1},{1,0},{2,3},{3,2},{4,5},{5,4},{6,7},{7,6},{8,9},{9,8},{10,11... | collective-permute-start | bytes 1572872 | tf_op jit(solution)/shard_map/ppermute | solution.py:40
  44.2 10.7 %collective-permute-start.17 = (bf16[256,512]{1,0:T(8,128)(2,1)S(1)}, bf16[256,512]{1,0:T(8,128)(2,1)S(1)}, u32[]{:S(2)}, u32[]{:S(2)}) collective-permute-start(bf16[256,512]{1,0:T(8,128)(2,1)S(1)} %get-tuple-element.54), channel_id=1, source_target_pairs={{0,2},{2,0},{1,3},{3,1},{4,6},{6,4},{5,7},{7,5},{8,10},{10,8},{9,1... | collective-permute-start | bytes 786440 | tf_op jit(solution)/shard_map/ppermute | solution.py:35
  49.6 11.1 %collective-permute-start.15 = (bf16[256,512]{1,0:T(8,128)(2,1)S(1)}, bf16[256,512]{1,0:T(8,128)(2,1)S(1)}, u32[]{:S(2)}, u32[]{:S(2)}) collective-permute-start(bf16[256,512]{1,0:T(8,128)(2,1)S(1)} %get-tuple-element.48), channel_id=1, source_target_pairs={{0,2},{2,0},{1,3},{3,1},{4,6},{6,4},{5,7},{7,5},{8,10},{10,8},{9,1... | collective-permute-start | bytes 786440 | tf_op jit(solution)/shard_map/ppermute | solution.py:35
  54.6 9.6 %collective-permute-start.16 = (bf16[256,512]{1,0:T(8,128)(2,1)S(1)}, bf16[256,512]{1,0:T(8,128)(2,1)S(1)}, u32[]{:S(2)}, u32[]{:S(2)}) collective-permute-start(bf16[256,512]{1,0:T(8,128)(2,1)S(1)} %get-tuple-element.51), channel_id=1, source_target_pairs={{0,2},{2,0},{1,3},{3,1},{4,6},{6,4},{5,7},{7,5},{8,10},{10,8},{9,1... | collective-permute-start | bytes 786440 | tf_op jit(solution)/shard_map/ppermute | solution.py:35
  64.5 7.0 %collective-permute-start.18 = (bf16[64,512]{1,0:T(8,128)(2,1)S(1)}, bf16[64,512]{1,0:T(8,128)(2,1)S(1)}, u32[]{:S(2)}, u32[]{:S(2)}) collective-permute-start(bf16[64,512]{1,0:T(8,128)(2,1)S(1)} %get-tuple-element.56), channel_id=1, source_target_pairs={{0,4},{1,5},{4,8},{5,9},{8,12},{9,13},{12,0},{13,1},{2,6},{3,7},{6... | collective-permute-start | bytes 196616 | tf_op jit(solution)/shard_map/ppermute | solution.py:35
  66.3 5.6 %collective-permute-start.19 = (bf16[64,512]{1,0:T(8,128)(2,1)S(1)}, bf16[64,512]{1,0:T(8,128)(2,1)S(1)}, u32[]{:S(2)}, u32[]{:S(2)}) collective-permute-start(bf16[64,512]{1,0:T(8,128)(2,1)S(1)} %get-tuple-element.57), channel_id=1, source_target_pairs={{0,1},{1,4},{4,5},{5,8},{8,9},{9,12},{12,13},{13,0},{2,3},{3,6},{6... | collective-permute-start | bytes 196616 | tf_op jit(solution)/shard_map/ppermute | solution.py:35
  66.4 5.6 %collective-permute-start.20 = (bf16[64,512]{1,0:T(8,128)(2,1)S(1)}, bf16[64,512]{1,0:T(8,128)(2,1)S(1)}, u32[]{:S(2)}, u32[]{:S(2)}) collective-permute-start(bf16[64,512]{1,0:T(8,128)(2,1)S(1)} %get-tuple-element.58), channel_id=1, source_target_pairs={{0,13},{1,0},{4,1},{5,4},{8,5},{9,8},{12,9},{13,12},{2,15},{3,2},{... | collective-permute-start | bytes 196616 | tf_op jit(solution)/shard_map/ppermute | solution.py:35
  69.9 4.3 %collective-permute-start.21 = (bf16[64,512]{1,0:T(8,128)(2,1)S(1)}, bf16[64,512]{1,0:T(8,128)(2,1)S(1)}, u32[]{:S(2)}, u32[]{:S(2)}) collective-permute-start(bf16[64,512]{1,0:T(8,128)(2,1)S(1)} %get-tuple-element.59), channel_id=1, source_target_pairs={{0,12},{1,13},{4,0},{5,1},{8,4},{9,5},{12,8},{13,9},{2,14},{3,15},... | collective-permute-start | bytes 196616 | tf_op jit(solution)/shard_map/ppermute | solution.py:35
